TPU v7x, 128 devices: a whole 4x4x4 slice. The times are simulated.
128 devices in a mesh: ctx: 32 (over z, y, core), exp: 4 (over x).
Axes of the slice: x: 4, y: 4, z: 4, core: 2. Of those that a mesh axis runs over, the one named last changes fastest.
Arguments:
- head_values: bfloat16 [8192, 8192], P('ctx', 'exp'), may hold values from -6 to 6
- gate_values: bfloat16 [8192, 8192], P('ctx', 'exp'), may hold values from -6 to 6
- write_keys: bfloat16 [8192, 128], P('ctx'), may hold values from -2 to 2
- read_keys: bfloat16 [8192, 128], P('ctx'), may hold values from -2 to 2
- step_size: float32 [8192, 64], P('ctx', 'exp'), may hold values from 0.012 to 0.21, as said below
- decay_rate: float32 [64], P('exp'), may hold values from 1.1765245e-05 to 0.67, as said below
- skip_weight: float32 [64], P('exp'), may hold values from 0.5 to 1.5
- prior_state: float32 [64, 128, 128], P('exp'), may hold values from -6 to 6
- norm_gain: float32 [8192], P('exp'), may hold values from 0.5 to 1.5
- out_weight: bfloat16 [8192, 8192], P('exp', 'ctx'), may hold values from -0.125 to 0.125
- residual: bfloat16 [8192, 8192], P('ctx', 'exp'), may hold values from -6 to 6
Outputs:
- layer_out: bfloat16 [8192, 8192], P('ctx', 'exp')
Inputs may be any that keep to these rules, and one draw needn't show every extreme that they name: `step_size`: positive steps. `decay_rate`: positive rates.
All inputs are finite; a program needn't handle non-finite values.
Results may differ from a plain program's by a relative error of at most 0.0049.
Values may be sent and summed in bfloat16 or wider, within the bound.
No kernel may reach another device: no remote copies, remote signals or barrier semaphores. Data moves between devices by JAX's collectives and lax.ppermute only.
A program may use at most 192 MiB of HBM per device.

v0:
```python
import jax
import jax.numpy as jnp
from jax import lax
from jax.sharding import PartitionSpec as P

BLOCK = 256


epsilon = 1e-05


def prefix(value, axis, join, neutral):
    count, mine = (lax.axis_size(axis), lax.axis_index(axis))
    pieces = jax.tree.map(lambda part: lax.all_gather(part, axis), value)
    total = jax.tree.map(
        lambda part, zero: jnp.full_like(part, 0) + jnp.asarray(zero, part.dtype), value, neutral
    )

    def lap(position, total):
        longer = join(total, jax.tree.map(lambda part: part[position], pieces))
        return jax.tree.map(lambda new, old: jnp.where(position < mine, new, old), longer, total)

    return lax.fori_loop(0, count - 1, lap, total)


def body(
    head_values,
    gate_values,
    write_keys,
    read_keys,
    step_size,
    decay_rate,
    skip_weight,
    prior_state,
    norm_gain,
    out_weight,
    residual,
):
    length = head_values.shape[0]
    head_count = decay_rate.shape[0]
    head_width = prior_state.shape[1]
    state_width = prior_state.shape[2]
    block_total = length // BLOCK
    values = head_values.reshape(block_total, BLOCK, head_count, head_width)
    writes = write_keys.reshape(block_total, BLOCK, state_width)
    reads = read_keys.reshape(block_total, BLOCK, state_width)
    steps = step_size.reshape(block_total, BLOCK, head_count)
    cumulative = jnp.cumsum(-steps * decay_rate[None, None, :], axis=1)
    scores = jnp.einsum("ktn,ksn->kts", reads, writes, preferred_element_type=jnp.float32)
    causal = jnp.arange(BLOCK)[:, None] >= jnp.arange(BLOCK)[None, :]
    spread_log = jnp.where(
        causal[None, :, :, None], cumulative[:, :, None, :] - cumulative[:, None, :, :], 0.0
    )
    mixing = (
        jnp.where(causal[None, :, :, None], jnp.exp(spread_log), 0.0)
        * scores[:, :, :, None]
        * steps[:, None, :, :]
    )
    mixing = mixing.astype(jnp.bfloat16)
    within = jnp.einsum("ktsh,kshp->kthp", mixing, values, preferred_element_type=jnp.float32)
    block_log = cumulative[:, -1]
    to_end = jnp.exp(block_log[:, None, :] - cumulative) * steps
    weighted = (values.astype(jnp.float32) * to_end[:, :, :, None]).astype(jnp.bfloat16)
    local_state = jnp.einsum("kthp,ktn->khpn", weighted, writes, preferred_element_type=jnp.float32)
    block_decay = jnp.exp(block_log)

    def chain_step(carry, inputs):
        decay_sofar, state_sofar = carry
        decay_here, state_here = inputs
        updated = (decay_sofar * decay_here, decay_here[:, None, None] * state_sofar + state_here)
        return (updated, (decay_sofar, state_sofar))

    start_carry = (
        jnp.ones((head_count,), jnp.float32),
        jnp.zeros((head_count, head_width, state_width), jnp.float32),
    )
    shard_total, inside = lax.scan(chain_step, start_carry, (block_decay, local_state))
    inside_decay, inside_state = inside

    def combine(earlier, latter):
        decay_first, state_first = earlier
        decay_second, state_second = latter
        return (
            decay_first * decay_second,
            decay_second[:, None, None] * state_first + state_second,
        )

    identity = (jnp.ones_like(shard_total[0]), jnp.zeros_like(shard_total[1]))
    before_decay, before_state = prefix(shard_total, "ctx", combine, identity)
    shard_entering = before_state + before_decay[:, None, None] * prior_state
    entering = inside_state + inside_decay[:, :, None, None] * shard_entering[None]
    carried = jnp.exp(cumulative)[:, :, :, None] * jnp.einsum(
        "ktn,khpn->kthp", reads.astype(jnp.float32), entering, precision=lax.Precision.HIGHEST
    )
    mixed = within + carried + skip_weight[None, None, :, None] * values.astype(jnp.float32)
    gated = mixed.reshape(length, head_count * head_width) * jax.nn.silu(
        gate_values.astype(jnp.float32)
    )
    square = lax.psum(jnp.sum(gated * gated, axis=1), "exp")
    inner_width = head_count * head_width * lax.axis_size("exp")
    normed = (
        gated * lax.rsqrt(square / inner_width + epsilon)[:, None] * norm_gain[None, :]
    ).astype(jnp.bfloat16)
    partial_value = jnp.dot(
        normed,
        lax.all_gather(out_weight, "ctx", axis=1, tiled=True),
        preferred_element_type=jnp.float32,
    )
    summed = lax.psum_scatter(partial_value, "exp", scatter_dimension=1, tiled=True)
    return (residual.astype(jnp.float32) + summed).astype(jnp.bfloat16)


def solution(mesh):
    in_specs = (
        P("ctx", "exp"),
        P("ctx", "exp"),
        P("ctx", None),
        P("ctx", None),
        P("ctx", "exp"),
        P("exp"),
        P("exp"),
        P("exp", None, None),
        P("exp"),
        P("exp", "ctx"),
        P("ctx", "exp"),
    )
    out_specs = P("ctx", "exp")
    return jax.shard_map(body, mesh=mesh, in_specs=in_specs, out_specs=out_specs, check_vma=False)
```

profile of v0, /device:TPU:2, one launch (start us, length us, event | category | flops | bytes accessed | tf_op | source)
XLA Modules:
  0.0 365.4 jit_solution(4736719247279925844)
XLA Ops:
  6.5 0.9 copy_bitcast_fusion
  8.2 0.8 copy.58
  10.3 1.1 fusion.6
  12.2 1.4 convolution_add_fusion
  15.0 1.6 copy.61
  16.8 22.9 %all-gather = f32[32,1,16]{2,1,0:T(1,128)S(1)} all-gather(f32[1,1,16]{2,1,0:T(1,128)} %get-tuple-element.200), channel_id=2, replica_groups=mesh['ctx'=32,'exp'=4] {'ctx'}, dimensions={0}, use_global_device_ids=true | all-gather | bytes 2112 | tf_op jit(solution)/shard_map/all_gather | solution.py:14
  40.0 2.9 fusion.1
  42.9 87.3 %all-gather.7.cloned.1.call-done = f32[512,128,128]{2,1,0:T(8,128)} async-done(((f32[16,128,128]{2,1,0:T(8,128)}), f32[512,128,128]{2,1,0:T(8,128)}) %all-gather.7.cloned.1.call-update) | async-done | bytes 33554448 | tf_op jit(solution)/shard_map/all_gather | solution.py:14
  130.1 47.5 %while.10 = (s32[]{:T(128)}, f32[16]{0:T(128)S(1)}, f32[16,128,128]{2,1,0:T(8,128)S(1)}, s32[]{:T(128)}, f32[32,16]{1,0:T(8,128)S(1)}, /*index=5*/f32[32,16,128,128]{3,2,1,0:T(8,128)}, s32[]{:T(128)}, s32[]{:T(128)}) while((s32[]{:T(128)}, f32[16]{0:T(128)S(1)}, f32[16,128,128]{2,1,0:T(8,128)S(1)}, s32[]{:T(128)}, ...), condition=%wide.region_3.4_spmd.clone, body=%wide.region_2.3_spmd.clone.sunk | while | flops 1048628 | bytes 3146163 | solution.py:23
  130.2 1.6 fusion.32
  131.8 1.5 fusion.32
  133.3 1.5 fusion.32
  134.8 1.5 fusion.32
  136.3 1.5 fusion.32
  137.8 1.5 fusion.32
  139.3 1.5 fusion.32
  140.8 1.6 fusion.32
  142.5 1.5 fusion.32
  144.0 1.5 fusion.32
  145.6 1.5 fusion.32
  147.1 1.5 fusion.32
  148.6 1.5 fusion.32
  150.1 1.5 fusion.32
  151.6 1.5 fusion.32
  153.1 1.5 fusion.32
  154.7 1.5 fusion.32
  156.2 1.5 fusion.32
  157.7 1.5 fusion.32
  159.2 1.5 fusion.32
  160.7 1.5 fusion.32
  162.3 1.5 fusion.32
  163.8 1.5 fusion.32
  165.3 1.5 fusion.32
  166.8 1.5 fusion.32
  168.3 1.5 fusion.32
  169.8 1.5 fusion.32
  171.3 1.5 fusion.32
  172.8 1.5 fusion.32
  174.3 1.5 fusion.32
  175.8 1.8 fusion.32
  177.7 4.5 %fusion.7 = f32[1,256,16,128]{1,3,2,0:T(8,128)} fusion(f32[16,256,128]{1,2,0:T(8,128)} %fusion.1, f32[1,256,16,128]{1,3,2,0:T(8,128)S(1)} %bitcast.77, f32[16]{0:T(128)S(1)} %copy-done.9, f32[16,128,128]{2,1,0:T(8,128)S(1)} %get-tuple-element.136, f32[16,128,128]{2,1,0:T(8,128)} %param.20, f32[256,16]{0,1:T(8,128)S(1)} %copy.56, ...), kind=kOutput, calls=%fused_computation.16 | convolution fusion | flops 807927808 | bytes 8470656 | tf_op jit(solution)/shard_map/ktn,khpn->kthp/dot_general | solution.py:92
  182.1 2.1 copy.62
  184.2 0.8 multiply_reduce_fusion
  185.0 8.6 %psum.7 = f32[256]{0:T(256)S(1)} all-reduce(f32[256]{0:T(256)S(1)} %multiply_reduce_fusion), channel_id=1, replica_groups=mesh['ctx'=32,'exp'=4] {'exp'}, use_global_device_ids=true, to_apply=%region_5.6 | all-reduce | flops 256 | bytes 2048 | tf_op jit(solution)/shard_map/psum | solution.py:99
  193.6 63.9 %all-gather.5.cloned.1.call-done = bf16[2048,8192]{1,0:T(8,128)(2,1)} async-done(((bf16[2048,256]{1,0:T(8,128)(2,1)}), bf16[2048,8192]{1,0:T(8,128)(2,1)}) %all-gather.5.cloned.1.call-update) | async-done | bytes 33554448 | tf_op jit(solution)/shard_map/all_gather | solution.py:106
  257.5 18.1 %fusion.14 = f32[256,8192]{1,0:T(8,128)} fusion(bf16[2048,8192]{1,0:T(8,128)(2,1)} %all-gather.5.cloned.1.call-done, f32[2048]{0:T(1024)S(1)} %copy-done.10, f32[256]{0:T(256)S(1)} %add_rsqrt_fusion, f32[256,2048]{1,0:T(8,128)S(1)} %copy.62, bf16[256,2048]{1,0:T(8,128)(2,1)S(1)} %copy-done.4), kind=kOutput, calls=%fused_computation.28 | convolution fusion | flops 8594653184 | bytes 45097984 | tf_op jit(solution)/shard_map/dot_general | solution.py:104
  275.6 80.4 %reduce-scatter.2.cloned.1.call-done = f32[256,2048]{1,0:T(8,128)} async-done(((f32[256,8192]{1,0:T(8,128)}), f32[256,2048]{1,0:T(8,128)}) %reduce-scatter.2.cloned.1.call-update) | async-done | bytes 2097168 | tf_op jit(solution)/shard_map/reduce_scatter | solution.py:109
  356.0 2.8 add_convert_fusion
  (79 shorter events, 5.1 us)
Async XLA Ops:
  6.5 33.2 %copy-start = (bf16[256,128]{1,0:T(8,128)(2,1)S(1)}, bf16[256,128]{1,0:T(8,128)(2,1)}, u32[]{:S(2)}) copy-start(bf16[256,128]{1,0:T(8,128)(2,1)} %param.16) | copy-start | bytes 196612
  6.5 3.8 %copy-start.2 = (bf16[256,2048]{1,0:T(8,128)(2,1)S(1)}, bf16[256,2048]{1,0:T(8,128)(2,1)}, u32[]{:S(2)}) copy-start(bf16[256,2048]{1,0:T(8,128)(2,1)} %param.13) | copy-start | bytes 3145732
  6.5 123.6 %all-gather.7.cloned.1.call-start = ((), (), s32[]{:S(2)}) async-start(), calls=%async_computation.3 | async-start | bytes 34603008 | tf_op jit(solution)/shard_map/all_gather | solution.py:14
  11.4 0.8 copy-start.6
  13.7 243.8 %all-gather.5.cloned.1.call-start = ((), (), s32[]{:S(2)}) async-start(), calls=%async_computation.1 | async-start | bytes 34603008 | tf_op jit(solution)/shard_map/all_gather | solution.py:106
  14.4 341.6 %reduce-scatter.2.cloned.1.call-start = ((), (), s32[]{:S(2)}) async-start(), calls=%async_computation.2 | async-start | bytes 10485760 | tf_op jit(solution)/shard_map/reduce_scatter | solution.py:109
  15.0 24.9 %copy-start.7 = (f32[256,16]{0,1:T(8,128)S(1)}, f32[256,16]{0,1:T(8,128)}, u32[]{:S(2)}) copy-start(f32[256,16]{0,1:T(8,128)} %param.17) | copy-start | bytes 49156
  39.9 90.2 %copy-start.8 = (f32[16]{0:T(128)S(1)}, f32[16]{0:T(128)}, u32[]{:S(2)}) copy-start(f32[16]{0:T(128)} %custom-call) | copy-start | bytes 196
  130.1 47.5 %copy-start.3 = (f32[256,2048]{0,1:T(8,128)S(1)}, f32[256,2048]{0,1:T(8,128)}, u32[]{:S(2)}) copy-start(f32[256,2048]{0,1:T(8,128)} %copy.61) | copy-start | bytes 6291460
  130.1 47.5 %copy-start.9 = (f32[16]{0:T(128)S(1)}, f32[16]{0:T(128)}, u32[]{:S(2)}) copy-start(f32[16]{0:T(128)} %param.19) | copy-start | bytes 196
  182.1 2.1 copy-start.4
  184.2 73.3 %copy-start.10 = (f32[2048]{0:T(1024)S(1)}, f32[2048]{0:T(1024)}, u32[]{:S(2)}) copy-start(f32[2048]{0:T(1024)} %param.21) | copy-start | bytes 24580
  275.6 80.4 %copy-start.5 = (bf16[256,2048]{1,0:T(8,128)(2,1)S(1)}, bf16[256,2048]{1,0:T(8,128)(2,1)}, u32[]{:S(2)}) copy-start(bf16[256,2048]{1,0:T(8,128)(2,1)} %param.23) | copy-start | bytes 3145732
  275.6 83.2 %copy-start.1 = (bf16[256,128]{1,0:T(8,128)(2,1)S(1)}, bf16[256,128]{1,0:T(8,128)(2,1)}, u32[]{:S(2)}) copy-start(bf16[256,128]{1,0:T(8,128)(2,1)} %param.16) | copy-start | bytes 196612
Sparse Core Ops, SparseCore 0:
  13.8 116.2 all-gather.6
  132.3 125.1 all-gather.4
  275.7 80.1 reduce-scatter.1
where the time goes:
time: 369 us; the launch traced here: 365 us
  waiting for transfers between devices  232 us (63%)
  other arithmetic  52.9 us (14%)
  blocking collectives  31.5 us (9%)
  matrix products  27 us (7%)
  between operations  13.3 us (4%)
  local copies, waits for them, and re-layouts  7.39 us (2%)
    all_gather x1, waiting for transfers between devices, prefix(): pieces = jax.tree.map(lambda part: lax.all_gather(part, axis), value)  87.3 us
    reduce_scatter x1, waiting for transfers between devices, body(): lax.psum_scatter(partial_value, 'exp', scatter_dimension=1, tiled=True)  80.4 us
    all_gather x1, waiting for transfers between devices, body(): lax.all_gather(out_weight, 'ctx', axis=1, tiled=True)  63.9 us
    select_n x62, other arithmetic, lap(): jnp.where(position < mine, new, old)  46.7 us
    all_gather x1, blocking collectives, prefix(): pieces = jax.tree.map(lambda part: lax.all_gather(part, axis), value)  22.9 us
    dot_general x1, matrix products, body(): jnp.dot(normed, lax.all_gather(out_weight, 'ctx', axis=1, tiled=True), pr...  18.1 us
    psum x1, blocking collectives, body(): square = lax.psum(jnp.sum(gated * gated, axis=1), 'exp')  8.59 us
  transfers between devices with their start and end apart: 3, of which 3 were waited for; matrix products, arithmetic and copies ran while one was open for 16% of the time, Pallas kernels for 0%

commit v1 on v0

v1 whole, which is shorter than its diff:
```python
import functools

import jax
import jax.numpy as jnp
from jax import lax
from jax.experimental import pallas as pl
from jax.experimental.pallas import tpu as pltpu
from jax.sharding import Mesh, PartitionSpec as P

EPSILON = 1e-05
ROWS = 256
HALF = 128
HEADS = 16
WIDTH = 128
LANES = HEADS * WIDTH
SPLIT = LANES // 2
PIECE = 512
INNER = 8192
F32 = jnp.float32
BF16 = jnp.bfloat16
HIGHEST = lax.Precision.HIGHEST
VMEM = pl.BlockSpec(memory_space=pltpu.VMEM)
SMEM = pl.BlockSpec(memory_space=pltpu.SMEM)


def params(mib=32):
    return pltpu.CompilerParams(vmem_limit_bytes=mib * 2**20)


def cost(flops, bytes_accessed, transcendentals=0):
    return pl.CostEstimate(
        flops=flops, bytes_accessed=bytes_accessed, transcendentals=transcendentals
    )


def lower(rows):
    return lax.broadcasted_iota(jnp.int32, (rows, rows), 0) >= lax.broadcasted_iota(
        jnp.int32, (rows, rows), 1
    )


def cumulate(step, rate):
    ones = jnp.where(lower(ROWS), 1.0, 0.0).astype(F32)
    return jnp.dot(ones, -step * rate, precision=HIGHEST, preferred_element_type=F32)


def three(row):
    high = row.astype(BF16)
    rest = row - high.astype(F32)
    middle = rest.astype(BF16)
    last = (rest - middle.astype(F32)).astype(BF16)
    return high.astype(F32), middle.astype(F32), last.astype(F32)


def stack_rows(rows, count):
    width = rows[0].shape[1]
    index = lax.broadcasted_iota(jnp.int32, (count, width), 0)
    result = jnp.zeros((count, width), F32)
    for place, row in enumerate(rows):
        result = jnp.where(index == place, row, result)
    return result


def unpack_rows(block):
    block = block.astype(F32)
    return block[0:1] + block[1:2] + block[2:3]


def state_kernel(place, value_ref, write_ref, step_ref, rate_ref, keep_ref, send_ref, state, logs):
    core = place[0]
    step = step_ref[...]
    cumulative = cumulate(step, rate_ref[...])
    last = cumulative[ROWS - 1 : ROWS]
    to_end = jnp.exp(last - cumulative) * step
    write = write_ref[...].T
    for head in range(HEADS):
        at = slice(head * WIDTH, (head + 1) * WIDTH)
        weighted = (value_ref[:, at].astype(F32) * to_end[:, head : head + 1]).astype(BF16)
        state[:, at] = jnp.dot(write, weighted, preferred_element_type=F32)
        logs[:, at] = jnp.broadcast_to(last[:, head : head + 1], (8, WIDTH))
    mine = pl.ds(pl.multiple_of(core * SPLIT, SPLIT), SPLIT)
    other = pl.ds(pl.multiple_of((1 - core) * SPLIT, SPLIT), SPLIT)
    keep_ref[0:WIDTH, :] = state[:, mine]
    keep_ref[WIDTH:, :] = logs[:, mine]
    send_ref[0:WIDTH, :] = state[:, other]
    send_ref[WIDTH:, :] = logs[:, other]


def local_state(place, values, writes, steps, rate):
    shape = jax.ShapeDtypeStruct((WIDTH + 8, SPLIT), F32)
    return pl.pallas_call(
        state_kernel,
        out_shape=(shape, shape),
        in_specs=[SMEM] + [VMEM] * 4,
        out_specs=(VMEM, VMEM),
        scratch_shapes=[pltpu.VMEM((WIDTH, LANES), F32), pltpu.VMEM((8, LANES), F32)],
        compiler_params=params(),
        cost_estimate=cost(2 * WIDTH * ROWS * LANES, 3 * 2**20),
        name="local_state",
    )(place, values, writes, steps, rate)


def plain_kernel(
    value_ref, gate_ref, write_ref, read_ref, step_ref, rate_ref, skip_ref, plain_ref, scale_ref
):
    step = step_ref[...]
    cumulative = cumulate(step, rate_ref[...])
    across = cumulative.T
    step_across = step.T
    decay = jnp.exp(cumulative)
    scores = lax.dot_general(
        read_ref[...], write_ref[...], (((1,), (1,)), ((), ())), preferred_element_type=F32
    )
    scores = jnp.where(lower(ROWS), scores, 0.0)
    for head in range(HEADS):
        at = slice(head * WIDTH, (head + 1) * WIDTH)
        spread = jnp.minimum(cumulative[:, head : head + 1] - across[head : head + 1, :], 0.0)
        mixing = (jnp.exp(spread) * scores * step_across[head : head + 1, :]).astype(BF16)
        value = value_ref[:, at]
        within = jnp.dot(mixing, value, preferred_element_type=F32)
        within = within + skip_ref[:, head : head + 1] * value.astype(F32)
        gate = gate_ref[:, at].astype(F32)
        gate = gate / (1.0 + jnp.exp(-gate))
        plain_ref[:, at] = within * gate
        scale_ref[:, at] = decay[:, head : head + 1] * gate


def plain_part(values, gates, writes, reads, steps, rate, skip):
    shape = jax.ShapeDtypeStruct((ROWS, LANES), F32)
    return pl.pallas_call(
        plain_kernel,
        out_shape=(shape, shape),
        in_specs=[VMEM] * 7,
        out_specs=(VMEM, VMEM),
        compiler_params=params(),
        cost_estimate=cost(
            2 * ROWS * ROWS * LANES, 7 * 2**20, HEADS * ROWS * ROWS + ROWS * LANES
        ),
        name="plain_part",
    )(values, gates, writes, reads, steps, rate, skip)


def turn_kernel(place, prior_ref, out_ref):
    out_ref[...] = prior_ref[0].T


def turned_prior(place, prior):
    heads = HEADS // 2
    return pl.pallas_call(
        turn_kernel,
        grid_spec=pltpu.PrefetchScalarGridSpec(
            num_scalar_prefetch=1,
            grid=(heads,),
            in_specs=[
                pl.BlockSpec((1, WIDTH, WIDTH), lambda i, place: (place[0] * heads + i, 0, 0))
            ],
            out_specs=pl.BlockSpec((WIDTH, WIDTH), lambda i, place: (0, i)),
        ),
        out_shape=jax.ShapeDtypeStruct((WIDTH, SPLIT), F32),
        compiler_params=params(),
        cost_estimate=cost(0, 2**20),
        name="turned_prior",
    )(place, prior)


MESSAGE = jax.ShapeDtypeStruct((WIDTH + 16, SPLIT), BF16)


def write_message(out_ref, state, log):
    out_ref[0:WIDTH, :] = state.astype(BF16)
    out_ref[WIDTH:, :] = stack_rows(three(log), 16).astype(BF16)


def ordered(core, keep_ref, got_ref):
    kept, got = keep_ref[...], got_ref[...]
    first = jnp.where(core == 0, kept, got)
    second = jnp.where(core == 0, got, kept)
    split = lambda part: (part[0:WIDTH], part[WIDTH : WIDTH + 1])
    return split(first), split(second)


def chip_kernel(place, keep_ref, got_ref, out_ref):
    (state0, log0), (state1, log1) = ordered(place[0], keep_ref, got_ref)
    write_message(out_ref, jnp.exp(log1) * state0 + state1, log0 + log1)


def chip_total(place, keep, got):
    return pl.pallas_call(
        chip_kernel,
        out_shape=MESSAGE,
        in_specs=[SMEM] + [VMEM] * 2,
        out_specs=VMEM,
        compiler_params=params(),
        cost_estimate=cost(2 * WIDTH * SPLIT, 2**20),
        name="chip_total",
    )(place, keep, got)


def fold(here, parts, whole):
    logs = [unpack_rows(part[WIDTH : WIDTH + 16, :]) for part in parts]
    at = [lax.rem(here - k + 4, 4) for k in range(4)]
    total = None
    for k in range(4):
        if not whole and k == 0:
            continue
        after = jnp.zeros_like(logs[0])
        for j in range(4):
            if j == k or (not whole and j == 0):
                continue
            counts = at[j] > at[k]
            if not whole:
                counts = jnp.logical_and(counts, at[j] < here)
            after = after + jnp.where(counts, logs[j], 0.0)
        weight = jnp.exp(after)
        if not whole:
            weight = jnp.where(at[k] < here, weight, 0.0)
        term = weight * parts[k][0:WIDTH, :].astype(F32)
        total = term if total is None else total + term
    log = jnp.zeros_like(logs[0])
    for k in range(4):
        if whole:
            log = log + logs[k]
        elif k:
            log = log + jnp.where(at[k] < here, logs[k], 0.0)
    return total, log


def row_kernel(place, p0, p1, p2, p3, out_ref, before_ref):
    parts = (p0, p1, p2, p3)
    total, log = fold(place[2], parts, True)
    write_message(out_ref, total, log)
    total, log = fold(place[2], parts, False)
    before_ref[0:WIDTH, :] = total
    before_ref[WIDTH:, :] = jnp.broadcast_to(log, (8, SPLIT))


def row_total(place, parts):
    return pl.pallas_call(
        row_kernel,
        out_shape=(MESSAGE, jax.ShapeDtypeStruct((WIDTH + 8, SPLIT), F32)),
        in_specs=[SMEM] + [VMEM] * 4,
        out_specs=(VMEM, VMEM),
        compiler_params=params(),
        cost_estimate=cost(16 * WIDTH * SPLIT, 2 * 2**20),
        name="row_total",
    )(place, *parts)


def enter_kernel(
    place, p0, p1, p2, p3, before_ref, prior_ref, keep_ref, got_ref, mine_ref, other_ref
):
    core = place[0]
    total, log = fold(place[3], (p0, p1, p2, p3), False)
    entering = total + jnp.exp(log) * prior_ref[...]
    entering = jnp.exp(before_ref[WIDTH : WIDTH + 1, :]) * entering + before_ref[0:WIDTH, :]
    (state0, log0), _ = ordered(core, keep_ref, got_ref)
    second = jnp.exp(log0) * entering + state0
    mine_ref[...] = jnp.where(core == 0, entering, second).astype(BF16)
    other_ref[...] = jnp.where(core == 0, second, entering).astype(BF16)


def entering_state(place, parts, before, prior, keep, got):
    shape = jax.ShapeDtypeStruct((WIDTH, SPLIT), BF16)
    return pl.pallas_call(
        enter_kernel,
        out_shape=(shape, shape),
        in_specs=[SMEM] + [VMEM] * 8,
        out_specs=(VMEM, VMEM),
        compiler_params=params(),
        cost_estimate=cost(16 * WIDTH * SPLIT, 4 * 2**20),
        name="entering_state",
    )(place, *parts, before, prior, keep, got)


def gated_kernel(
    place, mine_ref, other_ref, read_ref, plain_ref, scale_ref, gain_ref, top_ref, low_ref, stat_ref, acc
):
    step = pl.program_id(0)
    mine = place[0] == step // 2
    entering = jnp.where(mine, mine_ref[...], other_ref[...])
    carried = jnp.dot(read_ref[...], entering, preferred_element_type=F32)
    gated = plain_ref[...] + scale_ref[...] * carried
    result = (gated * gain_ref[...]).astype(BF16)
    top_ref[...] = result[:HALF]
    low_ref[...] = result[HALF:]
    square = gated * gated
    part = square[:, 0:128]
    for at in range(128, square.shape[1], 128):
        part = part + square[:, at : at + 128]

    @pl.when(step == 0)
    def _():
        acc[...] = part

    @pl.when(step > 0)
    def _():
        acc[...] += part

    @pl.when(step == pl.num_programs(0) - 1)
    def _():
        row = jnp.sum(acc[...].T, axis=0, keepdims=True)
        stat_ref[...] = jnp.zeros_like(stat_ref)
        stat_ref[:, 0:ROWS] = stack_rows(three(row), 16).astype(BF16)


def gated_part(place, mine, other, reads, plain, scale, gain):
    steps = 4
    width = LANES // steps
    half = pl.BlockSpec((HALF, width), lambda i, place: (0, i))
    wide = pl.BlockSpec((ROWS, width), lambda i, place: (0, i))
    state = pl.BlockSpec((WIDTH, width), lambda i, place: (0, lax.rem(i, 2)))
    whole = lambda shape: pl.BlockSpec(shape, lambda i, place: (0, 0))
    return pl.pallas_call(
        gated_kernel,
        grid_spec=pltpu.PrefetchScalarGridSpec(
            num_scalar_prefetch=1,
            grid=(steps,),
            in_specs=[
                state,
                state,
                whole((ROWS, WIDTH)),
                wide,
                wide,
                pl.BlockSpec((1, width), lambda i, place: (0, i)),
            ],
            out_specs=[half, half, whole((16, PIECE))],
            scratch_shapes=[pltpu.VMEM((ROWS, 128), F32)],
        ),
        out_shape=(
            jax.ShapeDtypeStruct((HALF, LANES), BF16),
            jax.ShapeDtypeStruct((HALF, LANES), BF16),
            jax.ShapeDtypeStruct((16, PIECE), BF16),
        ),
        compiler_params=params(),
        cost_estimate=cost(2 * ROWS * WIDTH * LANES, 6 * 2**20),
        name="gated_part",
    )(place, mine, other, reads, plain, scale, gain)


def project_kernel(place, top_ref, low_ref, weight_ref, *refs):
    stats = refs[:-4]
    step = pl.program_id(0)
    for k, out_ref in enumerate(refs[-4:]):

        @pl.when(step == k)
        def _(out_ref=out_ref):
            for core in range(2):
                at = slice(core * 256, (core + 1) * 256)
                weight = weight_ref[core]
                for rows, ref in ((0, top_ref), (HALF, low_ref)):
                    out_ref[rows : rows + HALF, at] = jnp.dot(
                        ref[...], weight, preferred_element_type=F32
                    ).astype(BF16)
            for stat in stats:
                out_ref[ROWS:, :] = stat[...]


def project(place, top, low, weight, stats=None):
    rows = ROWS if stats is None else ROWS + 16
    extra = () if stats is None else (stats,)
    half = pl.BlockSpec((HALF, LANES), lambda i, place: (0, 0))
    out = pl.BlockSpec((rows, PIECE), lambda i, place: (0, 0))
    return pl.pallas_call(
        project_kernel,
        grid_spec=pltpu.PrefetchScalarGridSpec(
            num_scalar_prefetch=1,
            grid=(4,),
            in_specs=[
                half,
                half,
                pl.BlockSpec(
                    (2, LANES, 256), lambda i, place: (lax.rem(place[1] + i, 4), 0, 0)
                ),
            ]
            + [pl.BlockSpec((16, PIECE), lambda i, place: (0, 0))] * len(extra),
            out_specs=[out] * 4,
        ),
        out_shape=[jax.ShapeDtypeStruct((rows, PIECE), BF16)] * 4,
        compiler_params=params(),
        cost_estimate=cost(2 * ROWS * LANES * 4 * PIECE, 10 * 2**20),
        name="project",
    )(place, top, low, weight, *extra)


def add(parts, rows):
    total = parts[0][rows, :].astype(F32)
    for part in parts[1:]:
        total = total + part[rows, :].astype(F32)
    return total


def sums_kernel(*refs):
    first, second, (down_ref, up_ref) = refs[0:4], refs[4:8], refs[8:]
    for at, parts in ((0, first), (HALF, second)):
        down_ref[at : at + HALF, :] = add(parts, slice(0, HALF)).astype(BF16)
        up_ref[at : at + HALF, :] = add(parts, slice(HALF, ROWS)).astype(BF16)


def neighbour_sums(first, second):
    shape = jax.ShapeDtypeStruct((ROWS, PIECE), BF16)
    return pl.pallas_call(
        sums_kernel,
        out_shape=(shape, shape),
        in_specs=[VMEM] * 8,
        out_specs=(VMEM, VMEM),
        compiler_params=params(),
        cost_estimate=cost(8 * ROWS * PIECE, 10 * ROWS * PIECE * 2),
        name="neighbour_sums",
    )(*first, *second)


def sum_kernel(*refs):
    refs[4][...] = add(refs[0:4], slice(0, ROWS)).astype(BF16)


def far_sums(parts):
    return pl.pallas_call(
        sum_kernel,
        out_shape=jax.ShapeDtypeStruct((ROWS, PIECE), BF16),
        in_specs=[VMEM] * 4,
        out_specs=VMEM,
        compiler_params=params(),
        cost_estimate=cost(4 * ROWS * PIECE, 5 * ROWS * PIECE * 2),
        name="far_sums",
    )(*parts)


def finish_kernel(place, p0, p1, p2, p3, up_ref, far_ref, down_ref, residual_ref, out_ref):
    own = (p0, p1, p2, p3)
    square = sum(unpack_rows(part[ROWS : ROWS + 16, 0:ROWS]) for part in own)
    row = lax.rsqrt(square / INNER + EPSILON)
    scale = jnp.broadcast_to(row, (128, ROWS)).T
    step = pl.program_id(0)

    def write(total):
        for at in range(0, PIECE, 128):
            cols = slice(at, at + 128)
            out_ref[:, cols] = (residual_ref[:, cols].astype(F32) + scale * total[:, cols]).astype(
                BF16
            )

    @pl.when(step == 0)
    def _():
        write(add(own, slice(0, ROWS)))

    for k, ref in ((1, up_ref), (2, far_ref), (3, down_ref)):

        @pl.when(step == k)
        def _(ref=ref):
            write(ref[...].astype(F32))


def finish(place, own, up, far, down, residual):
    whole = lambda rows: pl.BlockSpec((rows, PIECE), lambda i, place: (0, 0))
    block = pl.BlockSpec((ROWS, PIECE), lambda i, place: (0, lax.rem(place[2] + i, 4)))
    return pl.pallas_call(
        finish_kernel,
        grid_spec=pltpu.PrefetchScalarGridSpec(
            num_scalar_prefetch=1,
            grid=(4,),
            in_specs=[whole(ROWS + 16)] * 4 + [whole(ROWS)] * 3 + [block],
            out_specs=block,
        ),
        out_shape=jax.ShapeDtypeStruct((ROWS, 4 * PIECE), BF16),
        compiler_params=params(),
        cost_estimate=cost(4 * ROWS * 4 * PIECE, 4 * 2**20),
        name="finish",
    )(place, *own, up, far, down, residual)


def shift(value, axis, by):
    return lax.ppermute(value, axis, [(i, (i + by) % 4) for i in range(4)])


def swap(value):
    return lax.ppermute(value, "core", [(0, 1), (1, 0)])


def scatter(pieces):
    return [pieces[0]] + [shift(pieces[k], "x", k) for k in (1, 2, 3)]


def body(
    head_values,
    gate_values,
    write_keys,
    read_keys,
    step_size,
    decay_rate,
    skip_weight,
    prior_state,
    norm_gain,
    out_weight,
    residual,
):
    place = jnp.stack([lax.axis_index(name) for name in ("core", "x", "y", "z")]).astype(jnp.int32)
    weight = lax.all_gather(out_weight, ("z", "core"))
    rate = decay_rate[None, :]

    keep, send = local_state(place, head_values, write_keys, step_size, rate)
    got = swap(send)
    plain, scale = plain_part(
        head_values, gate_values, write_keys, read_keys, step_size, rate, skip_weight[None, :]
    )
    prior = turned_prior(place, prior_state)
    chip = chip_total(place, keep, got)
    row, before = row_total(place, [chip] + [shift(chip, "y", k) for k in (1, 2, 3)])
    mine, other = entering_state(
        place, [row] + [shift(row, "z", k) for k in (1, 2, 3)], before, prior, keep, got
    )
    other = swap(other)
    top, low, stats = gated_part(place, mine, other, read_keys, plain, scale, norm_gain[None, :])

    top_below, top_above = shift(top, "y", 1), shift(top, "y", -1)
    low_below, low_above = shift(low, "y", 1), shift(low, "y", -1)
    top_far, low_far = shift(top_below, "y", 1), shift(low_above, "y", -1)

    own = scatter(project(place, top, low, weight, stats))
    first = scatter(project(place, top_below, top_above, weight))
    second = scatter(project(place, low_below, low_above, weight))
    far = scatter(project(place, top_far, low_far, weight))

    down, up = neighbour_sums(first, second)
    from_above = shift(down, "y", -1)
    from_below = shift(up, "y", 1)
    from_far = shift(far_sums(far), "y", 2)
    return finish(place, own, from_above, from_far, from_below, residual)


def solution(mesh):
    grid = Mesh(mesh.devices.reshape(4, 4, 2, 4), ("z", "y", "core", "x"))
    ctx = ("z", "y", "core")
    in_specs = (
        P(ctx, "x"),
        P(ctx, "x"),
        P(ctx, None),
        P(ctx, None),
        P(ctx, "x"),
        P("x"),
        P("x"),
        P("x", None, None),
        P("x"),
        P("x", ctx),
        P(ctx, "x"),
    )
    return jax.shard_map(
        body, mesh=grid, in_specs=in_specs, out_specs=P(ctx, "x"), check_vma=False
    )
```

time: 369 us -> 184 us (0.50)
  waiting for transfers between devices: 232 us -> 85.3 us
  other arithmetic: 52.9 us -> 0.08 us
  starting transfers between devices: 0.08 us -> 44.5 us
  blocking collectives: 31.5 us -> 0 us
  Pallas kernels: 0 us -> 29 us
  matrix products: 27 us -> 0 us
    all_gather x2 -> x1, waiting for transfers between devices: 151 us -> 0.01 us  [body(): weight = lax.all_gather(out_weight, ('z', 'core'))]
    ppermute x0 -> x29, waiting for transfers between devices: none -> 84.5 us  [the longest x27 82.6 us: shift(): return lax.ppermute(value, axis, [(i, (i + by) % 4) for i in range(4)])]
    reduce_scatter x1 -> x0, waiting for transfers between devices: 80.4 us -> none  [body(): lax.psum_scatter(partial_value, 'exp', scatter_dimension=1, tiled=True)]
    select_n x62 -> x0, other arithmetic: 46.7 us -> none  [lap(): jnp.where(position < mine, new, old)]
    ppermute x0 -> x29, starting transfers between devices: none -> 44.5 us  [the longest x27 44.4 us: shift(): return lax.ppermute(value, axis, [(i, (i + by) % 4) for i in range(4)])]
    pallas_call x0 -> x14, Pallas kernels: none -> 29 us  [the longest x4 14.5 us: project(): pl.pallas_call(project_kernel, grid_spec=pltpu.PrefetchScalarGridSpec(num...]
    dot_general x5 -> x0, matrix products: 27 us -> none  [the longest x1 18.1 us: body(): jnp.dot(normed, lax.all_gather(out_weight, 'ctx', axis=1, tiled=True), pr...]
    all_gather x1 -> x0, blocking collectives: 22.9 us -> none  [prefix(): pieces = jax.tree.map(lambda part: lax.all_gather(part, axis), value)]
  transfers between devices with their start and end apart: 3 -> 30, of which waited for: 3 -> 12; matrix products, arithmetic and copies ran while one was open for 16% -> 1% of each run, Pallas kernels for 0% -> 14%
where the time goes in v1:
time: 184 us; the launch traced here: 183 us
  waiting for transfers between devices  85.3 us (46%)
  starting transfers between devices  44.5 us (24%)
  Pallas kernels  29 us (16%)
  between operations  13.7 us (7%)
  local copies, waits for them, and re-layouts  10.7 us (6%)
    ppermute x27, waiting for transfers between devices, shift(): return lax.ppermute(value, axis, [(i, (i + by) % 4) for i in range(4)])  82.6 us
    ppermute x27, starting transfers between devices, shift(): return lax.ppermute(value, axis, [(i, (i + by) % 4) for i in range(4)])  44.4 us
    pallas_call x4, Pallas kernels, project(): pl.pallas_call(project_kernel, grid_spec=pltpu.PrefetchScalarGridSpec(num...  14.5 us
    unnamed x37, local copies, waits for them, and re-layouts  10.7 us
  transfers between devices with their start and end apart: 30, of which 12 were waited for; matrix products, arithmetic and copies ran while one was open for 1% of the time, Pallas kernels for 14%

profile of v1, /device:TPU:2, one launch (start us, length us, event | category | flops | bytes accessed | tf_op | source)
XLA Modules:
  0.0 183.3 jit_solution(4887798505427637334)
XLA Ops:
  7.3 0.9 copy.12.step_ref
  8.3 1.2 copy-done.2
  9.5 0.8 copy-done.10
  11.0 2.0 %local_state.1 = (f32[136,1024]{1,0:T(8,128)S(1)}, f32[136,1024]{1,0:T(8,128)S(1)}) custom-call(s32[4]{0:T(128)S(1)} %pad_add_fusion.place, bf16[256,2048]{1,0:T(8,128)(2,1)S(1)} %copy-done.2, bf16[256,128]{1,0:T(8,128)(2,1)S(1)} %copy-done.10, f32[256,16]{1,0:T(8,128)S(1)} %copy.12.step_ref, f32[1,16]{1,0:T(1,128)S(1)} %bitcast.15), custom_call_target="tpu_custom_call" | custom-call | flops 134217728 | bytes 3145728 | tf_op jit(solution)/shard_map/local_state/pallas_call | solution.py:91
  13.1 1.9 %collective-permute-done.got_ref = f32[136,1024]{1,0:T(8,128)S(1)} collective-permute-done((f32[136,1024]{1,0:T(8,128)S(1)}, f32[136,1024]{1,0:T(8,128)S(1)}, u32[]{:S(2)}, u32[]{:S(2)}) %collective-permute-start) | collective-permute-done | bytes 557088 | tf_op jit(solution)/shard_map/ppermute | solution.py:476
  15.7 1.6 collective-permute-start.1
  17.3 2.9 %collective-permute-start.2 = (bf16[144,1024]{1,0:T(8,128)(2,1)S(1)}, bf16[144,1024]{1,0:T(8,128)(2,1)S(1)}, u32[]{:S(2)}, u32[]{:S(2)}) collective-permute-start(bf16[144,1024]{1,0:T(8,128)(2,1)S(1)} %chip_total.1.p0), channel_id=1, source_target_pairs={{0,16},{8,24},{16,0},{24,8},{1,17},{9,25},{17,1},{25,9},{2,18},{10... | collective-permute-start | bytes 884744 | tf_op jit(solution)/shard_map/ppermute | solution.py:472
  20.2 1.3 collective-permute-start.3
  21.6 4.5 %collective-permute-done.1.p1 = bf16[144,1024]{1,0:T(8,128)(2,1)S(1)} collective-permute-done((bf16[144,1024]{1,0:T(8,128)(2,1)S(1)}, bf16[144,1024]{1,0:T(8,128)(2,1)S(1)}, u32[]{:S(2)}, u32[]{:S(2)}) %collective-permute-start.1) | collective-permute-done | bytes 294944 | tf_op jit(solution)/shard_map/ppermute | solution.py:472
  26.1 7.5 %collective-permute-done.2.p2 = bf16[144,1024]{1,0:T(8,128)(2,1)S(1)} collective-permute-done((bf16[144,1024]{1,0:T(8,128)(2,1)S(1)}, bf16[144,1024]{1,0:T(8,128)(2,1)S(1)}, u32[]{:S(2)}, u32[]{:S(2)}) %collective-permute-start.2) | collective-permute-done | bytes 294944 | tf_op jit(solution)/shard_map/ppermute | solution.py:472
  33.6 1.0 row_total.1
  34.6 2.0 %collective-permute-start.4 = (bf16[144,1024]{1,0:T(8,128)(2,1)S(1)}, bf16[144,1024]{1,0:T(8,128)(2,1)S(1)}, u32[]{:S(2)}, u32[]{:S(2)}) collective-permute-start(bf16[144,1024]{1,0:T(8,128)(2,1)S(1)} %get-tuple-element.36.p0), channel_id=1, source_target_pairs={{0,32},{32,64},{64,96},{96,0},{1,33},{33,65},{65,97},{97,1},{2,34}... | collective-permute-start | bytes 884744 | tf_op jit(solution)/shard_map/ppermute | solution.py:472
  36.6 3.6 %collective-permute-start.5 = (bf16[144,1024]{1,0:T(8,128)(2,1)S(1)}, bf16[144,1024]{1,0:T(8,128)(2,1)S(1)}, u32[]{:S(2)}, u32[]{:S(2)}) collective-permute-start(bf16[144,1024]{1,0:T(8,128)(2,1)S(1)} %get-tuple-element.36.p0), channel_id=1, source_target_pairs={{0,64},{32,96},{64,0},{96,32},{1,65},{33,97},{65,1},{97,33},{2,66}... | collective-permute-start | bytes 884744 | tf_op jit(solution)/shard_map/ppermute | solution.py:472
  40.2 1.0 collective-permute-start.6
  41.2 1.5 turned_prior.1.prior_ref
  42.7 9.8 %collective-permute-done.4.p1 = bf16[144,1024]{1,0:T(8,128)(2,1)S(1)} collective-permute-done((bf16[144,1024]{1,0:T(8,128)(2,1)S(1)}, bf16[144,1024]{1,0:T(8,128)(2,1)S(1)}, u32[]{:S(2)}, u32[]{:S(2)}) %collective-permute-start.4) | collective-permute-done | bytes 294944 | tf_op jit(solution)/shard_map/ppermute | solution.py:472
  52.5 13.9 %collective-permute-done.5.p2 = bf16[144,1024]{1,0:T(8,128)(2,1)S(1)} collective-permute-done((bf16[144,1024]{1,0:T(8,128)(2,1)S(1)}, bf16[144,1024]{1,0:T(8,128)(2,1)S(1)}, u32[]{:S(2)}, u32[]{:S(2)}) %collective-permute-start.5) | collective-permute-done | bytes 294944 | tf_op jit(solution)/shard_map/ppermute | solution.py:472
  66.4 1.0 entering_state.1
  67.5 2.9 %plain_part.1 = (f32[256,2048]{1,0:T(8,128)S(1)}, f32[256,2048]{1,0:T(8,128)S(1)}) custom-call(bf16[256,2048]{1,0:T(8,128)(2,1)S(1)} %copy-done.3, bf16[256,2048]{1,0:T(8,128)(2,1)S(1)} %copy-done.14, bf16[256,128]{1,0:T(8,128)(2,1)S(1)} %copy-done.11, bf16[256,128]{1,0:T(8,128)(2,1)S(1)} %copy-done.9, f32[256,16]{1,0:T(8,128)S(1)} %copy.12.step_ref, ...), custom_call_target="tpu_custom_call" | custom-call | flops 268435456 | bytes 7340032 | tf_op jit(solution)/shard_map/plain_part/pallas_call | solution.py:130
  70.5 2.3 %gated_part.1 = (bf16[128,2048]{1,0:T(8,128)(2,1)S(1)}, bf16[128,2048]{1,0:T(8,128)(2,1)S(1)}, bf16[16,512]{1,0:T(8,128)(2,1)S(1)}) custom-call(s32[4]{0:T(128)S(1)} %pad_add_fusion.place, bf16[128,1024]{1,0:T(8,128)(2,1)S(1)} %get-tuple-element.38.mine_ref, bf16[128,1024]{1,0:T(8,128)(2,1)S(1)} %collective-permute-done.7.other_ref, ...), custom_call_target="tpu_custom_call" | custom-call | flops 134217728 | bytes 6291456 | tf_op jit(solution)/shard_map/gated_part/pallas_call | solution.py:313
  72.8 1.3 collective-permute-start.11
  74.1 2.0 %collective-permute-start.17 = (bf16[128,2048]{1,0:T(8,128)(2,1)S(1)}, bf16[128,2048]{1,0:T(8,128)(2,1)S(1)}, u32[]{:S(2)}, u32[]{:S(2)}) collective-permute-start(bf16[128,2048]{1,0:T(8,128)(2,1)S(1)} %get-tuple-element.43.low_ref), channel_id=1, source_target_pairs={{0,24},{8,0},{16,8},{24,16},{1,25},{9,1},{17,9},{25,17},{2,26},{10... | collective-permute-start | bytes 1572872 | tf_op jit(solution)/shard_map/ppermute | solution.py:472
  76.1 12.3 %collective-permute-done.11.top_ref = bf16[128,2048]{1,0:T(8,128)(2,1)S(1)} collective-permute-done((bf16[128,2048]{1,0:T(8,128)(2,1)S(1)}, bf16[128,2048]{1,0:T(8,128)(2,1)S(1)}, u32[]{:S(2)}, u32[]{:S(2)}) %collective-permute-start.11) | collective-permute-done | bytes 524320 | tf_op jit(solution)/shard_map/ppermute | solution.py:472
  88.4 3.2 %collective-permute-start.23 = (bf16[128,2048]{1,0:T(8,128)(2,1)S(1)}, bf16[128,2048]{1,0:T(8,128)(2,1)S(1)}, u32[]{:S(2)}, u32[]{:S(2)}) collective-permute-start(bf16[128,2048]{1,0:T(8,128)(2,1)S(1)} %collective-permute-done.17.low_ref), channel_id=1, source_target_pairs={{0,24},{8,0},{16,8},{24,16},{1,25},{9,1},{17,9},{25,17},{2,26},{10... | collective-permute-start | bytes 1572872 | tf_op jit(solution)/shard_map/ppermute | solution.py:472
  91.6 3.2 %collective-permute-start.12 = (bf16[128,2048]{1,0:T(8,128)(2,1)S(1)}, bf16[128,2048]{1,0:T(8,128)(2,1)S(1)}, u32[]{:S(2)}, u32[]{:S(2)}) collective-permute-start(bf16[128,2048]{1,0:T(8,128)(2,1)S(1)} %get-tuple-element.42.top_ref), channel_id=1, source_target_pairs={{0,24},{8,0},{16,8},{24,16},{1,25},{9,1},{17,9},{25,17},{2,26},{10... | collective-permute-start | bytes 1572872 | tf_op jit(solution)/shard_map/ppermute | solution.py:472
  94.8 9.6 %collective-permute-done.22.top_ref = bf16[128,2048]{1,0:T(8,128)(2,1)S(1)} collective-permute-done((bf16[128,2048]{1,0:T(8,128)(2,1)S(1)}, bf16[128,2048]{1,0:T(8,128)(2,1)S(1)}, u32[]{:S(2)}, u32[]{:S(2)}) %collective-permute-start.22) | collective-permute-done | bytes 524320 | tf_op jit(solution)/shard_map/ppermute | solution.py:472
  106.0 3.4 %copy-done = bf16[16384,256]{1,0:T(8,128)(2,1)S(1)} copy-done((bf16[16384,256]{1,0:T(8,128)(2,1)S(1)}, bf16[16384,256]{1,0:T(8,128)(2,1)}, u32[]{:S(2)}) %copy-start) | copy-done | bytes 8388632
  109.4 1.0 copy-done.6
  110.4 1.0 copy-done.8
  111.4 3.5 %project.7 = (bf16[256,512]{1,0:T(8,128)(2,1)S(1)}, bf16[256,512]{1,0:T(8,128)(2,1)S(1)}, bf16[256,512]{1,0:T(8,128)(2,1)S(1)}, bf16[256,512]{1,0:T(8,128)(2,1)S(1)}) custom-call(s32[4]{0:T(128)S(1)} %pad_add_fusion.place, bf16[128,2048]{1,0:T(8,128)(2,1)S(1)} %copy-done.6, bf16[128,2048]{1,0:T(8,128)(2,1)S(1)} %copy-done.8, bf16[8,2048,256]{2,1,0:T(8,128)(2,1)S(1)} %bitcast.8), custom_call_target="tpu_custom_call" | custom-call | flops 2147483648 | bytes 10485760 | tf_op jit(solution)/shard_map/project/pallas_call | solution.py:363
  115.0 1.6 collective-permute-start.24
  116.5 1.1 collective-permute-start.25
  117.7 2.2 %collective-permute-start.26 = (bf16[256,512]{1,0:T(8,128)(2,1)S(1)}, bf16[256,512]{1,0:T(8,128)(2,1)S(1)}, u32[]{:S(2)}, u32[]{:S(2)}) collective-permute-start(bf16[256,512]{1,0:T(8,128)(2,1)S(1)} %get-tuple-element.61), channel_id=1, source_target_pairs={{0,3},{1,0},{2,1},{3,2},{4,7},{5,4},{6,5},{7,6},{8,11},{9,8},{10,9... | collective-permute-start | bytes 786440 | tf_op jit(solution)/shard_map/ppermute | solution.py:472
  119.8 3.6 %project.6 = (bf16[256,512]{1,0:T(8,128)(2,1)S(1)}, bf16[256,512]{1,0:T(8,128)(2,1)S(1)}, bf16[256,512]{1,0:T(8,128)(2,1)S(1)}, bf16[256,512]{1,0:T(8,128)(2,1)S(1)}) custom-call(s32[4]{0:T(128)S(1)} %pad_add_fusion.place, bf16[128,2048]{1,0:T(8,128)(2,1)S(1)} %collective-permute-done.16.top_ref, bf16[128,2048]{1,0:T(8,128)(2,1)S(1)} %collective-permute-done.17.low_ref, ...), custom_call_target="tpu_custom_call" | custom-call | flops 2147483648 | bytes 10485760 | tf_op jit(solution)/shard_map/project/pallas_call | solution.py:363
  123.6 3.5 %collective-permute-start.19 = (bf16[256,512]{1,0:T(8,128)(2,1)S(1)}, bf16[256,512]{1,0:T(8,128)(2,1)S(1)}, u32[]{:S(2)}, u32[]{:S(2)}) collective-permute-start(bf16[256,512]{1,0:T(8,128)(2,1)S(1)} %get-tuple-element.55), channel_id=1, source_target_pairs={{0,2},{1,3},{2,0},{3,1},{4,6},{5,7},{6,4},{7,5},{8,10},{9,11},{10,... | collective-permute-start | bytes 786440 | tf_op jit(solution)/shard_map/ppermute | solution.py:472
  127.1 3.6 %project.4 = (bf16[272,512]{1,0:T(8,128)(2,1)S(1)}, bf16[272,512]{1,0:T(8,128)(2,1)S(1)}, bf16[272,512]{1,0:T(8,128)(2,1)S(1)}, bf16[272,512]{1,0:T(8,128)(2,1)S(1)}) custom-call(s32[4]{0:T(128)S(1)} %pad_add_fusion.place, bf16[128,2048]{1,0:T(8,128)(2,1)S(1)} %get-tuple-element.42.top_ref, bf16[128,2048]{1,0:T(8,128)(2,1)S(1)} %get-tuple-element.43.low_ref, ...), custom_call_target="tpu_custom_call" | custom-call | flops 2147483648 | bytes 10485760 | tf_op jit(solution)/shard_map/project/pallas_call | solution.py:363
  130.7 3.6 %project.5 = (bf16[256,512]{1,0:T(8,128)(2,1)S(1)}, bf16[256,512]{1,0:T(8,128)(2,1)S(1)}, bf16[256,512]{1,0:T(8,128)(2,1)S(1)}, bf16[256,512]{1,0:T(8,128)(2,1)S(1)}) custom-call(s32[4]{0:T(128)S(1)} %pad_add_fusion.place, bf16[128,2048]{1,0:T(8,128)(2,1)S(1)} %collective-permute-done.11.top_ref, bf16[128,2048]{1,0:T(8,128)(2,1)S(1)} %collective-permute-done.12.low_ref, ...), custom_call_target="tpu_custom_call" | custom-call | flops 2147483648 | bytes 10485760 | tf_op jit(solution)/shard_map/project/pallas_call | solution.py:363
  134.5 2.0 %collective-permute-start.13 = (bf16[256,512]{1,0:T(8,128)(2,1)S(1)}, bf16[256,512]{1,0:T(8,128)(2,1)S(1)}, u32[]{:S(2)}, u32[]{:S(2)}) collective-permute-start(bf16[256,512]{1,0:T(8,128)(2,1)S(1)} %get-tuple-element.50), channel_id=1, source_target_pairs={{0,1},{1,2},{2,3},{3,0},{4,5},{5,6},{6,7},{7,4},{8,9},{9,10},{10,1... | collective-permute-start | bytes 786440 | tf_op jit(solution)/shard_map/ppermute | solution.py:472
  136.6 1.7 collective-permute-start.14
  138.3 5.8 %collective-permute-start.15 = (bf16[256,512]{1,0:T(8,128)(2,1)S(1)}, bf16[256,512]{1,0:T(8,128)(2,1)S(1)}, u32[]{:S(2)}, u32[]{:S(2)}) collective-permute-start(bf16[256,512]{1,0:T(8,128)(2,1)S(1)} %get-tuple-element.52), channel_id=1, source_target_pairs={{0,3},{1,0},{2,1},{3,2},{4,7},{5,4},{6,5},{7,6},{8,11},{9,8},{10,9... | collective-permute-start | bytes 786440 | tf_op jit(solution)/shard_map/ppermute | solution.py:472
  144.0 4.3 %collective-permute-done.13.refs_1_ = bf16[256,512]{1,0:T(8,128)(2,1)S(1)} collective-permute-done((bf16[256,512]{1,0:T(8,128)(2,1)S(1)}, bf16[256,512]{1,0:T(8,128)(2,1)S(1)}, u32[]{:S(2)}, u32[]{:S(2)}) %collective-permute-start.13) | collective-permute-done | bytes 262176 | tf_op jit(solution)/shard_map/ppermute | solution.py:472
  148.4 1.3 collective-permute-start.9
  149.9 4.9 %collective-permute-done.14.refs_2_ = bf16[256,512]{1,0:T(8,128)(2,1)S(1)} collective-permute-done((bf16[256,512]{1,0:T(8,128)(2,1)S(1)}, bf16[256,512]{1,0:T(8,128)(2,1)S(1)}, u32[]{:S(2)}, u32[]{:S(2)}) %collective-permute-start.14) | collective-permute-done | bytes 262176 | tf_op jit(solution)/shard_map/ppermute | solution.py:472
  155.4 8.4 %collective-permute-done.15.refs_3_ = bf16[256,512]{1,0:T(8,128)(2,1)S(1)} collective-permute-done((bf16[256,512]{1,0:T(8,128)(2,1)S(1)}, bf16[256,512]{1,0:T(8,128)(2,1)S(1)}, u32[]{:S(2)}, u32[]{:S(2)}) %collective-permute-start.15) | collective-permute-done | bytes 262176 | tf_op jit(solution)/shard_map/ppermute | solution.py:472
  164.1 1.9 %collective-permute-start.21 = (bf16[256,512]{1,0:T(8,128)(2,1)S(1)}, bf16[256,512]{1,0:T(8,128)(2,1)S(1)}, u32[]{:S(2)}, u32[]{:S(2)}) collective-permute-start(bf16[256,512]{1,0:T(8,128)(2,1)S(1)} %get-tuple-element.57), channel_id=1, source_target_pairs={{0,24},{8,0},{16,8},{24,16},{1,25},{9,1},{17,9},{25,17},{2,26},{10... | collective-permute-start | bytes 786440 | tf_op jit(solution)/shard_map/ppermute | solution.py:472
  166.2 4.3 %collective-permute-done.21.up_ref = bf16[256,512]{1,0:T(8,128)(2,1)S(1)} collective-permute-done((bf16[256,512]{1,0:T(8,128)(2,1)S(1)}, bf16[256,512]{1,0:T(8,128)(2,1)S(1)}, u32[]{:S(2)}, u32[]{:S(2)}) %collective-permute-start.21) | collective-permute-done | bytes 262176 | tf_op jit(solution)/shard_map/ppermute | solution.py:472
  170.5 3.1 %collective-permute-done.28.down_ref = bf16[256,512]{1,0:T(8,128)(2,1)S(1)} collective-permute-done((bf16[256,512]{1,0:T(8,128)(2,1)S(1)}, bf16[256,512]{1,0:T(8,128)(2,1)S(1)}, u32[]{:S(2)}, u32[]{:S(2)}) %collective-permute-start.28) | collective-permute-done | bytes 262176 | tf_op jit(solution)/shard_map/ppermute | solution.py:472
  173.6 2.9 %finish.1 = bf16[256,2048]{1,0:T(8,128)(2,1)} custom-call(s32[4]{0:T(128)S(1)} %pad_add_fusion.place, bf16[272,512]{1,0:T(8,128)(2,1)S(1)} %get-tuple-element.45.p0, bf16[272,512]{1,0:T(8,128)(2,1)S(1)} %collective-permute-done.8.p1, bf16[272,512]{1,0:T(8,128)(2,1)S(1)} %collective-permute-done.9.p2, bf16[272,512]{1,0:T(8,128)(2,1)S(1)} %collective-permute-done.10.p3, ...), custom_call_target="tpu_custom_call" | custom-call | flops 2097152 | bytes 4194304 | tf_op jit(solution)/shard_map/finish/pallas_call | solution.py:456
  (66 shorter events, 5.5 us)
Async XLA Ops:
  6.5 99.4 %all-gather.3.cloned.1.call-start = ((), (), s32[]{:S(2)}) async-start(), calls=%async_computation | async-start | bytes 9437184 | tf_op jit(solution)/shard_map/all_gather | solution.py:497
  7.3 34.0 %copy-start.1 = (f32[16,128,128]{2,1,0:T(8,128)S(1)}, f32[16,128,128]{2,1,0:T(8,128)}, u32[]{:S(2)}) copy-start(f32[16,128,128]{2,1,0:T(8,128)} %prior_ref.1) | copy-start | bytes 3145732
  8.3 1.2 copy-start.2
  9.5 0.8 copy-start.10
  10.3 0.7 copy-start.13
  13.0 2.0 %collective-permute-start = (f32[136,1024]{1,0:T(8,128)S(1)}, f32[136,1024]{1,0:T(8,128)S(1)}, u32[]{:S(2)}, u32[]{:S(2)}) collective-permute-start(f32[136,1024]{1,0:T(8,128)S(1)} %get-tuple-element.35), channel_id=1, source_target_pairs={{0,4},{4,0},{1,5},{5,1},{2,6},{6,2},{3,7},{7,3},{8,12},{12,8},{9,1... | collective-permute-start | bytes 1671176 | tf_op jit(solution)/shard_map/ppermute | solution.py:476
  15.7 10.4 %collective-permute-start.1 = (bf16[144,1024]{1,0:T(8,128)(2,1)S(1)}, bf16[144,1024]{1,0:T(8,128)(2,1)S(1)}, u32[]{:S(2)}, u32[]{:S(2)}) collective-permute-start(bf16[144,1024]{1,0:T(8,128)(2,1)S(1)} %chip_total.1.p0), channel_id=1, source_target_pairs={{0,8},{8,16},{16,24},{24,0},{1,9},{9,17},{17,25},{25,1},{2,10},{10... | collective-permute-start | bytes 884744 | tf_op jit(solution)/shard_map/ppermute | solution.py:472
  17.3 16.2 %collective-permute-start.2 = (bf16[144,1024]{1,0:T(8,128)(2,1)S(1)}, bf16[144,1024]{1,0:T(8,128)(2,1)S(1)}, u32[]{:S(2)}, u32[]{:S(2)}) collective-permute-start(bf16[144,1024]{1,0:T(8,128)(2,1)S(1)} %chip_total.1.p0), channel_id=1, source_target_pairs={{0,16},{8,24},{16,0},{24,8},{1,17},{9,25},{17,1},{25,9},{2,18},{10... | collective-permute-start | bytes 884744 | tf_op jit(solution)/shard_map/ppermute | solution.py:472
  20.2 13.3 %collective-permute-start.3 = (bf16[144,1024]{1,0:T(8,128)(2,1)S(1)}, bf16[144,1024]{1,0:T(8,128)(2,1)S(1)}, u32[]{:S(2)}, u32[]{:S(2)}) collective-permute-start(bf16[144,1024]{1,0:T(8,128)(2,1)S(1)} %chip_total.1.p0), channel_id=1, source_target_pairs={{0,24},{8,0},{16,8},{24,16},{1,25},{9,1},{17,9},{25,17},{2,26},{10... | collective-permute-start | bytes 884744 | tf_op jit(solution)/shard_map/ppermute | solution.py:472
  34.6 32.9 %copy-start.3 = (bf16[256,2048]{1,0:T(8,128)(2,1)S(1)}, bf16[256,2048]{1,0:T(8,128)(2,1)}, u32[]{:S(2)}) copy-start(bf16[256,2048]{1,0:T(8,128)(2,1)} %value_ref.3) | copy-start | bytes 3145732
  34.6 32.9 %copy-start.9 = (bf16[256,128]{1,0:T(8,128)(2,1)S(1)}, bf16[256,128]{1,0:T(8,128)(2,1)}, u32[]{:S(2)}) copy-start(bf16[256,128]{1,0:T(8,128)(2,1)} %read_ref.3) | copy-start | bytes 196612
  34.6 32.9 %copy-start.11 = (bf16[256,128]{1,0:T(8,128)(2,1)S(1)}, bf16[256,128]{1,0:T(8,128)(2,1)}, u32[]{:S(2)}) copy-start(bf16[256,128]{1,0:T(8,128)(2,1)} %write_ref.3) | copy-start | bytes 196612
  34.6 32.9 %copy-start.14 = (bf16[256,2048]{1,0:T(8,128)(2,1)S(1)}, bf16[256,2048]{1,0:T(8,128)(2,1)}, u32[]{:S(2)}) copy-start(bf16[256,2048]{1,0:T(8,128)(2,1)} %gate_ref.1) | copy-start | bytes 3145732
  34.6 32.9 %copy-start.15 = (f32[16]{0:T(128)S(1)}, f32[16]{0:T(128)}, u32[]{:S(2)}) copy-start(f32[16]{0:T(128)} %param.17) | copy-start | bytes 196
  34.6 17.9 %collective-permute-start.4 = (bf16[144,1024]{1,0:T(8,128)(2,1)S(1)}, bf16[144,1024]{1,0:T(8,128)(2,1)S(1)}, u32[]{:S(2)}, u32[]{:S(2)}) collective-permute-start(bf16[144,1024]{1,0:T(8,128)(2,1)S(1)} %get-tuple-element.36.p0), channel_id=1, source_target_pairs={{0,32},{32,64},{64,96},{96,0},{1,33},{33,65},{65,97},{97,1},{2,34}... | collective-permute-start | bytes 884744 | tf_op jit(solution)/shard_map/ppermute | solution.py:472
  36.6 29.8 %collective-permute-start.5 = (bf16[144,1024]{1,0:T(8,128)(2,1)S(1)}, bf16[144,1024]{1,0:T(8,128)(2,1)S(1)}, u32[]{:S(2)}, u32[]{:S(2)}) collective-permute-start(bf16[144,1024]{1,0:T(8,128)(2,1)S(1)} %get-tuple-element.36.p0), channel_id=1, source_target_pairs={{0,64},{32,96},{64,0},{96,32},{1,65},{33,97},{65,1},{97,33},{2,66}... | collective-permute-start | bytes 884744 | tf_op jit(solution)/shard_map/ppermute | solution.py:472
  40.2 26.2 %collective-permute-start.6 = (bf16[144,1024]{1,0:T(8,128)(2,1)S(1)}, bf16[144,1024]{1,0:T(8,128)(2,1)S(1)}, u32[]{:S(2)}, u32[]{:S(2)}) collective-permute-start(bf16[144,1024]{1,0:T(8,128)(2,1)S(1)} %get-tuple-element.36.p0), channel_id=1, source_target_pairs={{0,96},{32,0},{64,32},{96,64},{1,97},{33,1},{65,33},{97,65},{2,98}... | collective-permute-start | bytes 884744 | tf_op jit(solution)/shard_map/ppermute | solution.py:472
  67.4 3.1 %copy-start.12 = (f32[2048]{0:T(1024)S(1)}, f32[2048]{0:T(1024)}, u32[]{:S(2)}) copy-start(f32[2048]{0:T(1024)} %param.19) | copy-start | bytes 24580
  67.4 3.1 %collective-permute-start.7 = (bf16[128,1024]{1,0:T(8,128)(2,1)S(1)}, bf16[128,1024]{1,0:T(8,128)(2,1)S(1)}, u32[]{:S(2)}, u32[]{:S(2)}) collective-permute-start(bf16[128,1024]{1,0:T(8,128)(2,1)S(1)} %get-tuple-element.39), channel_id=1, source_target_pairs={{0,4},{4,0},{1,5},{5,1},{2,6},{6,2},{3,7},{7,3},{8,12},{12,8},{9,1... | collective-permute-start | bytes 786440 | tf_op jit(solution)/shard_map/ppermute | solution.py:476
  72.8 15.6 %collective-permute-start.11 = (bf16[128,2048]{1,0:T(8,128)(2,1)S(1)}, bf16[128,2048]{1,0:T(8,128)(2,1)S(1)}, u32[]{:S(2)}, u32[]{:S(2)}) collective-permute-start(bf16[128,2048]{1,0:T(8,128)(2,1)S(1)} %get-tuple-element.42.top_ref), channel_id=1, source_target_pairs={{0,8},{8,16},{16,24},{24,0},{1,9},{9,17},{17,25},{25,1},{2,10},{10... | collective-permute-start | bytes 1572872 | tf_op jit(solution)/shard_map/ppermute | solution.py:472
  74.1 14.3 %collective-permute-start.17 = (bf16[128,2048]{1,0:T(8,128)(2,1)S(1)}, bf16[128,2048]{1,0:T(8,128)(2,1)S(1)}, u32[]{:S(2)}, u32[]{:S(2)}) collective-permute-start(bf16[128,2048]{1,0:T(8,128)(2,1)S(1)} %get-tuple-element.43.low_ref), channel_id=1, source_target_pairs={{0,24},{8,0},{16,8},{24,16},{1,25},{9,1},{17,9},{25,17},{2,26},{10... | collective-permute-start | bytes 1572872 | tf_op jit(solution)/shard_map/ppermute | solution.py:472
  88.3 16.0 %collective-permute-start.22 = (bf16[128,2048]{1,0:T(8,128)(2,1)S(1)}, bf16[128,2048]{1,0:T(8,128)(2,1)S(1)}, u32[]{:S(2)}, u32[]{:S(2)}) collective-permute-start(bf16[128,2048]{1,0:T(8,128)(2,1)S(1)} %collective-permute-done.11.top_ref), channel_id=1, source_target_pairs={{0,8},{8,16},{16,24},{24,0},{1,9},{9,17},{17,25},{25,1},{2,10},{10... | collective-permute-start | bytes 1572872 | tf_op jit(solution)/shard_map/ppermute | solution.py:472
  88.4 16.8 %collective-permute-start.23 = (bf16[128,2048]{1,0:T(8,128)(2,1)S(1)}, bf16[128,2048]{1,0:T(8,128)(2,1)S(1)}, u32[]{:S(2)}, u32[]{:S(2)}) collective-permute-start(bf16[128,2048]{1,0:T(8,128)(2,1)S(1)} %collective-permute-done.17.low_ref), channel_id=1, source_target_pairs={{0,24},{8,0},{16,8},{24,16},{1,25},{9,1},{17,9},{25,17},{2,26},{10... | collective-permute-start | bytes 1572872 | tf_op jit(solution)/shard_map/ppermute | solution.py:472
  91.6 28.3 %collective-permute-start.16 = (bf16[128,2048]{1,0:T(8,128)(2,1)S(1)}, bf16[128,2048]{1,0:T(8,128)(2,1)S(1)}, u32[]{:S(2)}, u32[]{:S(2)}) collective-permute-start(bf16[128,2048]{1,0:T(8,128)(2,1)S(1)} %get-tuple-element.43.low_ref), channel_id=1, source_target_pairs={{0,8},{8,16},{16,24},{24,0},{1,9},{9,17},{17,25},{25,1},{2,10},{10... | collective-permute-start | bytes 1572872 | tf_op jit(solution)/shard_map/ppermute | solution.py:472
  91.6 32.0 %collective-permute-start.12 = (bf16[128,2048]{1,0:T(8,128)(2,1)S(1)}, bf16[128,2048]{1,0:T(8,128)(2,1)S(1)}, u32[]{:S(2)}, u32[]{:S(2)}) collective-permute-start(bf16[128,2048]{1,0:T(8,128)(2,1)S(1)} %get-tuple-element.42.top_ref), channel_id=1, source_target_pairs={{0,24},{8,0},{16,8},{24,16},{1,25},{9,1},{17,9},{25,17},{2,26},{10... | collective-permute-start | bytes 1572872 | tf_op jit(solution)/shard_map/ppermute | solution.py:472
  104.4 0.8 copy-start.5
  105.2 0.8 copy-start.7
  106.0 3.4 %copy-start = (bf16[16384,256]{1,0:T(8,128)(2,1)S(1)}, bf16[16384,256]{1,0:T(8,128)(2,1)}, u32[]{:S(2)}) copy-start(bf16[16384,256]{1,0:T(8,128)(2,1)} %all-gather.3.cloned.1.call-done) | copy-start | bytes 25165828
  109.4 1.0 copy-start.6
  110.4 1.0 copy-start.8
  111.4 15.6 %slice-start = ((s8[8388608]{0:T(1024)(128)(4,1)}), s8[4194304]{0:T(1024)(128)(4,1)S(1)}, s32[]{:S(2)}) async-start(s8[8388608]{0:T(1024)(128)(4,1)} %bitcast.10), calls=%async_computation.1 | async-start | bytes 8388608
  115.0 19.4 %collective-permute-start.24 = (bf16[256,512]{1,0:T(8,128)(2,1)S(1)}, bf16[256,512]{1,0:T(8,128)(2,1)S(1)}, u32[]{:S(2)}, u32[]{:S(2)}) collective-permute-start(bf16[256,512]{1,0:T(8,128)(2,1)S(1)} %get-tuple-element.59), channel_id=1, source_target_pairs={{0,1},{1,2},{2,3},{3,0},{4,5},{5,6},{6,7},{7,4},{8,9},{9,10},{10,1... | collective-permute-start | bytes 786440 | tf_op jit(solution)/shard_map/ppermute | solution.py:472
  116.5 17.9 %collective-permute-start.25 = (bf16[256,512]{1,0:T(8,128)(2,1)S(1)}, bf16[256,512]{1,0:T(8,128)(2,1)S(1)}, u32[]{:S(2)}, u32[]{:S(2)}) collective-permute-start(bf16[256,512]{1,0:T(8,128)(2,1)S(1)} %get-tuple-element.60), channel_id=1, source_target_pairs={{0,2},{1,3},{2,0},{3,1},{4,6},{5,7},{6,4},{7,5},{8,10},{9,11},{10,... | collective-permute-start | bytes 786440 | tf_op jit(solution)/shard_map/ppermute | solution.py:472
  117.7 9.4 %slice-start.1 = ((s8[8388608]{0:T(1024)(128)(4,1)}), s8[4194304]{0:T(1024)(128)(4,1)S(1)}, s32[]{:S(2)}) async-start(s8[8388608]{0:T(1024)(128)(4,1)} %bitcast.10), calls=%async_computation.2 | async-start | bytes 8388608
  117.7 18.8 %collective-permute-start.26 = (bf16[256,512]{1,0:T(8,128)(2,1)S(1)}, bf16[256,512]{1,0:T(8,128)(2,1)S(1)}, u32[]{:S(2)}, u32[]{:S(2)}) collective-permute-start(bf16[256,512]{1,0:T(8,128)(2,1)S(1)} %get-tuple-element.61), channel_id=1, source_target_pairs={{0,3},{1,0},{2,1},{3,2},{4,7},{5,4},{6,5},{7,6},{8,11},{9,8},{10,9... | collective-permute-start | bytes 786440 | tf_op jit(solution)/shard_map/ppermute | solution.py:472
  123.5 13.1 %collective-permute-start.18 = (bf16[256,512]{1,0:T(8,128)(2,1)S(1)}, bf16[256,512]{1,0:T(8,128)(2,1)S(1)}, u32[]{:S(2)}, u32[]{:S(2)}) collective-permute-start(bf16[256,512]{1,0:T(8,128)(2,1)S(1)} %get-tuple-element.54), channel_id=1, source_target_pairs={{0,1},{1,2},{2,3},{3,0},{4,5},{5,6},{6,7},{7,4},{8,9},{9,10},{10,1... | collective-permute-start | bytes 786440 | tf_op jit(solution)/shard_map/ppermute | solution.py:472
  123.6 14.7 %collective-permute-start.19 = (bf16[256,512]{1,0:T(8,128)(2,1)S(1)}, bf16[256,512]{1,0:T(8,128)(2,1)S(1)}, u32[]{:S(2)}, u32[]{:S(2)}) collective-permute-start(bf16[256,512]{1,0:T(8,128)(2,1)S(1)} %get-tuple-element.55), channel_id=1, source_target_pairs={{0,2},{1,3},{2,0},{3,1},{4,6},{5,7},{6,4},{7,5},{8,10},{9,11},{10,... | collective-permute-start | bytes 786440 | tf_op jit(solution)/shard_map/ppermute | solution.py:472
  134.4 39.2 %copy-start.4 = (bf16[256,2048]{1,0:T(8,128)(2,1)S(1)}, bf16[256,2048]{1,0:T(8,128)(2,1)}, u32[]{:S(2)}) copy-start(bf16[256,2048]{1,0:T(8,128)(2,1)} %residual_ref.1) | copy-start | bytes 3145732
  134.4 9.7 %collective-permute-start.20 = (bf16[256,512]{1,0:T(8,128)(2,1)S(1)}, bf16[256,512]{1,0:T(8,128)(2,1)S(1)}, u32[]{:S(2)}, u32[]{:S(2)}) collective-permute-start(bf16[256,512]{1,0:T(8,128)(2,1)S(1)} %get-tuple-element.56), channel_id=1, source_target_pairs={{0,3},{1,0},{2,1},{3,2},{4,7},{5,4},{6,5},{7,6},{8,11},{9,8},{10,9... | collective-permute-start | bytes 786440 | tf_op jit(solution)/shard_map/ppermute | solution.py:472
  134.5 13.9 %collective-permute-start.13 = (bf16[256,512]{1,0:T(8,128)(2,1)S(1)}, bf16[256,512]{1,0:T(8,128)(2,1)S(1)}, u32[]{:S(2)}, u32[]{:S(2)}) collective-permute-start(bf16[256,512]{1,0:T(8,128)(2,1)S(1)} %get-tuple-element.50), channel_id=1, source_target_pairs={{0,1},{1,2},{2,3},{3,0},{4,5},{5,6},{6,7},{7,4},{8,9},{9,10},{10,1... | collective-permute-start | bytes 786440 | tf_op jit(solution)/shard_map/ppermute | solution.py:472
  136.5 29.5 %collective-permute-start.10 = (bf16[272,512]{1,0:T(8,128)(2,1)S(1)}, bf16[272,512]{1,0:T(8,128)(2,1)S(1)}, u32[]{:S(2)}, u32[]{:S(2)}) collective-permute-start(bf16[272,512]{1,0:T(8,128)(2,1)S(1)} %get-tuple-element.48), channel_id=1, source_target_pairs={{0,3},{1,0},{2,1},{3,2},{4,7},{5,4},{6,5},{7,6},{8,11},{9,8},{10,9... | collective-permute-start | bytes 835592 | tf_op jit(solution)/shard_map/ppermute | solution.py:472
  136.6 18.1 %collective-permute-start.14 = (bf16[256,512]{1,0:T(8,128)(2,1)S(1)}, bf16[256,512]{1,0:T(8,128)(2,1)S(1)}, u32[]{:S(2)}, u32[]{:S(2)}) collective-permute-start(bf16[256,512]{1,0:T(8,128)(2,1)S(1)} %get-tuple-element.51), channel_id=1, source_target_pairs={{0,2},{1,3},{2,0},{3,1},{4,6},{5,7},{6,4},{7,5},{8,10},{9,11},{10,... | collective-permute-start | bytes 786440 | tf_op jit(solution)/shard_map/ppermute | solution.py:472
  138.3 25.6 %collective-permute-start.15 = (bf16[256,512]{1,0:T(8,128)(2,1)S(1)}, bf16[256,512]{1,0:T(8,128)(2,1)S(1)}, u32[]{:S(2)}, u32[]{:S(2)}) collective-permute-start(bf16[256,512]{1,0:T(8,128)(2,1)S(1)} %get-tuple-element.52), channel_id=1, source_target_pairs={{0,3},{1,0},{2,1},{3,2},{4,7},{5,4},{6,5},{7,6},{8,11},{9,8},{10,9... | collective-permute-start | bytes 786440 | tf_op jit(solution)/shard_map/ppermute | solution.py:472
  144.0 22.2 %collective-permute-start.8 = (bf16[272,512]{1,0:T(8,128)(2,1)S(1)}, bf16[272,512]{1,0:T(8,128)(2,1)S(1)}, u32[]{:S(2)}, u32[]{:S(2)}) collective-permute-start(bf16[272,512]{1,0:T(8,128)(2,1)S(1)} %get-tuple-element.46), channel_id=1, source_target_pairs={{0,1},{1,2},{2,3},{3,0},{4,5},{5,6},{6,7},{7,4},{8,9},{9,10},{10,1... | collective-permute-start | bytes 835592 | tf_op jit(solution)/shard_map/ppermute | solution.py:472
  148.4 17.8 %collective-permute-start.9 = (bf16[272,512]{1,0:T(8,128)(2,1)S(1)}, bf16[272,512]{1,0:T(8,128)(2,1)S(1)}, u32[]{:S(2)}, u32[]{:S(2)}) collective-permute-start(bf16[272,512]{1,0:T(8,128)(2,1)S(1)} %get-tuple-element.47), channel_id=1, source_target_pairs={{0,2},{1,3},{2,0},{3,1},{4,6},{5,7},{6,4},{7,5},{8,10},{9,11},{10,... | collective-permute-start | bytes 835592 | tf_op jit(solution)/shard_map/ppermute | solution.py:472
  154.7 11.5 %collective-permute-start.27 = (bf16[256,512]{1,0:T(8,128)(2,1)S(1)}, bf16[256,512]{1,0:T(8,128)(2,1)S(1)}, u32[]{:S(2)}, u32[]{:S(2)}) collective-permute-start(bf16[256,512]{1,0:T(8,128)(2,1)S(1)} %far_sums.1), channel_id=1, source_target_pairs={{0,16},{8,24},{16,0},{24,8},{1,17},{9,25},{17,1},{25,9},{2,18},{10... | collective-permute-start | bytes 786440 | tf_op jit(solution)/shard_map/ppermute | solution.py:472
  164.1 6.4 %collective-permute-start.21 = (bf16[256,512]{1,0:T(8,128)(2,1)S(1)}, bf16[256,512]{1,0:T(8,128)(2,1)S(1)}, u32[]{:S(2)}, u32[]{:S(2)}) collective-permute-start(bf16[256,512]{1,0:T(8,128)(2,1)S(1)} %get-tuple-element.57), channel_id=1, source_target_pairs={{0,24},{8,0},{16,8},{24,16},{1,25},{9,1},{17,9},{25,17},{2,26},{10... | collective-permute-start | bytes 786440 | tf_op jit(solution)/shard_map/ppermute | solution.py:472
  166.0 7.6 %collective-permute-start.28 = (bf16[256,512]{1,0:T(8,128)(2,1)S(1)}, bf16[256,512]{1,0:T(8,128)(2,1)S(1)}, u32[]{:S(2)}, u32[]{:S(2)}) collective-permute-start(bf16[256,512]{1,0:T(8,128)(2,1)S(1)} %get-tuple-element.62), channel_id=1, source_target_pairs={{0,8},{8,16},{16,24},{24,0},{1,9},{9,17},{17,25},{25,1},{2,10},{10... | collective-permute-start | bytes 786440 | tf_op jit(solution)/shard_map/ppermute | solution.py:472
Sparse Core Ops, SparseCore 0:
  9.1 64.9 all-gather.2

commit v2 on v1

v2 whole, which is shorter than its diff:
```python
import functools

import jax
import jax.numpy as jnp
from jax import lax
from jax.experimental import pallas as pl
from jax.experimental.pallas import tpu as pltpu
from jax.sharding import Mesh, PartitionSpec as P

EPSILON = 1e-05
ROWS = 256
HALF = 128
HEADS = 16
WIDTH = 128
LANES = HEADS * WIDTH
SLICE = LANES // 8
SPLIT = LANES // 2
PIECE = 512
INNER = 8192
F32 = jnp.float32
BF16 = jnp.bfloat16
HIGHEST = lax.Precision.HIGHEST
VMEM = pl.BlockSpec(memory_space=pltpu.VMEM)
SMEM = pl.BlockSpec(memory_space=pltpu.SMEM)


def params(mib=16):
    return pltpu.CompilerParams(vmem_limit_bytes=mib * 2**20)


ANY = pl.BlockSpec(memory_space=pl.ANY)


def cost(flops, bytes_accessed, transcendentals=0):
    return pl.CostEstimate(
        flops=flops, bytes_accessed=bytes_accessed, transcendentals=transcendentals
    )


def lower(rows):
    return lax.broadcasted_iota(jnp.int32, (rows, rows), 0) >= lax.broadcasted_iota(
        jnp.int32, (rows, rows), 1
    )


def cumulate(step, rate):
    ones = jnp.where(lower(ROWS), 1.0, 0.0).astype(F32)
    column = jnp.broadcast_to(rate, (8, HEADS)).T[:, 0:1]
    return lax.dot_general(
        -step * column,
        ones,
        (((1,), (1,)), ((), ())),
        precision=HIGHEST,
        preferred_element_type=F32,
    )


def three(row):
    high = row.astype(BF16)
    rest = row - high.astype(F32)
    middle = rest.astype(BF16)
    last = (rest - middle.astype(F32)).astype(BF16)
    return high.astype(F32), middle.astype(F32), last.astype(F32)


def stack_rows(rows, count):
    width = rows[0].shape[1]
    index = lax.broadcasted_iota(jnp.int32, (count, width), 0)
    result = jnp.zeros((count, width), F32)
    for place, row in enumerate(rows):
        result = jnp.where(index == place, row, result)
    return result


def unpack_rows(block):
    block = block.astype(F32)
    return block[0:1] + block[1:2] + block[2:3]


def state_kernel(place, value_ref, write_ref, step_ref, rate_ref, keep_ref, send_ref, state, logs):
    core = place[0]
    step = step_ref[...]
    across = cumulate(step, rate_ref[...])
    to_end = (jnp.exp(across[:, ROWS - 1 : ROWS] - across) * step).T
    last = across.T[ROWS - 1 : ROWS]
    write = write_ref[...].T
    for head in range(HEADS):
        at = slice(head * WIDTH, (head + 1) * WIDTH)
        weighted = (value_ref[:, at].astype(F32) * to_end[:, head : head + 1]).astype(BF16)
        state[:, at] = jnp.dot(write, weighted, preferred_element_type=F32)
        logs[:, at] = jnp.broadcast_to(last[:, head : head + 1], (8, WIDTH))
    mine = pl.ds(pl.multiple_of(core * SPLIT, SPLIT), SPLIT)
    other = pl.ds(pl.multiple_of((1 - core) * SPLIT, SPLIT), SPLIT)
    keep_ref[0:WIDTH, :] = state[:, mine]
    keep_ref[WIDTH:, :] = logs[:, mine]
    send_ref[0:WIDTH, :] = state[:, other]
    send_ref[WIDTH:, :] = logs[:, other]


def whole(shape):
    return pl.BlockSpec(shape, lambda i, place: (0,) * len(shape))


def local_state(place, values, writes, steps, rate):
    shape = (WIDTH + 8, SPLIT)
    return pl.pallas_call(
        state_kernel,
        grid_spec=pltpu.PrefetchScalarGridSpec(
            num_scalar_prefetch=1,
            grid=(1,),
            in_specs=[whole(part.shape) for part in (values, writes, steps, rate)],
            out_specs=[whole(shape), whole(shape)],
            scratch_shapes=[pltpu.VMEM((WIDTH, LANES), F32), pltpu.VMEM((8, LANES), F32)],
        ),
        out_shape=[jax.ShapeDtypeStruct(shape, F32)] * 2,
        compiler_params=params(48),
        cost_estimate=cost(2 * WIDTH * ROWS * LANES, 3 * 2**20),
        name="local_state",
    )(place, values, writes, steps, rate)


def plain_kernel(
    value_ref, gate_ref, write_ref, read_ref, step_ref, rate_ref, skip_ref, _, plain_ref, scale_ref
):
    step = step_ref[...]
    across = cumulate(step, rate_ref[...])
    cumulative = across.T
    decay = jnp.exp(cumulative)
    scores = lax.dot_general(
        read_ref[...], write_ref[...], (((1,), (1,)), ((), ())), preferred_element_type=F32
    )
    scores = jnp.where(lower(ROWS), scores, 0.0)
    for head in range(HEADS):
        at = slice(head * WIDTH, (head + 1) * WIDTH)
        spread = jnp.minimum(cumulative[:, head : head + 1] - across[head : head + 1, :], 0.0)
        mixing = (jnp.exp(spread) * scores * step[head : head + 1, :]).astype(BF16)
        value = value_ref[:, at]
        within = jnp.dot(mixing, value, preferred_element_type=F32)
        within = within + skip_ref[:, head : head + 1] * value.astype(F32)
        gate = gate_ref[:, at].astype(F32)
        gate = gate / (1.0 + jnp.exp(-gate))
        plain_ref[:, at] = within * gate
        scale_ref[:, at] = decay[:, head : head + 1] * gate


def plain_part(values, gates, writes, reads, steps, rate, skip, after):
    shape = jax.ShapeDtypeStruct((ROWS, LANES), F32)
    return pl.pallas_call(
        plain_kernel,
        out_shape=(shape, shape),
        in_specs=[VMEM] * 7 + [ANY],
        out_specs=(VMEM, VMEM),
        compiler_params=params(),
        cost_estimate=cost(
            2 * ROWS * ROWS * LANES, 7 * 2**20, HEADS * ROWS * ROWS + ROWS * LANES
        ),
        name="plain_part",
    )(values, gates, writes, reads, steps, rate, skip, after)


def turn_kernel(place, prior_ref, _, out_ref):
    out_ref[...] = prior_ref[0].T


def turned_prior(place, prior, after):
    heads = 2
    first = lambda place: 4 * place[0] + place[2]
    return pl.pallas_call(
        turn_kernel,
        grid_spec=pltpu.PrefetchScalarGridSpec(
            num_scalar_prefetch=1,
            grid=(heads,),
            in_specs=[
                pl.BlockSpec((1, WIDTH, WIDTH), lambda i, place: (first(place) * heads + i, 0, 0)),
                ANY,
            ],
            out_specs=pl.BlockSpec((WIDTH, WIDTH), lambda i, place: (0, i)),
        ),
        out_shape=jax.ShapeDtypeStruct((WIDTH, SLICE), F32),
        compiler_params=params(),
        cost_estimate=cost(0, 2**20),
        name="turned_prior",
    )(place, prior, after)


MESSAGE = jax.ShapeDtypeStruct((WIDTH + 16, SLICE), BF16)


def write_message(out_ref, state, log):
    out_ref[0:WIDTH, :] = state.astype(BF16)
    out_ref[WIDTH:, :] = stack_rows(three(log), 16).astype(BF16)


def slice_of(place, k):
    return pl.ds(pl.multiple_of(lax.rem(place[2] + k + 4, 4) * SLICE, SLICE), SLICE)


def chip_kernel(place, keep_ref, got_ref, *refs):
    outs, total, logs = refs[:4], refs[4], refs[5]
    first = place[0] == 0
    kept, got = keep_ref[...], got_ref[...]
    state0 = jnp.where(first, kept, got)
    state1 = jnp.where(first, got, kept)
    log1 = state1[WIDTH : WIDTH + 1]
    total[...] = jnp.exp(log1) * state0[0:WIDTH] + state1[0:WIDTH]
    logs[...] = state0[WIDTH:] + state1[WIDTH:]
    for k, out_ref in enumerate(outs):
        at = slice_of(place, k)
        write_message(out_ref, total[:, at], logs[0:1, at])


def chip_total(place, keep, got):
    pieces = pl.pallas_call(
        chip_kernel,
        out_shape=[MESSAGE] * 4,
        in_specs=[SMEM] + [VMEM] * 2,
        out_specs=[VMEM] * 4,
        scratch_shapes=[pltpu.VMEM((WIDTH, SPLIT), F32), pltpu.VMEM((8, SPLIT), F32)],
        compiler_params=params(),
        cost_estimate=cost(2 * WIDTH * SPLIT, 2**20),
        name="chip_total",
    )(place, keep, got)
    return list(pieces)


def fold(here, parts, before):
    logs = [unpack_rows(part[WIDTH : WIDTH + 16, :]) for part in parts]
    at = [lax.rem(here - k + 4, 4) for k in range(4)]
    total = jnp.zeros((WIDTH, SLICE), F32)
    log = jnp.zeros_like(logs[0])
    for k in range(4):
        after = jnp.zeros_like(log)
        for j in range(4):
            if j != k:
                counts = jnp.logical_and(at[j] > at[k], at[j] < before)
                after = after + jnp.where(counts, logs[j], 0.0)
        weight = jnp.where(at[k] < before, jnp.exp(after), 0.0)
        total = total + weight * parts[k][0:WIDTH, :].astype(F32)
        log = log + jnp.where(at[k] < before, logs[k], 0.0)
    return total, log


def row_kernel(place, p0, p1, p2, p3, _plain, _prior, out_ref, before_ref):
    parts = (p0, p1, p2, p3)
    write_message(out_ref, *fold(place[2], parts, 4))
    for k in range(4):
        total, log = fold(place[2], parts, lax.rem(place[2] + k, 4))
        before_ref[k, 0:WIDTH, :] = total
        before_ref[k, WIDTH:, :] = jnp.broadcast_to(log, (8, SLICE))


def row_total(place, parts, after):
    return pl.pallas_call(
        row_kernel,
        out_shape=(MESSAGE, jax.ShapeDtypeStruct((4, WIDTH + 8, SLICE), F32)),
        in_specs=[SMEM] + [VMEM] * 4 + [ANY] * 2,
        out_specs=(VMEM, VMEM),
        compiler_params=params(),
        cost_estimate=cost(40 * WIDTH * SLICE, 2**20),
        name="row_total",
    )(place, *parts, *after)


def row_enter_kernel(place, p0, p1, p2, p3, before_ref, prior_ref, *refs):
    total, log = fold(place[3], (p0, p1, p2, p3), place[3])
    entering = total + jnp.exp(log) * prior_ref[...]
    for k, out_ref in enumerate(refs[-4:]):
        decay = jnp.exp(before_ref[k, WIDTH : WIDTH + 1, :])
        out_ref[...] = (decay * entering + before_ref[k, 0:WIDTH, :]).astype(BF16)


def row_enter(place, parts, before, prior, after):
    pieces = pl.pallas_call(
        row_enter_kernel,
        out_shape=[jax.ShapeDtypeStruct((WIDTH, SLICE), BF16)] * 4,
        in_specs=[SMEM] + [VMEM] * 6 + [ANY] * len(after),
        out_specs=[VMEM] * 4,
        compiler_params=params(),
        cost_estimate=cost(16 * WIDTH * SLICE, 2**20),
        name="row_enter",
    )(place, *parts, before, prior, *after)
    return list(pieces)


def enter_kernel(place, p0, p1, p2, p3, keep_ref, got_ref, mine_ref, other_ref, chip):
    first = place[0] == 0
    for k, part in enumerate((p0, p1, p2, p3)):
        chip[:, slice_of(place, -k)] = part[...].astype(F32)
    entering = chip[...]
    state0 = jnp.where(first, keep_ref[...], got_ref[...])
    second = jnp.exp(state0[WIDTH : WIDTH + 1]) * entering + state0[0:WIDTH]
    mine_ref[...] = jnp.where(first, entering, second).astype(BF16)
    other_ref[...] = jnp.where(first, second, entering).astype(BF16)


def entering_state(place, parts, keep, got):
    shape = jax.ShapeDtypeStruct((WIDTH, SPLIT), BF16)
    return pl.pallas_call(
        enter_kernel,
        out_shape=(shape, shape),
        in_specs=[SMEM] + [VMEM] * 6,
        out_specs=(VMEM, VMEM),
        scratch_shapes=[pltpu.VMEM((WIDTH, SPLIT), F32)],
        compiler_params=params(),
        cost_estimate=cost(8 * WIDTH * SPLIT, 2 * 2**20),
        name="entering_state",
    )(place, *parts, keep, got)


def gated_kernel(
    place, mine_ref, other_ref, read_ref, plain_ref, scale_ref, gain_ref, top_ref, low_ref, stat_ref, acc
):
    step = pl.program_id(0)
    mine = place[0] == step // 2
    entering = jnp.where(mine, mine_ref[...], other_ref[...])
    carried = jnp.dot(read_ref[...], entering, preferred_element_type=F32)
    gated = plain_ref[...] + scale_ref[...] * carried
    result = (gated * gain_ref[...]).astype(BF16)
    top_ref[...] = result[:HALF]
    low_ref[...] = result[HALF:]
    square = gated * gated
    part = square[:, 0:128]
    for at in range(128, square.shape[1], 128):
        part = part + square[:, at : at + 128]

    @pl.when(step == 0)
    def _():
        acc[...] = part

    @pl.when(step > 0)
    def _():
        acc[...] += part

    @pl.when(step == pl.num_programs(0) - 1)
    def _():
        row = jnp.sum(acc[...].T, axis=0, keepdims=True)
        stat_ref[...] = jnp.zeros_like(stat_ref)
        stat_ref[:, 0:ROWS] = stack_rows(three(row), 16).astype(BF16)


def gated_part(place, mine, other, reads, plain, scale, gain):
    steps = 4
    width = LANES // steps
    half = pl.BlockSpec((HALF, width), lambda i, place: (0, i))
    wide = pl.BlockSpec((ROWS, width), lambda i, place: (0, i))
    state = pl.BlockSpec((WIDTH, width), lambda i, place: (0, lax.rem(i, 2)))
    return pl.pallas_call(
        gated_kernel,
        grid_spec=pltpu.PrefetchScalarGridSpec(
            num_scalar_prefetch=1,
            grid=(steps,),
            in_specs=[
                state,
                state,
                whole((ROWS, WIDTH)),
                wide,
                wide,
                pl.BlockSpec((1, width), lambda i, place: (0, i)),
            ],
            out_specs=[half, half, whole((16, PIECE))],
            scratch_shapes=[pltpu.VMEM((ROWS, 128), F32)],
        ),
        out_shape=(
            jax.ShapeDtypeStruct((HALF, LANES), BF16),
            jax.ShapeDtypeStruct((HALF, LANES), BF16),
            jax.ShapeDtypeStruct((16, PIECE), BF16),
        ),
        compiler_params=params(),
        cost_estimate=cost(2 * ROWS * WIDTH * LANES, 6 * 2**20),
        name="gated_part",
    )(place, mine, other, reads, plain, scale, gain)


def project_kernel(has_stats, place, top_ref, low_ref, *refs):
    core, x, z = place[0], place[1], place[3]
    outs = refs[-4:]
    sides = (refs[0:5], refs[5:10])
    depth = LANES // 2
    left = jnp.concatenate([top_ref[...], low_ref[...]], axis=0)
    for j in range(4):
        k = lax.rem(z - x + j + 4, 4)
        for side in range(2):
            own, above, below, first, second = sides[side]
            at = pl.ds(pl.multiple_of(256 * (core if side == 0 else 1 - core), 256), 256)
            if j == 2:
                total = jnp.dot(left[:, :depth], first[...], preferred_element_type=F32)
                total += jnp.dot(left[:, depth:], second[...], preferred_element_type=F32)
            else:
                weight = {0: own, 1: above, 3: below}[j]
                total = jnp.dot(left, weight[...], preferred_element_type=F32)
            total = total.astype(BF16)
            for place_k, out_ref in enumerate(outs):

                @pl.when(k == place_k)
                def _(out_ref=out_ref, at=at, total=total):
                    out_ref[0:ROWS, at] = total

    if has_stats:
        for out_ref in outs:
            out_ref[ROWS:, :] = refs[10][...]


def project(place, top, low, weights, stats=None, after=()):
    rows = ROWS if stats is None else ROWS + 16
    extra = () if stats is None else (stats,)
    pieces = pl.pallas_call(
        functools.partial(project_kernel, stats is not None),
        in_specs=[SMEM] + [VMEM] * (12 + len(extra)) + [ANY] * len(after),
        out_specs=[VMEM] * 4,
        out_shape=[jax.ShapeDtypeStruct((rows, PIECE), BF16)] * 4,
        compiler_params=params(24),
        cost_estimate=cost(2 * ROWS * LANES * 4 * PIECE, 10 * 2**20),
        name="project",
    )(place, top, low, *weights, *extra, *after)
    return list(pieces)


def add(parts, rows):
    total = parts[0][rows, :].astype(F32)
    for part in parts[1:]:
        total = total + part[rows, :].astype(F32)
    return total


def sums_kernel(*refs):
    first, second, (down_ref, up_ref) = refs[0:4], refs[4:8], refs[8:]
    for at, parts in ((0, first), (HALF, second)):
        down_ref[at : at + HALF, :] = add(parts, slice(0, HALF)).astype(BF16)
        up_ref[at : at + HALF, :] = add(parts, slice(HALF, ROWS)).astype(BF16)


def neighbour_sums(first, second):
    shape = jax.ShapeDtypeStruct((ROWS, PIECE), BF16)
    return pl.pallas_call(
        sums_kernel,
        out_shape=(shape, shape),
        in_specs=[VMEM] * 8,
        out_specs=(VMEM, VMEM),
        compiler_params=params(),
        cost_estimate=cost(8 * ROWS * PIECE, 10 * ROWS * PIECE * 2),
        name="neighbour_sums",
    )(*first, *second)


def sum_kernel(*refs):
    refs[4][...] = add(refs[0:4], slice(0, ROWS)).astype(BF16)


def far_sums(parts):
    return pl.pallas_call(
        sum_kernel,
        out_shape=jax.ShapeDtypeStruct((ROWS, PIECE), BF16),
        in_specs=[VMEM] * 4,
        out_specs=VMEM,
        compiler_params=params(),
        cost_estimate=cost(4 * ROWS * PIECE, 5 * ROWS * PIECE * 2),
        name="far_sums",
    )(*parts)


def finish_kernel(place, p0, p1, p2, p3, up_ref, far_ref, down_ref, residual_ref, out_ref):
    own = (p0, p1, p2, p3)
    square = sum(unpack_rows(part[ROWS : ROWS + 16, 0:ROWS]) for part in own)
    row = lax.rsqrt(square / INNER + EPSILON)
    scale = jnp.broadcast_to(row, (128, ROWS)).T
    step = pl.program_id(0)

    def write(total):
        for at in range(0, PIECE, 128):
            cols = slice(at, at + 128)
            out_ref[:, cols] = (residual_ref[:, cols].astype(F32) + scale * total[:, cols]).astype(
                BF16
            )

    @pl.when(step == 0)
    def _():
        write(add(own, slice(0, ROWS)))

    for k, ref in ((1, up_ref), (2, far_ref), (3, down_ref)):

        @pl.when(step == k)
        def _(ref=ref):
            write(ref[...].astype(F32))


def finish(place, own, up, far, down, residual):
    block = pl.BlockSpec((ROWS, PIECE), lambda i, place: (0, lax.rem(place[2] + i, 4)))
    return pl.pallas_call(
        finish_kernel,
        grid_spec=pltpu.PrefetchScalarGridSpec(
            num_scalar_prefetch=1,
            grid=(4,),
            in_specs=[whole((ROWS + 16, PIECE))] * 4 + [whole((ROWS, PIECE))] * 3 + [block],
            out_specs=block,
        ),
        out_shape=jax.ShapeDtypeStruct((ROWS, 4 * PIECE), BF16),
        compiler_params=params(),
        cost_estimate=cost(4 * ROWS * 4 * PIECE, 4 * 2**20),
        name="finish",
    )(place, *own, up, far, down, residual)


def shift(value, axis, by):
    return lax.ppermute(value, axis, [(i, (i + by) % 4) for i in range(4)])


def swap(value):
    return lax.ppermute(value, "core", [(0, 1), (1, 0)])


def later(values, events):
    return lax.optimization_barrier((tuple(values), tuple(events)))[0]


def scatter(pieces, axis="x"):
    return [pieces[0]] + [shift(pieces[k], axis, k) for k in (1, 2, 3)]


def body(
    head_values,
    gate_values,
    write_keys,
    read_keys,
    step_size,
    decay_rate,
    skip_weight,
    prior_state,
    norm_gain,
    out_weight,
    residual,
):
    place = jnp.stack([lax.axis_index(name) for name in ("core", "x", "y", "z")]).astype(jnp.int32)
    rate = decay_rate[None, :]

    steps = step_size.T
    from_below, from_above = shift(out_weight, "z", 1), shift(out_weight, "z", -1)
    keep, send = local_state(place, head_values, write_keys, steps, rate)
    got = swap(send)
    chips = chip_total(place, keep, got)
    plain, scale = plain_part(
        head_values, gate_values, write_keys, read_keys, steps, rate, skip_weight[None, :], chips[0]
    )
    prior = turned_prior(place, prior_state, chips[0])
    row, before = row_total(place, scatter(chips, "y"), (plain, prior))
    rows = scatter([row] * 4, "z")
    kept = [out_weight, from_above, from_below]
    swapped = [swap(part) for part in kept]
    entering = scatter(row_enter(place, rows, before, prior, kept[1:]), "y")
    depth = out_weight.shape[0] // 2
    kept += [shift(from_below[:depth], "z", 1), shift(from_above[depth:], "z", -1)]
    mine, other = entering_state(place, entering, keep, got)
    other = swap(other)
    top, low, stats = gated_part(place, mine, other, read_keys, plain, scale, norm_gain[None, :])
    swapped += [swap(part) for part in later(kept[3:], [stats])]
    weights = kept + swapped

    top_below, top_above = shift(top, "y", 1), shift(top, "y", -1)
    low_below, low_above = shift(low, "y", 1), shift(low, "y", -1)

    own = scatter(project(place, top, low, weights, stats))
    first = project(place, top_below, top_above, weights, None, own[:1])
    top_go, low_go = later((top_below, low_above), (top_above, low_below, first[0]))
    top_far, low_far = shift(top_go, "y", 1), shift(low_go, "y", -1)
    second = project(place, low_below, low_above, weights, None, own[1:] + first[:1])
    first = scatter(first)
    far = scatter(project(place, top_far, low_far, weights, None, first[1:] + second[:1]))
    second = scatter(second)

    down, up = neighbour_sums(first, second)
    from_above = shift(down, "y", -1)
    from_below = shift(up, "y", 1)
    from_far = shift(far_sums(far), "y", 2)
    return finish(place, own, from_above, from_far, from_below, residual)


def solution(mesh):
    grid = Mesh(mesh.devices.reshape(4, 4, 2, 4), ("z", "y", "core", "x"))
    ctx = ("z", "y", "core")
    in_specs = (
        P(ctx, "x"),
        P(ctx, "x"),
        P(ctx, None),
        P(ctx, None),
        P(ctx, "x"),
        P("x"),
        P("x"),
        P("x", None, None),
        P("x"),
        P("x", ctx),
        P(ctx, "x"),
    )
    return jax.shard_map(
        body, mesh=grid, in_specs=in_specs, out_specs=P(ctx, "x"), check_vma=False
    )
```

time: 184 us -> 133 us (0.72)
  waiting for transfers between devices: 85.3 us -> 31.1 us
  between operations: 13.7 us -> 0.3 us
  starting transfers between devices: 44.5 us -> 57.5 us
  Pallas kernels: 29 us -> 39.7 us
  local copies, waits for them, and re-layouts: 10.7 us -> 3.55 us
    ppermute x27 -> x34, waiting for transfers between devices: 82.6 us -> 27.4 us  [shift(): return lax.ppermute(value, axis, [(i, (i + by) % 4) for i in range(4)])]
    ppermute x27 -> x34, starting transfers between devices: 44.4 us -> 56.2 us  [shift(): return lax.ppermute(value, axis, [(i, (i + by) % 4) for i in range(4)])]
    pallas_call x7 -> x8, Pallas kernels: 18.1 us -> 29.7 us  [the longest x4 24.9 us: project(): pl.pallas_call(functools.partial(project_kernel, stats is not None), in_s...]
    unnamed x37 -> x26, local copies, waits for them, and re-layouts: 10.7 us -> 3.48 us
    ppermute x2 -> x7, waiting for transfers between devices: 1.95 us -> 3.7 us  [swap(): return lax.ppermute(value, 'core', [(0, 1), (1, 0)])]
  transfers between devices with their start and end apart: 30 -> 41, of which waited for: 12 -> 15; matrix products, arithmetic and copies ran while one was open for 1% -> 0% of each run, Pallas kernels for 14% -> 27%
where the time goes in v2:
time: 133 us; the launch traced here: 132 us
  starting transfers between devices  57.5 us (43%)
  Pallas kernels  39.7 us (30%)
  waiting for transfers between devices  31.1 us (23%)
  local copies, waits for them, and re-layouts  3.55 us (3%)
    ppermute x34, starting transfers between devices, shift(): return lax.ppermute(value, axis, [(i, (i + by) % 4) for i in range(4)])  56.2 us
    ppermute x34, waiting for transfers between devices, shift(): return lax.ppermute(value, axis, [(i, (i + by) % 4) for i in range(4)])  27.4 us
    pallas_call x4, Pallas kernels, project(): pl.pallas_call(functools.partial(project_kernel, stats is not None), in_s...  24.9 us
    ppermute x7, waiting for transfers between devices, swap(): return lax.ppermute(value, 'core', [(0, 1), (1, 0)])  3.7 us
    unnamed x26, local copies, waits for them, and re-layouts  3.48 us
    pallas_call x1, Pallas kernels, finish(): pl.pallas_call(finish_kernel, grid_spec=pltpu.PrefetchScalarGridSpec(num_...  2.86 us
    pallas_call x1, Pallas kernels, plain_part(): pl.pallas_call(plain_kernel, out_shape=(shape, shape), in_specs=[VMEM] *...  2.85 us
  transfers between devices with their start and end apart: 41, of which 15 were waited for; matrix products, arithmetic and copies ran while one was open for 0% of the time, Pallas kernels for 27%

profile of v2, /device:TPU:2, one launch (start us, length us, event | category | flops | bytes accessed | tf_op | source)
XLA Modules:
  0.0 132.3 jit_solution(16040084053088982862)
XLA Ops:
  0.0 4.0 %collective-permute-start.7 = (bf16[2048,256]{1,0:T(8,128)(2,1)}, bf16[2048,256]{1,0:T(8,128)(2,1)S(1)}, u32[]{:S(2)}, u32[]{:S(2)}) collective-permute-start(bf16[2048,256]{1,0:T(8,128)(2,1)} %refs_0_.7), channel_id=1, source_target_pairs={{0,96},{32,0},{64,32},{96,64},{1,97},{33,1},{65,33},{97,65},{2,98}... | collective-permute-start | bytes 3145736 | tf_op jit(solution)/shard_map/ppermute | solution.py:504
  4.1 1.2 copy-done.1
  7.6 2.4 %local_state.1 = (f32[136,1024]{1,0:T(8,128)S(1)}, f32[136,1024]{1,0:T(8,128)S(1)}) custom-call(s32[4]{0:T(128)S(1)} %pad_add_fusion.place, bf16[256,2048]{1,0:T(8,128)(2,1)S(1)} %copy-done.1, bf16[256,128]{1,0:T(8,128)(2,1)S(1)} %copy-done.5, f32[16,256]{1,0:T(8,128)S(1)} %bitcast.8, f32[1,16]{1,0:T(1,128)S(1)} %bitcast.11), custom_call_target="tpu_custom_call" | custom-call | flops 134217728 | bytes 3145728 | tf_op jit(solution)/shard_map/local_state/pallas_call | solution.py:106
  10.1 1.9 %collective-permute-done.got_ref = f32[136,1024]{1,0:T(8,128)S(1)} collective-permute-done((f32[136,1024]{1,0:T(8,128)S(1)}, f32[136,1024]{1,0:T(8,128)S(1)}, u32[]{:S(2)}, u32[]{:S(2)}) %collective-permute-start) | collective-permute-done | bytes 557088 | tf_op jit(solution)/shard_map/ppermute | solution.py:508
  12.9 1.6 %collective-permute-start.1 = (bf16[144,256]{1,0:T(8,128)(2,1)S(1)}, bf16[144,256]{1,0:T(8,128)(2,1)S(1)}, u32[]{:S(2)}, u32[]{:S(2)}) collective-permute-start(bf16[144,256]{1,0:T(8,128)(2,1)S(1)} %get-tuple-element.49), channel_id=1, source_target_pairs={{0,8},{8,16},{16,24},{24,0},{1,9},{9,17},{17,25},{25,1},{2,10},{10... | collective-permute-start | bytes 221192 | tf_op jit(solution)/shard_map/ppermute | solution.py:504
  14.5 2.9 %collective-permute-start.2 = (bf16[144,256]{1,0:T(8,128)(2,1)S(1)}, bf16[144,256]{1,0:T(8,128)(2,1)S(1)}, u32[]{:S(2)}, u32[]{:S(2)}) collective-permute-start(bf16[144,256]{1,0:T(8,128)(2,1)S(1)} %get-tuple-element.50), channel_id=1, source_target_pairs={{0,16},{8,24},{16,0},{24,8},{1,17},{9,25},{17,1},{25,9},{2,18},{10... | collective-permute-start | bytes 221192 | tf_op jit(solution)/shard_map/ppermute | solution.py:504
  17.4 1.3 %collective-permute-start.3 = (bf16[144,256]{1,0:T(8,128)(2,1)S(1)}, bf16[144,256]{1,0:T(8,128)(2,1)S(1)}, u32[]{:S(2)}, u32[]{:S(2)}) collective-permute-start(bf16[144,256]{1,0:T(8,128)(2,1)S(1)} %get-tuple-element.51), channel_id=1, source_target_pairs={{0,24},{8,0},{16,8},{24,16},{1,25},{9,1},{17,9},{25,17},{2,26},{10... | collective-permute-start | bytes 221192 | tf_op jit(solution)/shard_map/ppermute | solution.py:504
  19.6 2.9 %plain_part.1 = (f32[256,2048]{1,0:T(8,128)S(1)}, f32[256,2048]{1,0:T(8,128)S(1)}) custom-call(bf16[256,2048]{1,0:T(8,128)(2,1)S(1)} %copy-done.1, bf16[256,2048]{1,0:T(8,128)(2,1)S(1)} %copy-done.11, bf16[256,128]{1,0:T(8,128)(2,1)S(1)} %copy-done.6, bf16[256,128]{1,0:T(8,128)(2,1)S(1)} %copy-done.4, f32[16,256]{1,0:T(8,128)S(1)} %bitcast.9, ...), custom_call_target="tpu_custom_call" | custom-call | flops 268435456 | bytes 7340032 | tf_op jit(solution)/shard_map/plain_part/pallas_call | solution.py:148
  22.5 0.9 row_total.1
  23.5 4.7 %collective-permute-start.5 = (bf16[144,256]{1,0:T(8,128)(2,1)S(1)}, bf16[144,256]{1,0:T(8,128)(2,1)S(1)}, u32[]{:S(2)}, u32[]{:S(2)}) collective-permute-start(bf16[144,256]{1,0:T(8,128)(2,1)S(1)} %get-tuple-element.53.p0), channel_id=1, source_target_pairs={{0,64},{32,96},{64,0},{96,32},{1,65},{33,97},{65,1},{97,33},{2,66}... | collective-permute-start | bytes 221192 | tf_op jit(solution)/shard_map/ppermute | solution.py:504
  28.2 5.1 %collective-permute-done.4.p1 = bf16[144,256]{1,0:T(8,128)(2,1)S(1)} collective-permute-done((bf16[144,256]{1,0:T(8,128)(2,1)S(1)}, bf16[144,256]{1,0:T(8,128)(2,1)S(1)}, u32[]{:S(2)}, u32[]{:S(2)}) %collective-permute-start.4) | collective-permute-done | bytes 73760 | tf_op jit(solution)/shard_map/ppermute | solution.py:504
  34.0 3.3 %collective-permute-start.10 = (bf16[128,256]{1,0:T(8,128)(2,1)S(1)}, bf16[128,256]{1,0:T(8,128)(2,1)S(1)}, u32[]{:S(2)}, u32[]{:S(2)}) collective-permute-start(bf16[128,256]{1,0:T(8,128)(2,1)S(1)} %get-tuple-element.57), channel_id=1, source_target_pairs={{0,16},{8,24},{16,0},{24,8},{1,17},{9,25},{17,1},{25,9},{2,18},{10... | collective-permute-start | bytes 196616 | tf_op jit(solution)/shard_map/ppermute | solution.py:504
  37.3 1.1 collective-permute-start.11
  38.3 1.0 collective-permute-start.9
  39.4 3.3 %collective-permute-start.14 = (bf16[1024,256]{1,0:T(8,128)(2,1)S(1)}, bf16[1024,256]{1,0:T(8,128)(2,1)S(1)}, u32[]{:S(2)}, u32[]{:S(2)}) collective-permute-start(bf16[1024,256]{1,0:T(8,128)(2,1)S(1)} %slice.9), channel_id=1, source_target_pairs={{0,96},{32,0},{64,32},{96,64},{1,97},{33,1},{65,33},{97,65},{2,98}... | collective-permute-start | bytes 1572872 | tf_op jit(solution)/shard_map/ppermute | solution.py:504
  42.8 1.0 collective-permute-done.9.p1
  43.8 0.9 entering_state.1
  45.3 1.0 collective-permute-done.12.other_ref
  46.4 2.3 %gated_part.1 = (bf16[128,2048]{1,0:T(8,128)(2,1)S(1)}, bf16[128,2048]{1,0:T(8,128)(2,1)S(1)}, bf16[16,512]{1,0:T(8,128)(2,1)S(1)}) custom-call(s32[4]{0:T(128)S(1)} %pad_add_fusion.place, bf16[128,1024]{1,0:T(8,128)(2,1)S(1)} %get-tuple-element.59.mine_ref, bf16[128,1024]{1,0:T(8,128)(2,1)S(1)} %collective-permute-done.12.other_ref, ...), custom_call_target="tpu_custom_call" | custom-call | flops 134217728 | bytes 6291456 | tf_op jit(solution)/shard_map/gated_part/pallas_call | solution.py:347
  48.7 2.7 %collective-permute-done.13.refs_3_ = bf16[1024,256]{1,0:T(8,128)(2,1)S(1)} collective-permute-done((bf16[1024,256]{1,0:T(8,128)(2,1)S(1)}, bf16[1024,256]{1,0:T(8,128)(2,1)S(1)}, u32[]{:S(2)}, u32[]{:S(2)}) %collective-permute-start.13) | collective-permute-done | bytes 524320 | tf_op jit(solution)/shard_map/ppermute | solution.py:504
  53.4 2.3 %collective-permute-start.24 = (bf16[128,2048]{1,0:T(8,128)(2,1)S(1)}, bf16[128,2048]{1,0:T(8,128)(2,1)S(1)}, u32[]{:S(2)}, u32[]{:S(2)}) collective-permute-start(bf16[128,2048]{1,0:T(8,128)(2,1)S(1)} %get-tuple-element.62.top_ref), channel_id=1, source_target_pairs={{0,24},{8,0},{16,8},{24,16},{1,25},{9,1},{17,9},{25,17},{2,26},{10... | collective-permute-start | bytes 1572872 | tf_op jit(solution)/shard_map/ppermute | solution.py:504
  55.6 3.2 %collective-permute-start.29 = (bf16[128,2048]{1,0:T(8,128)(2,1)S(1)}, bf16[128,2048]{1,0:T(8,128)(2,1)S(1)}, u32[]{:S(2)}, u32[]{:S(2)}) collective-permute-start(bf16[128,2048]{1,0:T(8,128)(2,1)S(1)} %get-tuple-element.63.low_ref), channel_id=1, source_target_pairs={{0,24},{8,0},{16,8},{24,16},{1,25},{9,1},{17,9},{25,17},{2,26},{10... | collective-permute-start | bytes 1572872 | tf_op jit(solution)/shard_map/ppermute | solution.py:504
  58.9 6.2 %project.4 = (bf16[272,512]{1,0:T(8,128)(2,1)S(1)}, bf16[272,512]{1,0:T(8,128)(2,1)S(1)}, bf16[272,512]{1,0:T(8,128)(2,1)S(1)}, bf16[272,512]{1,0:T(8,128)(2,1)S(1)}) custom-call(s32[4]{0:T(128)S(1)} %pad_add_fusion.place, bf16[128,2048]{1,0:T(8,128)(2,1)S(1)} %get-tuple-element.62.top_ref, bf16[128,2048]{1,0:T(8,128)(2,1)S(1)} %get-tuple-element.63.low_ref, ...), custom_call_target="tpu_custom_call" | custom-call | flops 2147483648 | bytes 10485760 | tf_op jit(solution)/shard_map/project/pallas_call | solution.py:406
  65.0 1.6 %collective-permute-start.20 = (bf16[272,512]{1,0:T(8,128)(2,1)S(1)}, bf16[272,512]{1,0:T(8,128)(2,1)S(1)}, u32[]{:S(2)}, u32[]{:S(2)}) collective-permute-start(bf16[272,512]{1,0:T(8,128)(2,1)S(1)} %get-tuple-element.68), channel_id=1, source_target_pairs={{0,1},{1,2},{2,3},{3,0},{4,5},{5,6},{6,7},{7,4},{8,9},{9,10},{10,1... | collective-permute-start | bytes 835592 | tf_op jit(solution)/shard_map/ppermute | solution.py:504
  66.6 1.4 %collective-permute-done.23.top_ref = bf16[128,2048]{1,0:T(8,128)(2,1)S(1)} collective-permute-done((bf16[128,2048]{1,0:T(8,128)(2,1)S(1)}, bf16[128,2048]{1,0:T(8,128)(2,1)S(1)}, u32[]{:S(2)}, u32[]{:S(2)}) %collective-permute-start.23) | collective-permute-done | bytes 524320 | tf_op jit(solution)/shard_map/ppermute | solution.py:504
  68.0 2.1 %collective-permute-start.21 = (bf16[272,512]{1,0:T(8,128)(2,1)S(1)}, bf16[272,512]{1,0:T(8,128)(2,1)S(1)}, u32[]{:S(2)}, u32[]{:S(2)}) collective-permute-start(bf16[272,512]{1,0:T(8,128)(2,1)S(1)} %get-tuple-element.69), channel_id=1, source_target_pairs={{0,2},{1,3},{2,0},{3,1},{4,6},{5,7},{6,4},{7,5},{8,10},{9,11},{10,... | collective-permute-start | bytes 835592 | tf_op jit(solution)/shard_map/ppermute | solution.py:504
  70.1 1.4 %collective-permute-start.22 = (bf16[272,512]{1,0:T(8,128)(2,1)S(1)}, bf16[272,512]{1,0:T(8,128)(2,1)S(1)}, u32[]{:S(2)}, u32[]{:S(2)}) collective-permute-start(bf16[272,512]{1,0:T(8,128)(2,1)S(1)} %get-tuple-element.70), channel_id=1, source_target_pairs={{0,3},{1,0},{2,1},{3,2},{4,7},{5,4},{6,5},{7,6},{8,11},{9,8},{10,9... | collective-permute-start | bytes 835592 | tf_op jit(solution)/shard_map/ppermute | solution.py:504
  71.5 6.2 %project.5 = (bf16[256,512]{1,0:T(8,128)(2,1)S(1)}, bf16[256,512]{1,0:T(8,128)(2,1)S(1)}, bf16[256,512]{1,0:T(8,128)(2,1)S(1)}, bf16[256,512]{1,0:T(8,128)(2,1)S(1)}) custom-call(s32[4]{0:T(128)S(1)} %pad_add_fusion.place, bf16[128,2048]{1,0:T(8,128)(2,1)S(1)} %collective-permute-done.23.top_ref, bf16[128,2048]{1,0:T(8,128)(2,1)S(1)} %collective-permute-done.24.low_ref, ...), custom_call_target="tpu_custom_call" | custom-call | flops 2147483648 | bytes 10485760 | tf_op jit(solution)/shard_map/project/pallas_call | solution.py:406
  79.2 2.8 %collective-permute-start.35 = (bf16[128,2048]{1,0:T(8,128)(2,1)S(1)}, bf16[128,2048]{1,0:T(8,128)(2,1)S(1)}, u32[]{:S(2)}, u32[]{:S(2)}) collective-permute-start(bf16[128,2048]{1,0:T(8,128)(2,1)S(1)} %collective-permute-done.29.low_ref), channel_id=1, source_target_pairs={{0,24},{8,0},{16,8},{24,16},{1,25},{9,1},{17,9},{25,17},{2,26},{10... | collective-permute-start | bytes 1572872 | tf_op jit(solution)/shard_map/ppermute | solution.py:504
  82.0 1.5 %collective-permute-start.25 = (bf16[256,512]{1,0:T(8,128)(2,1)S(1)}, bf16[256,512]{1,0:T(8,128)(2,1)S(1)}, u32[]{:S(2)}, u32[]{:S(2)}) collective-permute-start(bf16[256,512]{1,0:T(8,128)(2,1)S(1)} %get-tuple-element.72), channel_id=1, source_target_pairs={{0,1},{1,2},{2,3},{3,0},{4,5},{5,6},{6,7},{7,4},{8,9},{9,10},{10,1... | collective-permute-start | bytes 786440 | tf_op jit(solution)/shard_map/ppermute | solution.py:504
  83.5 1.1 collective-permute-start.26
  84.7 2.2 %collective-permute-start.27 = (bf16[256,512]{1,0:T(8,128)(2,1)S(1)}, bf16[256,512]{1,0:T(8,128)(2,1)S(1)}, u32[]{:S(2)}, u32[]{:S(2)}) collective-permute-start(bf16[256,512]{1,0:T(8,128)(2,1)S(1)} %get-tuple-element.74), channel_id=1, source_target_pairs={{0,3},{1,0},{2,1},{3,2},{4,7},{5,4},{6,5},{7,6},{8,11},{9,8},{10,9... | collective-permute-start | bytes 786440 | tf_op jit(solution)/shard_map/ppermute | solution.py:504
  86.8 6.4 %project.6 = (bf16[256,512]{1,0:T(8,128)(2,1)S(1)}, bf16[256,512]{1,0:T(8,128)(2,1)S(1)}, bf16[256,512]{1,0:T(8,128)(2,1)S(1)}, bf16[256,512]{1,0:T(8,128)(2,1)S(1)}) custom-call(s32[4]{0:T(128)S(1)} %pad_add_fusion.place, bf16[128,2048]{1,0:T(8,128)(2,1)S(1)} %collective-permute-done.28.top_ref, bf16[128,2048]{1,0:T(8,128)(2,1)S(1)} %collective-permute-done.29.low_ref, ...), custom_call_target="tpu_custom_call" | custom-call | flops 2147483648 | bytes 10485760 | tf_op jit(solution)/shard_map/project/pallas_call | solution.py:406
  93.3 1.0 collective-permute-done.26.refs_2_.refs_11_
  94.3 2.5 %collective-permute-start.31 = (bf16[256,512]{1,0:T(8,128)(2,1)S(1)}, bf16[256,512]{1,0:T(8,128)(2,1)S(1)}, u32[]{:S(2)}, u32[]{:S(2)}) collective-permute-start(bf16[256,512]{1,0:T(8,128)(2,1)S(1)} %get-tuple-element.77), channel_id=1, source_target_pairs={{0,2},{1,3},{2,0},{3,1},{4,6},{5,7},{6,4},{7,5},{8,10},{9,11},{10,... | collective-permute-start | bytes 786440 | tf_op jit(solution)/shard_map/ppermute | solution.py:504
  96.8 1.4 %collective-permute-done.27.refs_3_.refs_12_ = bf16[256,512]{1,0:T(8,128)(2,1)S(1)} collective-permute-done((bf16[256,512]{1,0:T(8,128)(2,1)S(1)}, bf16[256,512]{1,0:T(8,128)(2,1)S(1)}, u32[]{:S(2)}, u32[]{:S(2)}) %collective-permute-start.27) | collective-permute-done | bytes 262176 | tf_op jit(solution)/shard_map/ppermute | solution.py:504
  98.2 1.5 %collective-permute-start.32 = (bf16[256,512]{1,0:T(8,128)(2,1)S(1)}, bf16[256,512]{1,0:T(8,128)(2,1)S(1)}, u32[]{:S(2)}, u32[]{:S(2)}) collective-permute-start(bf16[256,512]{1,0:T(8,128)(2,1)S(1)} %get-tuple-element.78), channel_id=1, source_target_pairs={{0,3},{1,0},{2,1},{3,2},{4,7},{5,4},{6,5},{7,6},{8,11},{9,8},{10,9... | collective-permute-start | bytes 786440 | tf_op jit(solution)/shard_map/ppermute | solution.py:504
  99.7 6.2 %project.7 = (bf16[256,512]{1,0:T(8,128)(2,1)S(1)}, bf16[256,512]{1,0:T(8,128)(2,1)S(1)}, bf16[256,512]{1,0:T(8,128)(2,1)S(1)}, bf16[256,512]{1,0:T(8,128)(2,1)S(1)}) custom-call(s32[4]{0:T(128)S(1)} %pad_add_fusion.place, bf16[128,2048]{1,0:T(8,128)(2,1)S(1)} %collective-permute-done.34.top_ref, bf16[128,2048]{1,0:T(8,128)(2,1)S(1)} %collective-permute-done.35.low_ref, ...), custom_call_target="tpu_custom_call" | custom-call | flops 2147483648 | bytes 10485760 | tf_op jit(solution)/shard_map/project/pallas_call | solution.py:406
  105.8 1.5 %collective-permute-start.36 = (bf16[256,512]{1,0:T(8,128)(2,1)S(1)}, bf16[256,512]{1,0:T(8,128)(2,1)S(1)}, u32[]{:S(2)}, u32[]{:S(2)}) collective-permute-start(bf16[256,512]{1,0:T(8,128)(2,1)S(1)} %get-tuple-element.83), channel_id=1, source_target_pairs={{0,1},{1,2},{2,3},{3,0},{4,5},{5,6},{6,7},{7,4},{8,9},{9,10},{10,1... | collective-permute-start | bytes 786440 | tf_op jit(solution)/shard_map/ppermute | solution.py:504
  107.4 1.5 %collective-permute-start.37 = (bf16[256,512]{1,0:T(8,128)(2,1)S(1)}, bf16[256,512]{1,0:T(8,128)(2,1)S(1)}, u32[]{:S(2)}, u32[]{:S(2)}) collective-permute-start(bf16[256,512]{1,0:T(8,128)(2,1)S(1)} %get-tuple-element.84), channel_id=1, source_target_pairs={{0,2},{1,3},{2,0},{3,1},{4,6},{5,7},{6,4},{7,5},{8,10},{9,11},{10,... | collective-permute-start | bytes 786440 | tf_op jit(solution)/shard_map/ppermute | solution.py:504
  108.9 2.5 %collective-permute-start.38 = (bf16[256,512]{1,0:T(8,128)(2,1)S(1)}, bf16[256,512]{1,0:T(8,128)(2,1)S(1)}, u32[]{:S(2)}, u32[]{:S(2)}) collective-permute-start(bf16[256,512]{1,0:T(8,128)(2,1)S(1)} %get-tuple-element.85), channel_id=1, source_target_pairs={{0,3},{1,0},{2,1},{3,2},{4,7},{5,4},{6,5},{7,6},{8,11},{9,8},{10,9... | collective-permute-start | bytes 786440 | tf_op jit(solution)/shard_map/ppermute | solution.py:504
  111.7 2.1 %collective-permute-start.33 = (bf16[256,512]{1,0:T(8,128)(2,1)S(1)}, bf16[256,512]{1,0:T(8,128)(2,1)S(1)}, u32[]{:S(2)}, u32[]{:S(2)}) collective-permute-start(bf16[256,512]{1,0:T(8,128)(2,1)S(1)} %get-tuple-element.79), channel_id=1, source_target_pairs={{0,24},{8,0},{16,8},{24,16},{1,25},{9,1},{17,9},{25,17},{2,26},{10... | collective-permute-start | bytes 786440 | tf_op jit(solution)/shard_map/ppermute | solution.py:504
  113.8 0.9 collective-permute-done.36.refs_1_
  114.7 2.8 %collective-permute-done.37.refs_2_ = bf16[256,512]{1,0:T(8,128)(2,1)S(1)} collective-permute-done((bf16[256,512]{1,0:T(8,128)(2,1)S(1)}, bf16[256,512]{1,0:T(8,128)(2,1)S(1)}, u32[]{:S(2)}, u32[]{:S(2)}) %collective-permute-start.37) | collective-permute-done | bytes 262176 | tf_op jit(solution)/shard_map/ppermute | solution.py:504
  117.5 2.7 %collective-permute-done.38.refs_3_ = bf16[256,512]{1,0:T(8,128)(2,1)S(1)} collective-permute-done((bf16[256,512]{1,0:T(8,128)(2,1)S(1)}, bf16[256,512]{1,0:T(8,128)(2,1)S(1)}, u32[]{:S(2)}, u32[]{:S(2)}) %collective-permute-start.38) | collective-permute-done | bytes 262176 | tf_op jit(solution)/shard_map/ppermute | solution.py:504
  120.3 1.5 %collective-permute-start.39 = (bf16[256,512]{1,0:T(8,128)(2,1)S(1)}, bf16[256,512]{1,0:T(8,128)(2,1)S(1)}, u32[]{:S(2)}, u32[]{:S(2)}) collective-permute-start(bf16[256,512]{1,0:T(8,128)(2,1)S(1)} %far_sums.1), channel_id=1, source_target_pairs={{0,16},{8,24},{16,0},{24,8},{1,17},{9,25},{17,1},{25,9},{2,18},{10... | collective-permute-start | bytes 786440 | tf_op jit(solution)/shard_map/ppermute | solution.py:504
  121.9 7.6 %collective-permute-done.39.far_ref = bf16[256,512]{1,0:T(8,128)(2,1)S(1)} collective-permute-done((bf16[256,512]{1,0:T(8,128)(2,1)S(1)}, bf16[256,512]{1,0:T(8,128)(2,1)S(1)}, u32[]{:S(2)}, u32[]{:S(2)}) %collective-permute-start.39) | collective-permute-done | bytes 262176 | tf_op jit(solution)/shard_map/ppermute | solution.py:504
  129.4 2.9 %finish.1 = bf16[256,2048]{1,0:T(8,128)(2,1)} custom-call(s32[4]{0:T(128)S(1)} %pad_add_fusion.place, bf16[272,512]{1,0:T(8,128)(2,1)S(1)} %get-tuple-element.67.refs_10_.p0, bf16[272,512]{1,0:T(8,128)(2,1)S(1)} %collective-permute-done.20.refs_10_.p1, bf16[272,512]{1,0:T(8,128)(2,1)S(1)} %collective-permute-done.21.refs_11_.p2, ...), custom_call_target="tpu_custom_call" | custom-call | flops 2097152 | bytes 4194304 | tf_op jit(solution)/shard_map/finish/pallas_call | solution.py:488
  (78 shorter events, 9.7 us)
Async XLA Ops:
  0.0 19.6 %copy-start.8 = (f32[256,16]{0,1:T(8,128)S(1)}, f32[256,16]{0,1:T(8,128)}, u32[]{:S(2)}) copy-start(f32[256,16]{0,1:T(8,128)} %param.15) | copy-start | bytes 49156
  0.0 19.6 %copy-start.12 = (f32[16]{0:T(128)S(1)}, f32[16]{0:T(128)}, u32[]{:S(2)}) copy-start(f32[16]{0:T(128)} %param.17) | copy-start | bytes 196
  0.0 33.2 %collective-permute-start.7 = (bf16[2048,256]{1,0:T(8,128)(2,1)}, bf16[2048,256]{1,0:T(8,128)(2,1)S(1)}, u32[]{:S(2)}, u32[]{:S(2)}) collective-permute-start(bf16[2048,256]{1,0:T(8,128)(2,1)} %refs_0_.7), channel_id=1, source_target_pairs={{0,96},{32,0},{64,32},{96,64},{1,97},{33,1},{65,33},{97,65},{2,98}... | collective-permute-start | bytes 3145736 | tf_op jit(solution)/shard_map/ppermute | solution.py:504
  4.0 29.2 %collective-permute-start.8 = (bf16[2048,256]{1,0:T(8,128)(2,1)}, bf16[2048,256]{1,0:T(8,128)(2,1)S(1)}, u32[]{:S(2)}, u32[]{:S(2)}) collective-permute-start(bf16[2048,256]{1,0:T(8,128)(2,1)} %refs_0_.7), channel_id=1, source_target_pairs={{0,32},{32,64},{64,96},{96,0},{1,33},{33,65},{65,97},{97,1},{2,34}... | collective-permute-start | bytes 3145736 | tf_op jit(solution)/shard_map/ppermute | solution.py:504
  7.6 12.0 %copy-start.4 = (bf16[256,128]{1,0:T(8,128)(2,1)S(1)}, bf16[256,128]{1,0:T(8,128)(2,1)}, u32[]{:S(2)}) copy-start(bf16[256,128]{1,0:T(8,128)(2,1)} %read_ref.3) | copy-start | bytes 196612
  7.6 12.0 %copy-start.6 = (bf16[256,128]{1,0:T(8,128)(2,1)S(1)}, bf16[256,128]{1,0:T(8,128)(2,1)}, u32[]{:S(2)}) copy-start(bf16[256,128]{1,0:T(8,128)(2,1)} %write_ref.3) | copy-start | bytes 196612
  7.6 12.0 %copy-start.11 = (bf16[256,2048]{1,0:T(8,128)(2,1)S(1)}, bf16[256,2048]{1,0:T(8,128)(2,1)}, u32[]{:S(2)}) copy-start(bf16[256,2048]{1,0:T(8,128)(2,1)} %gate_ref.1) | copy-start | bytes 3145732
  10.0 2.0 %collective-permute-start = (f32[136,1024]{1,0:T(8,128)S(1)}, f32[136,1024]{1,0:T(8,128)S(1)}, u32[]{:S(2)}, u32[]{:S(2)}) collective-permute-start(f32[136,1024]{1,0:T(8,128)S(1)} %get-tuple-element.47), channel_id=1, source_target_pairs={{0,4},{4,0},{1,5},{5,1},{2,6},{6,2},{3,7},{7,3},{8,12},{12,8},{9,1... | collective-permute-start | bytes 1671176 | tf_op jit(solution)/shard_map/ppermute | solution.py:508
  12.9 9.6 %collective-permute-start.1 = (bf16[144,256]{1,0:T(8,128)(2,1)S(1)}, bf16[144,256]{1,0:T(8,128)(2,1)S(1)}, u32[]{:S(2)}, u32[]{:S(2)}) collective-permute-start(bf16[144,256]{1,0:T(8,128)(2,1)S(1)} %get-tuple-element.49), channel_id=1, source_target_pairs={{0,8},{8,16},{16,24},{24,0},{1,9},{9,17},{17,25},{25,1},{2,10},{10... | collective-permute-start | bytes 221192 | tf_op jit(solution)/shard_map/ppermute | solution.py:504
  14.5 8.0 %collective-permute-start.2 = (bf16[144,256]{1,0:T(8,128)(2,1)S(1)}, bf16[144,256]{1,0:T(8,128)(2,1)S(1)}, u32[]{:S(2)}, u32[]{:S(2)}) collective-permute-start(bf16[144,256]{1,0:T(8,128)(2,1)S(1)} %get-tuple-element.50), channel_id=1, source_target_pairs={{0,16},{8,24},{16,0},{24,8},{1,17},{9,25},{17,1},{25,9},{2,18},{10... | collective-permute-start | bytes 221192 | tf_op jit(solution)/shard_map/ppermute | solution.py:504
  17.4 5.1 %collective-permute-start.3 = (bf16[144,256]{1,0:T(8,128)(2,1)S(1)}, bf16[144,256]{1,0:T(8,128)(2,1)S(1)}, u32[]{:S(2)}, u32[]{:S(2)}) collective-permute-start(bf16[144,256]{1,0:T(8,128)(2,1)S(1)} %get-tuple-element.51), channel_id=1, source_target_pairs={{0,24},{8,0},{16,8},{24,16},{1,25},{9,1},{17,9},{25,17},{2,26},{10... | collective-permute-start | bytes 221192 | tf_op jit(solution)/shard_map/ppermute | solution.py:504
  23.4 9.9 %collective-permute-start.4 = (bf16[144,256]{1,0:T(8,128)(2,1)S(1)}, bf16[144,256]{1,0:T(8,128)(2,1)S(1)}, u32[]{:S(2)}, u32[]{:S(2)}) collective-permute-start(bf16[144,256]{1,0:T(8,128)(2,1)S(1)} %get-tuple-element.53.p0), channel_id=1, source_target_pairs={{0,32},{32,64},{64,96},{96,0},{1,33},{33,65},{65,97},{97,1},{2,34}... | collective-permute-start | bytes 221192 | tf_op jit(solution)/shard_map/ppermute | solution.py:504
  23.5 9.8 %collective-permute-start.5 = (bf16[144,256]{1,0:T(8,128)(2,1)S(1)}, bf16[144,256]{1,0:T(8,128)(2,1)S(1)}, u32[]{:S(2)}, u32[]{:S(2)}) collective-permute-start(bf16[144,256]{1,0:T(8,128)(2,1)S(1)} %get-tuple-element.53.p0), channel_id=1, source_target_pairs={{0,64},{32,96},{64,0},{96,32},{1,65},{33,97},{65,1},{97,33},{2,66}... | collective-permute-start | bytes 221192 | tf_op jit(solution)/shard_map/ppermute | solution.py:504
  28.2 5.1 %collective-permute-start.6 = (bf16[144,256]{1,0:T(8,128)(2,1)S(1)}, bf16[144,256]{1,0:T(8,128)(2,1)S(1)}, u32[]{:S(2)}, u32[]{:S(2)}) collective-permute-start(bf16[144,256]{1,0:T(8,128)(2,1)S(1)} %get-tuple-element.53.p0), channel_id=1, source_target_pairs={{0,96},{32,0},{64,32},{96,64},{1,97},{33,1},{65,33},{97,65},{2,98}... | collective-permute-start | bytes 221192 | tf_op jit(solution)/shard_map/ppermute | solution.py:504
  34.0 12.5 %copy-start.9 = (f32[2048]{0:T(1024)S(1)}, f32[2048]{0:T(1024)}, u32[]{:S(2)}) copy-start(f32[2048]{0:T(1024)} %param.19) | copy-start | bytes 24580
  34.0 8.8 %collective-permute-start.10 = (bf16[128,256]{1,0:T(8,128)(2,1)S(1)}, bf16[128,256]{1,0:T(8,128)(2,1)S(1)}, u32[]{:S(2)}, u32[]{:S(2)}) collective-permute-start(bf16[128,256]{1,0:T(8,128)(2,1)S(1)} %get-tuple-element.57), channel_id=1, source_target_pairs={{0,16},{8,24},{16,0},{24,8},{1,17},{9,25},{17,1},{25,9},{2,18},{10... | collective-permute-start | bytes 196616 | tf_op jit(solution)/shard_map/ppermute | solution.py:504
  37.3 5.5 %collective-permute-start.11 = (bf16[128,256]{1,0:T(8,128)(2,1)S(1)}, bf16[128,256]{1,0:T(8,128)(2,1)S(1)}, u32[]{:S(2)}, u32[]{:S(2)}) collective-permute-start(bf16[128,256]{1,0:T(8,128)(2,1)S(1)} %get-tuple-element.58), channel_id=1, source_target_pairs={{0,24},{8,0},{16,8},{24,16},{1,25},{9,1},{17,9},{25,17},{2,26},{10... | collective-permute-start | bytes 196616 | tf_op jit(solution)/shard_map/ppermute | solution.py:504
  38.3 5.5 %collective-permute-start.9 = (bf16[128,256]{1,0:T(8,128)(2,1)S(1)}, bf16[128,256]{1,0:T(8,128)(2,1)S(1)}, u32[]{:S(2)}, u32[]{:S(2)}) collective-permute-start(bf16[128,256]{1,0:T(8,128)(2,1)S(1)} %get-tuple-element.56), channel_id=1, source_target_pairs={{0,8},{8,16},{16,24},{24,0},{1,9},{9,17},{17,25},{25,1},{2,10},{10... | collective-permute-start | bytes 196616 | tf_op jit(solution)/shard_map/ppermute | solution.py:504
  39.3 12.1 %collective-permute-start.13 = (bf16[1024,256]{1,0:T(8,128)(2,1)S(1)}, bf16[1024,256]{1,0:T(8,128)(2,1)S(1)}, u32[]{:S(2)}, u32[]{:S(2)}) collective-permute-start(bf16[1024,256]{1,0:T(8,128)(2,1)S(1)} %slice.8), channel_id=1, source_target_pairs={{0,32},{32,64},{64,96},{96,0},{1,33},{33,65},{65,97},{97,1},{2,34}... | collective-permute-start | bytes 1572872 | tf_op jit(solution)/shard_map/ppermute | solution.py:504
  39.4 12.0 %collective-permute-start.14 = (bf16[1024,256]{1,0:T(8,128)(2,1)S(1)}, bf16[1024,256]{1,0:T(8,128)(2,1)S(1)}, u32[]{:S(2)}, u32[]{:S(2)}) collective-permute-start(bf16[1024,256]{1,0:T(8,128)(2,1)S(1)} %slice.9), channel_id=1, source_target_pairs={{0,96},{32,0},{64,32},{96,64},{1,97},{33,1},{65,33},{97,65},{2,98}... | collective-permute-start | bytes 1572872 | tf_op jit(solution)/shard_map/ppermute | solution.py:504
  42.7 9.2 %collective-permute-start.15 = (bf16[2048,256]{1,0:T(8,128)(2,1)S(1)}, bf16[2048,256]{1,0:T(8,128)(2,1)S(1)}, u32[]{:S(2)}, u32[]{:S(2)}) collective-permute-start(bf16[2048,256]{1,0:T(8,128)(2,1)S(1)} %copy-done), channel_id=1, source_target_pairs={{0,4},{4,0},{1,5},{5,1},{2,6},{6,2},{3,7},{7,3},{8,12},{12,8},{9,1... | collective-permute-start | bytes 3145736 | tf_op jit(solution)/shard_map/ppermute | solution.py:508
  44.7 1.6 %collective-permute-start.12 = (bf16[128,1024]{1,0:T(8,128)(2,1)S(1)}, bf16[128,1024]{1,0:T(8,128)(2,1)S(1)}, u32[]{:S(2)}, u32[]{:S(2)}) collective-permute-start(bf16[128,1024]{1,0:T(8,128)(2,1)S(1)} %get-tuple-element.60), channel_id=1, source_target_pairs={{0,4},{4,0},{1,5},{5,1},{2,6},{6,2},{3,7},{7,3},{8,12},{12,8},{9,1... | collective-permute-start | bytes 786440 | tf_op jit(solution)/shard_map/ppermute | solution.py:508
  44.8 10.9 %collective-permute-start.16 = (bf16[2048,256]{1,0:T(8,128)(2,1)S(1)}, bf16[2048,256]{1,0:T(8,128)(2,1)S(1)}, u32[]{:S(2)}, u32[]{:S(2)}) collective-permute-start(bf16[2048,256]{1,0:T(8,128)(2,1)S(1)} %collective-permute-done.7.refs_0_.refs_1_), channel_id=1, source_target_pairs={{0,4},{4,0},{1,5},{5,1},{2,6},{6,2},{3,7},{7,3},{8,12},{12,8},{9,1... | collective-permute-start | bytes 3145736 | tf_op jit(solution)/shard_map/ppermute | solution.py:508
  46.3 12.6 %collective-permute-start.17 = (bf16[2048,256]{1,0:T(8,128)(2,1)S(1)}, bf16[2048,256]{1,0:T(8,128)(2,1)S(1)}, u32[]{:S(2)}, u32[]{:S(2)}) collective-permute-start(bf16[2048,256]{1,0:T(8,128)(2,1)S(1)} %collective-permute-done.8.refs_1_.refs_2_), channel_id=1, source_target_pairs={{0,4},{4,0},{1,5},{5,1},{2,6},{6,2},{3,7},{7,3},{8,12},{12,8},{9,1... | collective-permute-start | bytes 3145736 | tf_op jit(solution)/shard_map/ppermute | solution.py:508
  51.4 1.9 %collective-permute-start.18 = (bf16[1024,256]{1,0:T(8,128)(2,1)S(1)}, bf16[1024,256]{1,0:T(8,128)(2,1)S(1)}, u32[]{:S(2)}, u32[]{:S(2)}) collective-permute-start(bf16[1024,256]{1,0:T(8,128)(2,1)S(1)} %collective-permute-done.13.refs_3_), channel_id=1, source_target_pairs={{0,4},{4,0},{1,5},{5,1},{2,6},{6,2},{3,7},{7,3},{8,12},{12,8},{9,1... | collective-permute-start | bytes 1572872 | tf_op jit(solution)/shard_map/ppermute | solution.py:508
  51.5 4.2 %collective-permute-start.19 = (bf16[1024,256]{1,0:T(8,128)(2,1)S(1)}, bf16[1024,256]{1,0:T(8,128)(2,1)S(1)}, u32[]{:S(2)}, u32[]{:S(2)}) collective-permute-start(bf16[1024,256]{1,0:T(8,128)(2,1)S(1)} %collective-permute-done.14.refs_4_), channel_id=1, source_target_pairs={{0,4},{4,0},{1,5},{5,1},{2,6},{6,2},{3,7},{7,3},{8,12},{12,8},{9,1... | collective-permute-start | bytes 1572872 | tf_op jit(solution)/shard_map/ppermute | solution.py:508
  52.0 16.0 %collective-permute-start.23 = (bf16[128,2048]{1,0:T(8,128)(2,1)S(1)}, bf16[128,2048]{1,0:T(8,128)(2,1)S(1)}, u32[]{:S(2)}, u32[]{:S(2)}) collective-permute-start(bf16[128,2048]{1,0:T(8,128)(2,1)S(1)} %get-tuple-element.62.top_ref), channel_id=1, source_target_pairs={{0,8},{8,16},{16,24},{24,0},{1,9},{9,17},{17,25},{25,1},{2,10},{10... | collective-permute-start | bytes 1572872 | tf_op jit(solution)/shard_map/ppermute | solution.py:504
  53.4 16.7 %collective-permute-start.24 = (bf16[128,2048]{1,0:T(8,128)(2,1)S(1)}, bf16[128,2048]{1,0:T(8,128)(2,1)S(1)}, u32[]{:S(2)}, u32[]{:S(2)}) collective-permute-start(bf16[128,2048]{1,0:T(8,128)(2,1)S(1)} %get-tuple-element.62.top_ref), channel_id=1, source_target_pairs={{0,24},{8,0},{16,8},{24,16},{1,25},{9,1},{17,9},{25,17},{2,26},{10... | collective-permute-start | bytes 1572872 | tf_op jit(solution)/shard_map/ppermute | solution.py:504
  55.6 22.6 %collective-permute-start.28 = (bf16[128,2048]{1,0:T(8,128)(2,1)S(1)}, bf16[128,2048]{1,0:T(8,128)(2,1)S(1)}, u32[]{:S(2)}, u32[]{:S(2)}) collective-permute-start(bf16[128,2048]{1,0:T(8,128)(2,1)S(1)} %get-tuple-element.63.low_ref), channel_id=1, source_target_pairs={{0,8},{8,16},{16,24},{24,0},{1,9},{9,17},{17,25},{25,1},{2,10},{10... | collective-permute-start | bytes 1572872 | tf_op jit(solution)/shard_map/ppermute | solution.py:504
  55.6 22.9 %collective-permute-start.29 = (bf16[128,2048]{1,0:T(8,128)(2,1)S(1)}, bf16[128,2048]{1,0:T(8,128)(2,1)S(1)}, u32[]{:S(2)}, u32[]{:S(2)}) collective-permute-start(bf16[128,2048]{1,0:T(8,128)(2,1)S(1)} %get-tuple-element.63.low_ref), channel_id=1, source_target_pairs={{0,24},{8,0},{16,8},{24,16},{1,25},{9,1},{17,9},{25,17},{2,26},{10... | collective-permute-start | bytes 1572872 | tf_op jit(solution)/shard_map/ppermute | solution.py:504
  65.0 17.0 %collective-permute-start.20 = (bf16[272,512]{1,0:T(8,128)(2,1)S(1)}, bf16[272,512]{1,0:T(8,128)(2,1)S(1)}, u32[]{:S(2)}, u32[]{:S(2)}) collective-permute-start(bf16[272,512]{1,0:T(8,128)(2,1)S(1)} %get-tuple-element.68), channel_id=1, source_target_pairs={{0,1},{1,2},{2,3},{3,0},{4,5},{5,6},{6,7},{7,4},{8,9},{9,10},{10,1... | collective-permute-start | bytes 835592 | tf_op jit(solution)/shard_map/ppermute | solution.py:504
  68.0 15.6 %collective-permute-start.21 = (bf16[272,512]{1,0:T(8,128)(2,1)S(1)}, bf16[272,512]{1,0:T(8,128)(2,1)S(1)}, u32[]{:S(2)}, u32[]{:S(2)}) collective-permute-start(bf16[272,512]{1,0:T(8,128)(2,1)S(1)} %get-tuple-element.69), channel_id=1, source_target_pairs={{0,2},{1,3},{2,0},{3,1},{4,6},{5,7},{6,4},{7,5},{8,10},{9,11},{10,... | collective-permute-start | bytes 835592 | tf_op jit(solution)/shard_map/ppermute | solution.py:504
  70.1 14.6 %collective-permute-start.22 = (bf16[272,512]{1,0:T(8,128)(2,1)S(1)}, bf16[272,512]{1,0:T(8,128)(2,1)S(1)}, u32[]{:S(2)}, u32[]{:S(2)}) collective-permute-start(bf16[272,512]{1,0:T(8,128)(2,1)S(1)} %get-tuple-element.70), channel_id=1, source_target_pairs={{0,3},{1,0},{2,1},{3,2},{4,7},{5,4},{6,5},{7,6},{8,11},{9,8},{10,9... | collective-permute-start | bytes 835592 | tf_op jit(solution)/shard_map/ppermute | solution.py:504
  78.6 21.1 %collective-permute-start.34 = (bf16[128,2048]{1,0:T(8,128)(2,1)S(1)}, bf16[128,2048]{1,0:T(8,128)(2,1)S(1)}, u32[]{:S(2)}, u32[]{:S(2)}) collective-permute-start(bf16[128,2048]{1,0:T(8,128)(2,1)S(1)} %collective-permute-done.23.top_ref), channel_id=1, source_target_pairs={{0,8},{8,16},{16,24},{24,0},{1,9},{9,17},{17,25},{25,1},{2,10},{10... | collective-permute-start | bytes 1572872 | tf_op jit(solution)/shard_map/ppermute | solution.py:504
  79.2 20.4 %collective-permute-start.35 = (bf16[128,2048]{1,0:T(8,128)(2,1)S(1)}, bf16[128,2048]{1,0:T(8,128)(2,1)S(1)}, u32[]{:S(2)}, u32[]{:S(2)}) collective-permute-start(bf16[128,2048]{1,0:T(8,128)(2,1)S(1)} %collective-permute-done.29.low_ref), channel_id=1, source_target_pairs={{0,24},{8,0},{16,8},{24,16},{1,25},{9,1},{17,9},{25,17},{2,26},{10... | collective-permute-start | bytes 1572872 | tf_op jit(solution)/shard_map/ppermute | solution.py:504
  82.0 11.2 %collective-permute-start.25 = (bf16[256,512]{1,0:T(8,128)(2,1)S(1)}, bf16[256,512]{1,0:T(8,128)(2,1)S(1)}, u32[]{:S(2)}, u32[]{:S(2)}) collective-permute-start(bf16[256,512]{1,0:T(8,128)(2,1)S(1)} %get-tuple-element.72), channel_id=1, source_target_pairs={{0,1},{1,2},{2,3},{3,0},{4,5},{5,6},{6,7},{7,4},{8,9},{9,10},{10,1... | collective-permute-start | bytes 786440 | tf_op jit(solution)/shard_map/ppermute | solution.py:504
  83.5 10.7 %collective-permute-start.26 = (bf16[256,512]{1,0:T(8,128)(2,1)S(1)}, bf16[256,512]{1,0:T(8,128)(2,1)S(1)}, u32[]{:S(2)}, u32[]{:S(2)}) collective-permute-start(bf16[256,512]{1,0:T(8,128)(2,1)S(1)} %get-tuple-element.73), channel_id=1, source_target_pairs={{0,2},{1,3},{2,0},{3,1},{4,6},{5,7},{6,4},{7,5},{8,10},{9,11},{10,... | collective-permute-start | bytes 786440 | tf_op jit(solution)/shard_map/ppermute | solution.py:504
  84.7 13.5 %collective-permute-start.27 = (bf16[256,512]{1,0:T(8,128)(2,1)S(1)}, bf16[256,512]{1,0:T(8,128)(2,1)S(1)}, u32[]{:S(2)}, u32[]{:S(2)}) collective-permute-start(bf16[256,512]{1,0:T(8,128)(2,1)S(1)} %get-tuple-element.74), channel_id=1, source_target_pairs={{0,3},{1,0},{2,1},{3,2},{4,7},{5,4},{6,5},{7,6},{8,11},{9,8},{10,9... | collective-permute-start | bytes 786440 | tf_op jit(solution)/shard_map/ppermute | solution.py:504
  93.2 15.7 %collective-permute-start.30 = (bf16[256,512]{1,0:T(8,128)(2,1)S(1)}, bf16[256,512]{1,0:T(8,128)(2,1)S(1)}, u32[]{:S(2)}, u32[]{:S(2)}) collective-permute-start(bf16[256,512]{1,0:T(8,128)(2,1)S(1)} %get-tuple-element.76), channel_id=1, source_target_pairs={{0,1},{1,2},{2,3},{3,0},{4,5},{5,6},{6,7},{7,4},{8,9},{9,10},{10,1... | collective-permute-start | bytes 786440 | tf_op jit(solution)/shard_map/ppermute | solution.py:504
  94.3 17.2 %collective-permute-start.31 = (bf16[256,512]{1,0:T(8,128)(2,1)S(1)}, bf16[256,512]{1,0:T(8,128)(2,1)S(1)}, u32[]{:S(2)}, u32[]{:S(2)}) collective-permute-start(bf16[256,512]{1,0:T(8,128)(2,1)S(1)} %get-tuple-element.77), channel_id=1, source_target_pairs={{0,2},{1,3},{2,0},{3,1},{4,6},{5,7},{6,4},{7,5},{8,10},{9,11},{10,... | collective-permute-start | bytes 786440 | tf_op jit(solution)/shard_map/ppermute | solution.py:504
  98.2 13.3 %collective-permute-start.32 = (bf16[256,512]{1,0:T(8,128)(2,1)S(1)}, bf16[256,512]{1,0:T(8,128)(2,1)S(1)}, u32[]{:S(2)}, u32[]{:S(2)}) collective-permute-start(bf16[256,512]{1,0:T(8,128)(2,1)S(1)} %get-tuple-element.78), channel_id=1, source_target_pairs={{0,3},{1,0},{2,1},{3,2},{4,7},{5,4},{6,5},{7,6},{8,11},{9,8},{10,9... | collective-permute-start | bytes 786440 | tf_op jit(solution)/shard_map/ppermute | solution.py:504
  105.8 23.6 %copy-start.3 = (bf16[256,2048]{1,0:T(8,128)(2,1)S(1)}, bf16[256,2048]{1,0:T(8,128)(2,1)}, u32[]{:S(2)}) copy-start(bf16[256,2048]{1,0:T(8,128)(2,1)} %residual_ref.1) | copy-start | bytes 3145732
  105.8 8.9 %collective-permute-start.36 = (bf16[256,512]{1,0:T(8,128)(2,1)S(1)}, bf16[256,512]{1,0:T(8,128)(2,1)S(1)}, u32[]{:S(2)}, u32[]{:S(2)}) collective-permute-start(bf16[256,512]{1,0:T(8,128)(2,1)S(1)} %get-tuple-element.83), channel_id=1, source_target_pairs={{0,1},{1,2},{2,3},{3,0},{4,5},{5,6},{6,7},{7,4},{8,9},{9,10},{10,1... | collective-permute-start | bytes 786440 | tf_op jit(solution)/shard_map/ppermute | solution.py:504
  107.4 10.1 %collective-permute-start.37 = (bf16[256,512]{1,0:T(8,128)(2,1)S(1)}, bf16[256,512]{1,0:T(8,128)(2,1)S(1)}, u32[]{:S(2)}, u32[]{:S(2)}) collective-permute-start(bf16[256,512]{1,0:T(8,128)(2,1)S(1)} %get-tuple-element.84), channel_id=1, source_target_pairs={{0,2},{1,3},{2,0},{3,1},{4,6},{5,7},{6,4},{7,5},{8,10},{9,11},{10,... | collective-permute-start | bytes 786440 | tf_op jit(solution)/shard_map/ppermute | solution.py:504
  108.9 11.3 %collective-permute-start.38 = (bf16[256,512]{1,0:T(8,128)(2,1)S(1)}, bf16[256,512]{1,0:T(8,128)(2,1)S(1)}, u32[]{:S(2)}, u32[]{:S(2)}) collective-permute-start(bf16[256,512]{1,0:T(8,128)(2,1)S(1)} %get-tuple-element.85), channel_id=1, source_target_pairs={{0,3},{1,0},{2,1},{3,2},{4,7},{5,4},{6,5},{7,6},{8,11},{9,8},{10,9... | collective-permute-start | bytes 786440 | tf_op jit(solution)/shard_map/ppermute | solution.py:504
  111.7 10.1 %collective-permute-start.33 = (bf16[256,512]{1,0:T(8,128)(2,1)S(1)}, bf16[256,512]{1,0:T(8,128)(2,1)S(1)}, u32[]{:S(2)}, u32[]{:S(2)}) collective-permute-start(bf16[256,512]{1,0:T(8,128)(2,1)S(1)} %get-tuple-element.79), channel_id=1, source_target_pairs={{0,24},{8,0},{16,8},{24,16},{1,25},{9,1},{17,9},{25,17},{2,26},{10... | collective-permute-start | bytes 786440 | tf_op jit(solution)/shard_map/ppermute | solution.py:504
  113.8 8.0 %collective-permute-start.40 = (bf16[256,512]{1,0:T(8,128)(2,1)S(1)}, bf16[256,512]{1,0:T(8,128)(2,1)S(1)}, u32[]{:S(2)}, u32[]{:S(2)}) collective-permute-start(bf16[256,512]{1,0:T(8,128)(2,1)S(1)} %get-tuple-element.86), channel_id=1, source_target_pairs={{0,8},{8,16},{16,24},{24,0},{1,9},{9,17},{17,25},{25,1},{2,10},{10... | collective-permute-start | bytes 786440 | tf_op jit(solution)/shard_map/ppermute | solution.py:504
  120.3 9.1 %collective-permute-start.39 = (bf16[256,512]{1,0:T(8,128)(2,1)S(1)}, bf16[256,512]{1,0:T(8,128)(2,1)S(1)}, u32[]{:S(2)}, u32[]{:S(2)}) collective-permute-start(bf16[256,512]{1,0:T(8,128)(2,1)S(1)} %far_sums.1), channel_id=1, source_target_pairs={{0,16},{8,24},{16,0},{24,8},{1,17},{9,25},{17,1},{25,9},{2,18},{10... | collective-permute-start | bytes 786440 | tf_op jit(solution)/shard_map/ppermute | solution.py:504
  (6 other events, 24.1 us)

commit v3 on v2

--- a/solution.py
+++ b/solution.py
@@ -17,9 +17,11 @@
 SPLIT = LANES // 2
 PIECE = 512
 INNER = 8192
+SHARE = 1
 F32 = jnp.float32
 BF16 = jnp.bfloat16
 HIGHEST = lax.Precision.HIGHEST
+HBM = pl.BlockSpec(memory_space=pltpu.HBM)
 VMEM = pl.BlockSpec(memory_space=pltpu.VMEM)
 SMEM = pl.BlockSpec(memory_space=pltpu.SMEM)
 
@@ -33,7 +35,7 @@
 
 def cost(flops, bytes_accessed, transcendentals=0):
     return pl.CostEstimate(
-        flops=flops, bytes_accessed=bytes_accessed, transcendentals=transcendentals
+        flops=flops // SHARE, bytes_accessed=bytes_accessed // SHARE, transcendentals=0
     )
 
 
@@ -77,7 +79,26 @@
     return block[0:1] + block[1:2] + block[2:3]
 
 
-def state_kernel(place, value_ref, write_ref, step_ref, rate_ref, keep_ref, send_ref, state, logs):
+def fetch(sources, targets, sems):
+    copies = [
+        pltpu.make_async_copy(source, target, sems.at[i])
+        for i, (source, target) in enumerate(zip(sources, targets))
+    ]
+    for copy in copies:
+        copy.start()
+    for copy in copies:
+        copy.wait()
+    return targets
+
+
+def room(sources):
+    targets = [pltpu.VMEM(source.shape, source.dtype) for source in sources]
+    return targets + [pltpu.SemaphoreType.DMA((len(sources),))]
+
+
+def state_kernel(place, *refs):
+    keep_ref, send_ref, state, logs = refs[4:8]
+    value_ref, write_ref, step_ref, rate_ref = fetch(refs[0:4], refs[8:12], refs[12])
     core = place[0]
     step = step_ref[...]
     across = cumulate(step, rate_ref[...])
@@ -103,25 +124,24 @@
 
 def local_state(place, values, writes, steps, rate):
     shape = (WIDTH + 8, SPLIT)
+    sources = (values, writes, steps, rate)
     return pl.pallas_call(
         state_kernel,
-        grid_spec=pltpu.PrefetchScalarGridSpec(
-            num_scalar_prefetch=1,
-            grid=(1,),
-            in_specs=[whole(part.shape) for part in (values, writes, steps, rate)],
-            out_specs=[whole(shape), whole(shape)],
-            scratch_shapes=[pltpu.VMEM((WIDTH, LANES), F32), pltpu.VMEM((8, LANES), F32)],
-        ),
         out_shape=[jax.ShapeDtypeStruct(shape, F32)] * 2,
-        compiler_params=params(48),
+        in_specs=[SMEM] + [HBM] * 4,
+        out_specs=[VMEM] * 2,
+        scratch_shapes=[pltpu.VMEM((WIDTH, LANES), F32), pltpu.VMEM((8, LANES), F32)]
+        + room(sources),
+        compiler_params=params(),
         cost_estimate=cost(2 * WIDTH * ROWS * LANES, 3 * 2**20),
         name="local_state",
-    )(place, values, writes, steps, rate)
-
-
-def plain_kernel(
-    value_ref, gate_ref, write_ref, read_ref, step_ref, rate_ref, skip_ref, _, plain_ref, scale_ref
-):
+    )(place, *sources)
+
+
+def plain_kernel(*refs):
+    plain_ref, scale_ref = refs[8:10]
+    targets = fetch(refs[0:7], refs[10:17], refs[17])
+    value_ref, gate_ref, write_ref, read_ref, step_ref, rate_ref, skip_ref = targets
     step = step_ref[...]
     across = cumulate(step, rate_ref[...])
     cumulative = across.T
@@ -145,17 +165,19 @@
 
 def plain_part(values, gates, writes, reads, steps, rate, skip, after):
     shape = jax.ShapeDtypeStruct((ROWS, LANES), F32)
+    sources = (values, gates, writes, reads, steps, rate, skip)
     return pl.pallas_call(
         plain_kernel,
         out_shape=(shape, shape),
-        in_specs=[VMEM] * 7 + [ANY],
+        in_specs=[HBM] * 7 + [ANY],
         out_specs=(VMEM, VMEM),
+        scratch_shapes=room(sources),
         compiler_params=params(),
         cost_estimate=cost(
             2 * ROWS * ROWS * LANES, 7 * 2**20, HEADS * ROWS * ROWS + ROWS * LANES
         ),
         name="plain_part",
-    )(values, gates, writes, reads, steps, rate, skip, after)
+    )(*sources, after)
 
 
 def turn_kernel(place, prior_ref, _, out_ref):
@@ -196,7 +218,7 @@
 
 
 def chip_kernel(place, keep_ref, got_ref, *refs):
-    outs, total, logs = refs[:4], refs[4], refs[5]
+    outs, total, logs = refs[-6:-2], refs[-2], refs[-1]
     first = place[0] == 0
     kept, got = keep_ref[...], got_ref[...]
     state0 = jnp.where(first, kept, got)
@@ -209,17 +231,17 @@
         write_message(out_ref, total[:, at], logs[0:1, at])
 
 
-def chip_total(place, keep, got):
+def chip_total(place, keep, got, after):
     pieces = pl.pallas_call(
         chip_kernel,
         out_shape=[MESSAGE] * 4,
-        in_specs=[SMEM] + [VMEM] * 2,
+        in_specs=[SMEM] + [VMEM] * 2 + [ANY] * len(after),
         out_specs=[VMEM] * 4,
         scratch_shapes=[pltpu.VMEM((WIDTH, SPLIT), F32), pltpu.VMEM((8, SPLIT), F32)],
         compiler_params=params(),
         cost_estimate=cost(2 * WIDTH * SPLIT, 2**20),
         name="chip_total",
-    )(place, keep, got)
+    )(place, keep, got, *after)
     return list(pieces)
 
 
@@ -240,8 +262,9 @@
     return total, log
 
 
-def row_kernel(place, p0, p1, p2, p3, _plain, _prior, out_ref, before_ref):
+def row_kernel(place, p0, p1, p2, p3, *refs):
     parts = (p0, p1, p2, p3)
+    out_ref, before_ref = refs[-2:]
     write_message(out_ref, *fold(place[2], parts, 4))
     for k in range(4):
         total, log = fold(place[2], parts, lax.rem(place[2] + k, 4))
@@ -253,7 +276,7 @@
     return pl.pallas_call(
         row_kernel,
         out_shape=(MESSAGE, jax.ShapeDtypeStruct((4, WIDTH + 8, SLICE), F32)),
-        in_specs=[SMEM] + [VMEM] * 4 + [ANY] * 2,
+        in_specs=[SMEM] + [VMEM] * 4 + [ANY] * len(after),
         out_specs=(VMEM, VMEM),
         compiler_params=params(),
         cost_estimate=cost(40 * WIDTH * SLICE, 2**20),
@@ -282,7 +305,55 @@
     return list(pieces)
 
 
-def enter_kernel(place, p0, p1, p2, p3, keep_ref, got_ref, mine_ref, other_ref, chip):
+def row_enter_all_kernel(place, p0, p1, p2, p3, before_ref, prior_ref, *refs):
+    total, log = fold(place[3], (p0, p1, p2, p3), place[3])
+    entering = total + jnp.exp(log) * prior_ref[...]
+    for at in range(4):
+        before = before_ref[lax.rem(at - place[2] + 4, 4)]
+        decay = jnp.exp(before[WIDTH : WIDTH + 1, :])
+        refs[-1][at] = (decay * entering + before[0:WIDTH, :]).astype(BF16)
+
+
+def row_enter_all(place, parts, before, prior, after):
+    return pl.pallas_call(
+        row_enter_all_kernel,
+        out_shape=jax.ShapeDtypeStruct((4, WIDTH, SLICE), BF16),
+        in_specs=[SMEM] + [VMEM] * 6 + [ANY] * len(after),
+        out_specs=VMEM,
+        compiler_params=params(),
+        cost_estimate=cost(16 * WIDTH * SLICE, 2**20),
+        name="row_enter",
+    )(place, *parts, before, prior, *after)
+
+
+def enter_all_kernel(place, parts_ref, keep_ref, got_ref, *refs):
+    mine_ref, other_ref, chip = refs[-3:]
+    first = place[0] == 0
+    for at in range(4):
+        chip[:, at * SLICE : (at + 1) * SLICE] = parts_ref[at].astype(F32)
+    entering = chip[...]
+    state0 = jnp.where(first, keep_ref[...], got_ref[...])
+    second = jnp.exp(state0[WIDTH : WIDTH + 1]) * entering + state0[0:WIDTH]
+    mine_ref[...] = jnp.where(first, entering, second).astype(BF16)
+    other_ref[...] = jnp.where(first, second, entering).astype(BF16)
+
+
+def entering_state_all(place, parts, keep, got, after=()):
+    shape = jax.ShapeDtypeStruct((WIDTH, SPLIT), BF16)
+    return pl.pallas_call(
+        enter_all_kernel,
+        out_shape=(shape, shape),
+        in_specs=[SMEM] + [VMEM] * 3 + [ANY] * len(after),
+        out_specs=(VMEM, VMEM),
+        scratch_shapes=[pltpu.VMEM((WIDTH, SPLIT), F32)],
+        compiler_params=params(),
+        cost_estimate=cost(8 * WIDTH * SPLIT, 2 * 2**20),
+        name="entering_state",
+    )(place, parts, keep, got, *after)
+
+
+def enter_kernel(place, p0, p1, p2, p3, keep_ref, got_ref, *refs):
+    mine_ref, other_ref, chip = refs[-3:]
     first = place[0] == 0
     for k, part in enumerate((p0, p1, p2, p3)):
         chip[:, slice_of(place, -k)] = part[...].astype(F32)
@@ -293,23 +364,22 @@
     other_ref[...] = jnp.where(first, second, entering).astype(BF16)
 
 
-def entering_state(place, parts, keep, got):
+def entering_state(place, parts, keep, got, after=()):
     shape = jax.ShapeDtypeStruct((WIDTH, SPLIT), BF16)
     return pl.pallas_call(
         enter_kernel,
         out_shape=(shape, shape),
-        in_specs=[SMEM] + [VMEM] * 6,
+        in_specs=[SMEM] + [VMEM] * 6 + [ANY] * len(after),
         out_specs=(VMEM, VMEM),
         scratch_shapes=[pltpu.VMEM((WIDTH, SPLIT), F32)],
         compiler_params=params(),
         cost_estimate=cost(8 * WIDTH * SPLIT, 2 * 2**20),
         name="entering_state",
-    )(place, *parts, keep, got)
-
-
-def gated_kernel(
-    place, mine_ref, other_ref, read_ref, plain_ref, scale_ref, gain_ref, top_ref, low_ref, stat_ref, acc
-):
+    )(place, *parts, keep, got, *after)
+
+
+def gated_kernel(place, mine_ref, other_ref, read_ref, plain_ref, scale_ref, gain_ref, *refs):
+    top_ref, low_ref, stat_ref, acc = refs[-4:]
     step = pl.program_id(0)
     mine = place[0] == step // 2
     entering = jnp.where(mine, mine_ref[...], other_ref[...])
@@ -338,7 +408,7 @@
         stat_ref[:, 0:ROWS] = stack_rows(three(row), 16).astype(BF16)
 
 
-def gated_part(place, mine, other, reads, plain, scale, gain):
+def gated_part(place, mine, other, reads, plain, scale, gain, after):
     steps = 4
     width = LANES // steps
     half = pl.BlockSpec((HALF, width), lambda i, place: (0, i))
@@ -356,7 +426,8 @@
                 wide,
                 wide,
                 pl.BlockSpec((1, width), lambda i, place: (0, i)),
-            ],
+            ]
+            + [ANY] * len(after),
             out_specs=[half, half, whole((16, PIECE))],
             scratch_shapes=[pltpu.VMEM((ROWS, 128), F32)],
         ),
@@ -368,50 +439,112 @@
         compiler_params=params(),
         cost_estimate=cost(2 * ROWS * WIDTH * LANES, 6 * 2**20),
         name="gated_part",
-    )(place, mine, other, reads, plain, scale, gain)
-
-
-def project_kernel(has_stats, place, top_ref, low_ref, *refs):
+    )(place, mine, other, reads, plain, scale, gain, *after)
+
+
+def multiply(lefts, weights, out):
+    depth = LANES // len(weights)
+    for row, ref in enumerate(lefts):
+        rows = row * HALF
+        total = None
+        for part, weight in enumerate(weights):
+            at = slice(part * depth, (part + 1) * depth)
+            term = jnp.dot(ref[:, at], weight[...], preferred_element_type=F32)
+            total = term if total is None else total + term
+        out[rows : rows + HALF, :] = total.astype(BF16)
+
+
+def hand_out(place, total, outs):
     core, x, z = place[0], place[1], place[3]
-    outs = refs[-4:]
-    sides = (refs[0:5], refs[5:10])
-    depth = LANES // 2
-    left = jnp.concatenate([top_ref[...], low_ref[...]], axis=0)
-    for j in range(4):
-        k = lax.rem(z - x + j + 4, 4)
-        for side in range(2):
-            own, above, below, first, second = sides[side]
-            at = pl.ds(pl.multiple_of(256 * (core if side == 0 else 1 - core), 256), 256)
-            if j == 2:
-                total = jnp.dot(left[:, :depth], first[...], preferred_element_type=F32)
-                total += jnp.dot(left[:, depth:], second[...], preferred_element_type=F32)
+    for k in range(4):
+        out_ref = outs[k if k < 3 or len(outs) == 4 else 4]
+        j = lax.rem(x + k - z + 4, 4)
+        for half in range(2):
+            at = slice(half * 256, (half + 1) * 256)
+            side = lax.rem(half + core, 2)
+            if len(outs) == 5 and k == 2:
+                outs[2 + half][...] = total[j, side]
             else:
-                weight = {0: own, 1: above, 3: below}[j]
-                total = jnp.dot(left, weight[...], preferred_element_type=F32)
-            total = total.astype(BF16)
-            for place_k, out_ref in enumerate(outs):
-
-                @pl.when(k == place_k)
-                def _(out_ref=out_ref, at=at, total=total):
-                    out_ref[0:ROWS, at] = total
-
-    if has_stats:
+                out_ref[0 : total.shape[2], at] = total[j, side]
+
+
+def project_kernel(tall, count, far, stats, ring, place, *refs):
+    lefts, refs = refs[:tall], refs[tall:]
+    outs, total = refs[-5 - ring : -1], refs[-1]
+    for side in range(2):
+        own, above, below = refs[side * count : side * count + 3]
+        beyond = refs[side * count + 3 : side * count + 3 + far]
+        for j, parts in enumerate(((own,), (above,), beyond, (below,))):
+            multiply(lefts, parts, total.at[j, side])
+    hand_out(place, total, outs)
+    for stat in stats:
         for out_ref in outs:
-            out_ref[ROWS:, :] = refs[10][...]
-
-
-def project(place, top, low, weights, stats=None, after=()):
-    rows = ROWS if stats is None else ROWS + 16
+            out_ref[tall * HALF :, :] = refs[stat][...]
+
+
+def project(place, lefts, weights, stats=None, after=(), ring=False):
+    tall = len(lefts)
+    rows = tall * HALF + (0 if stats is None else 16)
     extra = () if stats is None else (stats,)
+    widths = [PIECE, PIECE, 256, 256, PIECE] if ring else [PIECE] * 4
+    count = len(weights) // 2
+    place_of_stats = (len(weights),) * len(extra)
     pieces = pl.pallas_call(
-        functools.partial(project_kernel, stats is not None),
-        in_specs=[SMEM] + [VMEM] * (12 + len(extra)) + [ANY] * len(after),
-        out_specs=[VMEM] * 4,
-        out_shape=[jax.ShapeDtypeStruct((rows, PIECE), BF16)] * 4,
+        functools.partial(project_kernel, tall, count, count - 3, place_of_stats, int(ring)),
+        in_specs=[SMEM] + [VMEM] * (tall + len(weights) + len(extra)) + [ANY] * len(after),
+        out_specs=[VMEM] * len(widths),
+        out_shape=[jax.ShapeDtypeStruct((rows, width), BF16) for width in widths],
+        scratch_shapes=[pltpu.VMEM((4, 2, tall * HALF, 256), BF16)],
         compiler_params=params(24),
         cost_estimate=cost(2 * ROWS * LANES * 4 * PIECE, 10 * 2**20),
         name="project",
-    )(place, top, low, *weights, *extra, *after)
+    )(place, *lefts, *weights, *extra, *after)
+    return list(pieces)
+
+
+def near_kernel(top_ref, low_ref, *refs):
+    out = refs[-1]
+    for side in range(2):
+        own, above, below = refs[3 * side : 3 * side + 3]
+        for j, part in ((0, own), (1, above), (2, below)):
+            multiply((top_ref, low_ref), (part,), out.at[j, side])
+
+
+def project_near(top, low, weights, after):
+    return pl.pallas_call(
+        near_kernel,
+        in_specs=[VMEM] * 8 + [ANY] * len(after),
+        out_specs=VMEM,
+        out_shape=jax.ShapeDtypeStruct((3, 2, ROWS, 256), BF16),
+        compiler_params=params(24),
+        cost_estimate=cost(2 * ROWS * LANES * 3 * PIECE, 8 * 2**20),
+        name="project_near",
+    )(top, low, *weights, *after)
+
+
+def far_kernel(place, top_ref, low_ref, *refs):
+    near, stat_ref, outs, total = refs[-7], refs[-6], refs[-5:-1], refs[-1]
+    for j, source in ((0, 0), (1, 1), (3, 2)):
+        total[j] = near[source]
+    parts = (len(refs) - 7) // 2
+    for side in range(2):
+        multiply((top_ref, low_ref), refs[parts * side : parts * side + parts], total.at[2, side])
+    hand_out(place, total, outs)
+    for out_ref in outs:
+        out_ref[ROWS:, :] = stat_ref[...]
+
+
+def project_far(place, top, low, weights, near, stats):
+    pieces = pl.pallas_call(
+        far_kernel,
+        in_specs=[SMEM] + [VMEM] * (4 + len(weights)),
+        out_specs=[VMEM] * 4,
+        out_shape=[jax.ShapeDtypeStruct((ROWS + 16, PIECE), BF16)] * 4,
+        scratch_shapes=[pltpu.VMEM((4, 2, ROWS, 256), BF16)],
+        compiler_params=params(24),
+        cost_estimate=cost(2 * ROWS * LANES * PIECE, 4 * 2**20),
+        name="project_far",
+    )(place, top, low, *weights, near, stats)
     return list(pieces)
 
 
@@ -422,19 +555,24 @@
     return total
 
 
-def sums_kernel(*refs):
-    first, second, (down_ref, up_ref) = refs[0:4], refs[4:8], refs[8:]
+def start_of(part):
+    return ROWS if part.shape[0] > 2 * ROWS else 0
+
+
+def sums_kernel(count, *refs):
+    first, second, (down_ref, up_ref) = refs[:count], refs[count:-2], refs[-2:]
     for at, parts in ((0, first), (HALF, second)):
-        down_ref[at : at + HALF, :] = add(parts, slice(0, HALF)).astype(BF16)
-        up_ref[at : at + HALF, :] = add(parts, slice(HALF, ROWS)).astype(BF16)
+        row = start_of(parts[0])
+        down_ref[at : at + HALF, :] = add(parts, slice(row, row + HALF)).astype(BF16)
+        up_ref[at : at + HALF, :] = add(parts, slice(row + HALF, row + ROWS)).astype(BF16)
 
 
 def neighbour_sums(first, second):
     shape = jax.ShapeDtypeStruct((ROWS, PIECE), BF16)
     return pl.pallas_call(
-        sums_kernel,
+        functools.partial(sums_kernel, len(first)),
         out_shape=(shape, shape),
-        in_specs=[VMEM] * 8,
+        in_specs=[VMEM] * (len(first) + len(second)),
         out_specs=(VMEM, VMEM),
         compiler_params=params(),
         cost_estimate=cost(8 * ROWS * PIECE, 10 * ROWS * PIECE * 2),
@@ -443,14 +581,15 @@
 
 
 def sum_kernel(*refs):
-    refs[4][...] = add(refs[0:4], slice(0, ROWS)).astype(BF16)
+    row = start_of(refs[0])
+    refs[-1][...] = add(refs[:-1], slice(row, row + ROWS)).astype(BF16)
 
 
 def far_sums(parts):
     return pl.pallas_call(
         sum_kernel,
         out_shape=jax.ShapeDtypeStruct((ROWS, PIECE), BF16),
-        in_specs=[VMEM] * 4,
+        in_specs=[VMEM] * len(parts),
         out_specs=VMEM,
         compiler_params=params(),
         cost_estimate=cost(4 * ROWS * PIECE, 5 * ROWS * PIECE * 2),
@@ -458,46 +597,95 @@
     )(*parts)
 
 
-def finish_kernel(place, p0, p1, p2, p3, up_ref, far_ref, down_ref, residual_ref, out_ref):
+def merge_kernel(up_ref, down_ref, left_ref, right_ref, sum_up_ref, sum_down_ref):
+    for ref, half_ref, out_ref, at in (
+        (up_ref, left_ref, sum_up_ref, 0),
+        (down_ref, right_ref, sum_down_ref, 256),
+    ):
+        out_ref[:, 256 - at : 512 - at] = ref[:, 256 - at : 512 - at]
+        total = ref[:, at : at + 256].astype(F32) + half_ref[...].astype(F32)
+        out_ref[:, at : at + 256] = total.astype(BF16)
+
+
+def merge(up, down, left, right):
+    shape = jax.ShapeDtypeStruct((ROWS, PIECE), BF16)
+    return pl.pallas_call(
+        merge_kernel,
+        out_shape=(shape, shape),
+        in_specs=[VMEM] * 4,
+        out_specs=(VMEM, VMEM),
+        compiler_params=params(),
+        cost_estimate=cost(ROWS * PIECE, 5 * ROWS * PIECE * 2),
+        name="merge",
+    )(up, down, left, right)
+
+
+def write_columns(out_ref, residual_ref, scale, total):
+    for at in range(0, PIECE, 128):
+        cols = slice(at, at + 128)
+        out_ref[:, cols] = (residual_ref[:, cols].astype(F32) + scale * total[:, cols]).astype(BF16)
+
+
+def finish_kernel(tall, place, p0, p1, p2, p3, up_ref, down_ref, residual_ref, _, out_ref, scale_ref):
     own = (p0, p1, p2, p3)
-    square = sum(unpack_rows(part[ROWS : ROWS + 16, 0:ROWS]) for part in own)
-    row = lax.rsqrt(square / INNER + EPSILON)
-    scale = jnp.broadcast_to(row, (128, ROWS)).T
     step = pl.program_id(0)
-
-    def write(total):
-        for at in range(0, PIECE, 128):
-            cols = slice(at, at + 128)
-            out_ref[:, cols] = (residual_ref[:, cols].astype(F32) + scale * total[:, cols]).astype(
-                BF16
-            )
 
     @pl.when(step == 0)
     def _():
-        write(add(own, slice(0, ROWS)))
-
-    for k, ref in ((1, up_ref), (2, far_ref), (3, down_ref)):
+        square = sum(unpack_rows(part[tall : tall + 16, 0:ROWS]) for part in own)
+        row = lax.rsqrt(square / INNER + EPSILON)
+        scale_ref[...] = jnp.broadcast_to(row, (128, ROWS)).T
+        write_columns(out_ref, residual_ref, scale_ref[...], add(own, slice(0, ROWS)))
+
+    for k, ref in ((1, up_ref), (2, down_ref)):
 
         @pl.when(step == k)
         def _(ref=ref):
-            write(ref[...].astype(F32))
-
-
-def finish(place, own, up, far, down, residual):
-    block = pl.BlockSpec((ROWS, PIECE), lambda i, place: (0, lax.rem(place[2] + i, 4)))
-    return pl.pallas_call(
-        finish_kernel,
+            write_columns(out_ref, residual_ref, scale_ref[...], ref[...].astype(F32))
+
+
+OUT = jax.ShapeDtypeStruct((ROWS, 4 * PIECE), BF16)
+
+
+def finish(place, own, up, down, residual, after):
+    block = pl.BlockSpec(
+        (ROWS, PIECE), lambda i, place: (0, lax.rem(place[2] + jnp.where(i == 2, 3, i), 4))
+    )
+    return pl.pallas_call(
+        functools.partial(finish_kernel, own[0].shape[0] - 16),
         grid_spec=pltpu.PrefetchScalarGridSpec(
             num_scalar_prefetch=1,
-            grid=(4,),
-            in_specs=[whole((ROWS + 16, PIECE))] * 4 + [whole((ROWS, PIECE))] * 3 + [block],
+            grid=(3,),
+            in_specs=[whole(own[0].shape)] * 4 + [whole((ROWS, PIECE))] * 2 + [block, ANY],
+            out_specs=[block, whole((ROWS, 128))],
+        ),
+        out_shape=(OUT, jax.ShapeDtypeStruct((ROWS, 128), F32)),
+        compiler_params=params(),
+        cost_estimate=cost(4 * ROWS * 3 * PIECE, 3 * 2**20),
+        name="finish",
+    )(place, *own, up, down, residual, after)
+
+
+def finish_far_kernel(place, far_ref, scale_ref, residual_ref, _, out_ref):
+    write_columns(out_ref, residual_ref, scale_ref[...], far_ref[...].astype(F32))
+
+
+def finish_far(place, far, scale, residual, out):
+    block = pl.BlockSpec((ROWS, PIECE), lambda i, place: (0, lax.rem(place[2] + 2, 4)))
+    return pl.pallas_call(
+        finish_far_kernel,
+        grid_spec=pltpu.PrefetchScalarGridSpec(
+            num_scalar_prefetch=1,
+            grid=(1,),
+            in_specs=[whole((ROWS, PIECE)), whole((ROWS, 128)), block, ANY],
             out_specs=block,
         ),
-        out_shape=jax.ShapeDtypeStruct((ROWS, 4 * PIECE), BF16),
-        compiler_params=params(),
-        cost_estimate=cost(4 * ROWS * 4 * PIECE, 4 * 2**20),
-        name="finish",
-    )(place, *own, up, far, down, residual)
+        out_shape=OUT,
+        input_output_aliases={4: 0},
+        compiler_params=params(),
+        cost_estimate=cost(4 * ROWS * PIECE, 2**20),
+        name="finish_far",
+    )(place, far, scale, residual, out)
 
 
 def shift(value, axis, by):
@@ -513,7 +701,11 @@
 
 
 def scatter(pieces, axis="x"):
-    return [pieces[0]] + [shift(pieces[k], axis, k) for k in (1, 2, 3)]
+    if len(pieces) == 4:
+        return [pieces[0]] + [shift(pieces[k], axis, k) for k in (1, 2, 3)]
+    here, up, left, right, down = pieces
+    up, down = merge(up, down, shift(left, axis, 1), shift(right, axis, -1))
+    return [here, shift(up, axis, 1), shift(down, axis, -1)]
 
 
 def body(
@@ -536,41 +728,50 @@
     from_below, from_above = shift(out_weight, "z", 1), shift(out_weight, "z", -1)
     keep, send = local_state(place, head_values, write_keys, steps, rate)
     got = swap(send)
-    chips = chip_total(place, keep, got)
-    plain, scale = plain_part(
-        head_values, gate_values, write_keys, read_keys, steps, rate, skip_weight[None, :], chips[0]
-    )
+    weight = [out_weight, from_above, from_below]
+    swapped = [swap(out_weight)]
+    chips = chip_total(place, keep, got, [])
+    sources = (head_values, gate_values, write_keys, read_keys, steps, rate, skip_weight[None, :])
+    plain, scale = plain_part(*sources, chips[0])
     prior = turned_prior(place, prior_state, chips[0])
-    row, before = row_total(place, scatter(chips, "y"), (plain, prior))
+    row, before = row_total(place, scatter(chips, "y"), (prior, plain,))
     rows = scatter([row] * 4, "z")
-    kept = [out_weight, from_above, from_below]
-    swapped = [swap(part) for part in kept]
-    entering = scatter(row_enter(place, rows, before, prior, kept[1:]), "y")
+    swapped += [swap(part) for part in later(weight[1:], rows[1:])]
+    entered = row_enter(place, rows, before, prior, [*weight[1:]])
     depth = out_weight.shape[0] // 2
-    kept += [shift(from_below[:depth], "z", 1), shift(from_above[depth:], "z", -1)]
-    mine, other = entering_state(place, entering, keep, got)
+    halves = (from_below[:depth], from_above[depth:])
+    halves = later(halves, entered)
+    entering = scatter(entered, "y")
+    far_weight = [shift(halves[0], "z", 1), shift(halves[1], "z", -1)]
+    mine, other = entering_state(place, entering, keep, got, [*swapped])
     other = swap(other)
-    top, low, stats = gated_part(place, mine, other, read_keys, plain, scale, norm_gain[None, :])
-    swapped += [swap(part) for part in later(kept[3:], [stats])]
-    weights = kept + swapped
-
+    gain = norm_gain[None, :]
+    top, low, stats = gated_part(place, mine, other, read_keys, plain, scale, gain, [])
     top_below, top_above = shift(top, "y", 1), shift(top, "y", -1)
-    low_below, low_above = shift(low, "y", 1), shift(low, "y", -1)
-
-    own = scatter(project(place, top, low, weights, stats))
-    first = project(place, top_below, top_above, weights, None, own[:1])
-    top_go, low_go = later((top_below, low_above), (top_above, low_below, first[0]))
-    top_far, low_far = shift(top_go, "y", 1), shift(low_go, "y", -1)
-    second = project(place, low_below, low_above, weights, None, own[1:] + first[:1])
+    near = project_near(top, low, weight + swapped, [])
+    far_swapped = [swap(part) for part in later(far_weight, [near])]
+    weights = weight + far_weight + swapped + far_swapped
+    own = project_far(place, top, low, far_weight + far_swapped, near, stats)
+    low_go = low
+    (low_go,) = later([low], [top_below, top_above])
+    low_below, low_above = shift(low_go, "y", 1), shift(low_go, "y", -1)
+    own = scatter(own)
+    first = project(place, [top_below, top_above], weights, None, [], False)
+    go = (top_below, low_above)
+    top_far, low_far = shift(go[0], "y", 1), shift(go[1], "y", -1)
     first = scatter(first)
-    far = scatter(project(place, top_far, low_far, weights, None, first[1:] + second[:1]))
+    second = project(place, [low_below, low_above], weights, None, own[1:] + first[:1], False)
     second = scatter(second)
+    far = project(place, [top_far, low_far], weights, None, second[:1], False)
+    far = scatter(far)
 
     down, up = neighbour_sums(first, second)
     from_above = shift(down, "y", -1)
     from_below = shift(up, "y", 1)
-    from_far = shift(far_sums(far), "y", 2)
-    return finish(place, own, from_above, from_far, from_below, residual)
+    far = far_sums(far)
+    from_far = shift(far, "y", 2)
+    out, scale = finish(place, own, from_above, from_below, residual, far)
+    return finish_far(place, from_far, scale, residual, out)
 
 
 def solution(mesh):

time: 133 us -> 133 us (level)
  waiting for transfers between devices: 31.1 us -> 44 us
  Pallas kernels: 39.7 us -> 28.4 us
    ppermute x34, waiting for transfers between devices: 27.4 us -> 40.5 us  [shift(): return lax.ppermute(value, axis, [(i, (i + by) % 4) for i in range(4)])]
    pallas_call x8 -> x10, Pallas kernels: 33.2 us -> 21.9 us  [the longest x3 8.95 us: project(): pl.pallas_call(functools.partial(project_kernel, tall, count, count - 3,...]
    unnamed x26 -> x28, local copies, waits for them, and re-layouts: 3.48 us -> 3.48 us
  transfers between devices with their start and end apart: 41 -> 41, of which waited for: 15 -> 18; matrix products, arithmetic and copies ran while one was open for 0% -> 0% of each run, Pallas kernels for 27% -> 20%
where the time goes in v3:
time: 133 us
  starting transfers between devices  56.7 us (43%)
  waiting for transfers between devices  44 us (33%)
  Pallas kernels  28.4 us (21%)
  local copies, waits for them, and re-layouts  3.55 us (3%)
    ppermute x34, starting transfers between devices, shift(): return lax.ppermute(value, axis, [(i, (i + by) % 4) for i in range(4)])  55.3 us
    ppermute x34, waiting for transfers between devices, shift(): return lax.ppermute(value, axis, [(i, (i + by) % 4) for i in range(4)])  40.5 us
    pallas_call x3, Pallas kernels, project(): pl.pallas_call(functools.partial(project_kernel, tall, count, count - 3,...  8.95 us
    unnamed x28, local copies, waits for them, and re-layouts  3.48 us
    ppermute x7, waiting for transfers between devices, swap(): return lax.ppermute(value, 'core', [(0, 1), (1, 0)])  3.48 us
    pallas_call x1, Pallas kernels, plain_part(): pl.pallas_call(plain_kernel, out_shape=(shape, shape), in_specs=[HBM] * 7...  3.12 us
  transfers between devices with their start and end apart: 41, of which 18 were waited for; matrix products, arithmetic and copies ran while one was open for 0% of the time, Pallas kernels for 20%

profile of v3, /device:TPU:2, one launch (start us, length us, event | category | flops | bytes accessed | tf_op | source)
XLA Modules:
  0.0 133.0 jit_solution(14259456701388485117)
XLA Ops:
  0.0 4.0 %collective-permute-start.7 = (bf16[2048,256]{1,0:T(8,128)(2,1)}, bf16[2048,256]{1,0:T(8,128)(2,1)S(1)}, u32[]{:S(2)}, u32[]{:S(2)}) collective-permute-start(bf16[2048,256]{1,0:T(8,128)(2,1)} %refs_2_.7), channel_id=1, source_target_pairs={{0,96},{32,0},{64,32},{96,64},{1,97},{33,1},{65,33},{97,65},{2,98}... | collective-permute-start | bytes 3145736 | tf_op jit(solution)/shard_map/ppermute | solution.py:692
  4.1 1.2 copy-done.1
  7.6 2.6 %local_state.1 = (f32[136,1024]{1,0:T(8,128)S(1)}, f32[136,1024]{1,0:T(8,128)S(1)}) custom-call(s32[4]{0:T(128)S(1)} %pad_add_fusion.place, bf16[256,2048]{1,0:T(8,128)(2,1)S(1)} %copy-done.1, bf16[256,128]{1,0:T(8,128)(2,1)S(1)} %copy-done.7, f32[16,256]{1,0:T(8,128)S(1)} %bitcast.8, f32[1,16]{1,0:T(1,128)S(1)} %bitcast.11), custom_call_target="tpu_custom_call" | custom-call | flops 134217728 | bytes 3145728 | tf_op jit(solution)/shard_map/local_state/pallas_call | solution.py:128
  10.3 1.9 %collective-permute-done.got_ref = f32[136,1024]{1,0:T(8,128)S(1)} collective-permute-done((f32[136,1024]{1,0:T(8,128)S(1)}, f32[136,1024]{1,0:T(8,128)S(1)}, u32[]{:S(2)}, u32[]{:S(2)}) %collective-permute-start) | collective-permute-done | bytes 557088 | tf_op jit(solution)/shard_map/ppermute | solution.py:696
  13.1 1.6 %collective-permute-start.1 = (bf16[144,256]{1,0:T(8,128)(2,1)S(1)}, bf16[144,256]{1,0:T(8,128)(2,1)S(1)}, u32[]{:S(2)}, u32[]{:S(2)}) collective-permute-start(bf16[144,256]{1,0:T(8,128)(2,1)S(1)} %get-tuple-element.54), channel_id=1, source_target_pairs={{0,8},{8,16},{16,24},{24,0},{1,9},{9,17},{17,25},{25,1},{2,10},{10... | collective-permute-start | bytes 221192 | tf_op jit(solution)/shard_map/ppermute | solution.py:692
  14.7 2.9 %collective-permute-start.2 = (bf16[144,256]{1,0:T(8,128)(2,1)S(1)}, bf16[144,256]{1,0:T(8,128)(2,1)S(1)}, u32[]{:S(2)}, u32[]{:S(2)}) collective-permute-start(bf16[144,256]{1,0:T(8,128)(2,1)S(1)} %get-tuple-element.55), channel_id=1, source_target_pairs={{0,16},{8,24},{16,0},{24,8},{1,17},{9,25},{17,1},{25,9},{2,18},{10... | collective-permute-start | bytes 221192 | tf_op jit(solution)/shard_map/ppermute | solution.py:692
  17.6 1.3 %collective-permute-start.3 = (bf16[144,256]{1,0:T(8,128)(2,1)S(1)}, bf16[144,256]{1,0:T(8,128)(2,1)S(1)}, u32[]{:S(2)}, u32[]{:S(2)}) collective-permute-start(bf16[144,256]{1,0:T(8,128)(2,1)S(1)} %get-tuple-element.56), channel_id=1, source_target_pairs={{0,24},{8,0},{16,8},{24,16},{1,25},{9,1},{17,9},{25,17},{2,26},{10... | collective-permute-start | bytes 221192 | tf_op jit(solution)/shard_map/ppermute | solution.py:692
  19.8 3.1 %plain_part.1 = (f32[256,2048]{1,0:T(8,128)S(1)}, f32[256,2048]{1,0:T(8,128)S(1)}) custom-call(bf16[256,2048]{1,0:T(8,128)(2,1)S(1)} %copy-done.2, bf16[256,2048]{1,0:T(8,128)(2,1)S(1)} %copy-done.5, bf16[256,128]{1,0:T(8,128)(2,1)S(1)} %copy-done.8, bf16[256,128]{1,0:T(8,128)(2,1)S(1)} %copy-done.6, f32[16,256]{1,0:T(8,128)S(1)} %bitcast.9, ...), custom_call_target="tpu_custom_call" | custom-call | flops 268435456 | bytes 7340032 | tf_op jit(solution)/shard_map/plain_part/pallas_call | solution.py:169
  24.0 4.7 %collective-permute-start.5 = (bf16[144,256]{1,0:T(8,128)(2,1)S(1)}, bf16[144,256]{1,0:T(8,128)(2,1)S(1)}, u32[]{:S(2)}, u32[]{:S(2)}) collective-permute-start(bf16[144,256]{1,0:T(8,128)(2,1)S(1)} %get-tuple-element.58.p0), channel_id=1, source_target_pairs={{0,64},{32,96},{64,0},{96,32},{1,65},{33,97},{65,1},{97,33},{2,66}... | collective-permute-start | bytes 221192 | tf_op jit(solution)/shard_map/ppermute | solution.py:692
  28.7 4.6 %collective-permute-done.4.p1 = bf16[144,256]{1,0:T(8,128)(2,1)S(1)} collective-permute-done((bf16[144,256]{1,0:T(8,128)(2,1)S(1)}, bf16[144,256]{1,0:T(8,128)(2,1)S(1)}, u32[]{:S(2)}, u32[]{:S(2)}) %collective-permute-start.4) | collective-permute-done | bytes 73760 | tf_op jit(solution)/shard_map/ppermute | solution.py:692
  34.6 3.3 %collective-permute-start.10 = (bf16[128,256]{1,0:T(8,128)(2,1)S(1)}, bf16[128,256]{1,0:T(8,128)(2,1)S(1)}, u32[]{:S(2)}, u32[]{:S(2)}) collective-permute-start(bf16[128,256]{1,0:T(8,128)(2,1)S(1)} %get-tuple-element.62), channel_id=1, source_target_pairs={{0,16},{8,24},{16,0},{24,8},{1,17},{9,25},{17,1},{25,9},{2,18},{10... | collective-permute-start | bytes 196616 | tf_op jit(solution)/shard_map/ppermute | solution.py:692
  37.9 1.1 collective-permute-start.11
  40.7 1.7 %collective-permute-done.11.p3 = bf16[128,256]{1,0:T(8,128)(2,1)S(1)} collective-permute-done((bf16[128,256]{1,0:T(8,128)(2,1)S(1)}, bf16[128,256]{1,0:T(8,128)(2,1)S(1)}, u32[]{:S(2)}, u32[]{:S(2)}) %collective-permute-start.11) | collective-permute-done | bytes 65568 | tf_op jit(solution)/shard_map/ppermute | solution.py:692
  42.4 1.5 %collective-permute-start.22 = (bf16[1024,256]{1,0:T(8,128)(2,1)S(1)}, bf16[1024,256]{1,0:T(8,128)(2,1)S(1)}, u32[]{:S(2)}, u32[]{:S(2)}) collective-permute-start(bf16[1024,256]{1,0:T(8,128)(2,1)S(1)} %slice.9), channel_id=1, source_target_pairs={{0,96},{32,0},{64,32},{96,64},{1,97},{33,1},{65,33},{97,65},{2,98}... | collective-permute-start | bytes 1572872 | tf_op jit(solution)/shard_map/ppermute | solution.py:692
  45.4 1.5 %collective-permute-done.15.other_ref = bf16[128,1024]{1,0:T(8,128)(2,1)S(1)} collective-permute-done((bf16[128,1024]{1,0:T(8,128)(2,1)S(1)}, bf16[128,1024]{1,0:T(8,128)(2,1)S(1)}, u32[]{:S(2)}, u32[]{:S(2)}) %collective-permute-start.15) | collective-permute-done | bytes 262176 | tf_op jit(solution)/shard_map/ppermute | solution.py:696
  47.0 2.3 %gated_part.1 = (bf16[128,2048]{1,0:T(8,128)(2,1)S(1)}, bf16[128,2048]{1,0:T(8,128)(2,1)S(1)}, bf16[16,512]{1,0:T(8,128)(2,1)S(1)}) custom-call(s32[4]{0:T(128)S(1)} %pad_add_fusion.place, bf16[128,1024]{1,0:T(8,128)(2,1)S(1)} %get-tuple-element.66.mine_ref, bf16[128,1024]{1,0:T(8,128)(2,1)S(1)} %collective-permute-done.15.other_ref, ...), custom_call_target="tpu_custom_call" | custom-call | flops 134217728 | bytes 6291456 | tf_op jit(solution)/shard_map/gated_part/pallas_call | solution.py:417
  49.2 1.6 %collective-permute-start.16 = (bf16[128,2048]{1,0:T(8,128)(2,1)S(1)}, bf16[128,2048]{1,0:T(8,128)(2,1)S(1)}, u32[]{:S(2)}, u32[]{:S(2)}) collective-permute-start(bf16[128,2048]{1,0:T(8,128)(2,1)S(1)} %get-tuple-element.69.top_ref), channel_id=1, source_target_pairs={{0,8},{8,16},{16,24},{24,0},{1,9},{9,17},{17,25},{25,1},{2,10},{10... | collective-permute-start | bytes 1572872 | tf_op jit(solution)/shard_map/ppermute | solution.py:692
  50.8 1.7 %collective-permute-start.18 = (bf16[128,2048]{1,0:T(8,128)(2,1)S(1)}, bf16[128,2048]{1,0:T(8,128)(2,1)S(1)}, u32[]{:S(2)}, u32[]{:S(2)}) collective-permute-start(bf16[128,2048]{1,0:T(8,128)(2,1)S(1)} %get-tuple-element.69.top_ref), channel_id=1, source_target_pairs={{0,24},{8,0},{16,8},{24,16},{1,25},{9,1},{17,9},{25,17},{2,26},{10... | collective-permute-start | bytes 1572872 | tf_op jit(solution)/shard_map/ppermute | solution.py:692
  52.5 1.8 %project_near.1.refs_4_ = bf16[3,2,256,256]{3,2,1,0:T(8,128)(2,1)S(1)} custom-call(bf16[128,2048]{1,0:T(8,128)(2,1)S(1)} %get-tuple-element.69.top_ref, bf16[128,2048]{1,0:T(8,128)(2,1)S(1)} %get-tuple-element.71.low_ref, bf16[2048,256]{1,0:T(8,128)(2,1)S(1)} %copy-done, bf16[2048,256]{1,0:T(8,128)(2,1)S(1)} %collective-permute-done.7.refs_0_.refs_1_.refs_3_, ...), custom_call_target="tpu_custom_call" | custom-call | flops 1610612736 | bytes 8388608 | tf_op jit(solution)/shard_map/project_near/pallas_call | solution.py:514
  56.4 8.1 %collective-permute-done.16.refs_0_ = bf16[128,2048]{1,0:T(8,128)(2,1)S(1)} collective-permute-done((bf16[128,2048]{1,0:T(8,128)(2,1)S(1)}, bf16[128,2048]{1,0:T(8,128)(2,1)S(1)}, u32[]{:S(2)}, u32[]{:S(2)}) %collective-permute-start.16) | collective-permute-done | bytes 524320 | tf_op jit(solution)/shard_map/ppermute | solution.py:692
  64.5 3.1 %collective-permute-start.19 = (bf16[128,2048]{1,0:T(8,128)(2,1)S(1)}, bf16[128,2048]{1,0:T(8,128)(2,1)S(1)}, u32[]{:S(2)}, u32[]{:S(2)}) collective-permute-start(bf16[128,2048]{1,0:T(8,128)(2,1)S(1)} %get-tuple-element.71.low_ref), channel_id=1, source_target_pairs={{0,24},{8,0},{16,8},{24,16},{1,25},{9,1},{17,9},{25,17},{2,26},{10... | collective-permute-start | bytes 1572872 | tf_op jit(solution)/shard_map/ppermute | solution.py:692
  67.6 1.4 %project_far.1 = (bf16[272,512]{1,0:T(8,128)(2,1)S(1)}, bf16[272,512]{1,0:T(8,128)(2,1)S(1)}, bf16[272,512]{1,0:T(8,128)(2,1)S(1)}, bf16[272,512]{1,0:T(8,128)(2,1)S(1)}) custom-call(s32[4]{0:T(128)S(1)} %pad_add_fusion.place, bf16[128,2048]{1,0:T(8,128)(2,1)S(1)} %get-tuple-element.69.top_ref, bf16[128,2048]{1,0:T(8,128)(2,1)S(1)} %get-tuple-element.71.low_ref, ...), custom_call_target="tpu_custom_call" | custom-call | flops 536870912 | bytes 4194304 | tf_op jit(solution)/shard_map/project_far/pallas_call | solution.py:538
  69.0 1.6 %collective-permute-start.26 = (bf16[272,512]{1,0:T(8,128)(2,1)S(1)}, bf16[272,512]{1,0:T(8,128)(2,1)S(1)}, u32[]{:S(2)}, u32[]{:S(2)}) collective-permute-start(bf16[272,512]{1,0:T(8,128)(2,1)S(1)} %get-tuple-element.77), channel_id=1, source_target_pairs={{0,1},{1,2},{2,3},{3,0},{4,5},{5,6},{6,7},{7,4},{8,9},{9,10},{10,1... | collective-permute-start | bytes 835592 | tf_op jit(solution)/shard_map/ppermute | solution.py:692
  70.6 1.1 collective-permute-start.27
  71.7 2.2 %collective-permute-start.28 = (bf16[272,512]{1,0:T(8,128)(2,1)S(1)}, bf16[272,512]{1,0:T(8,128)(2,1)S(1)}, u32[]{:S(2)}, u32[]{:S(2)}) collective-permute-start(bf16[272,512]{1,0:T(8,128)(2,1)S(1)} %get-tuple-element.79), channel_id=1, source_target_pairs={{0,3},{1,0},{2,1},{3,2},{4,7},{5,4},{6,5},{7,6},{8,11},{9,8},{10,9... | collective-permute-start | bytes 835592 | tf_op jit(solution)/shard_map/ppermute | solution.py:692
  73.8 4.8 %collective-permute-done.26.refs_12_.p1 = bf16[272,512]{1,0:T(8,128)(2,1)S(1)} collective-permute-done((bf16[272,512]{1,0:T(8,128)(2,1)S(1)}, bf16[272,512]{1,0:T(8,128)(2,1)S(1)}, u32[]{:S(2)}, u32[]{:S(2)}) %collective-permute-start.26) | collective-permute-done | bytes 278560 | tf_op jit(solution)/shard_map/ppermute | solution.py:692
  78.7 3.2 %collective-permute-start.20 = (bf16[128,2048]{1,0:T(8,128)(2,1)S(1)}, bf16[128,2048]{1,0:T(8,128)(2,1)S(1)}, u32[]{:S(2)}, u32[]{:S(2)}) collective-permute-start(bf16[128,2048]{1,0:T(8,128)(2,1)S(1)} %collective-permute-done.19.refs_1_), channel_id=1, source_target_pairs={{0,24},{8,0},{16,8},{24,16},{1,25},{9,1},{17,9},{25,17},{2,26},{10... | collective-permute-start | bytes 1572872 | tf_op jit(solution)/shard_map/ppermute | solution.py:692
  81.9 3.0 %project.3 = (bf16[256,512]{1,0:T(8,128)(2,1)S(1)}, bf16[256,512]{1,0:T(8,128)(2,1)S(1)}, bf16[256,512]{1,0:T(8,128)(2,1)S(1)}, bf16[256,512]{1,0:T(8,128)(2,1)S(1)}) custom-call(s32[4]{0:T(128)S(1)} %pad_add_fusion.place, bf16[128,2048]{1,0:T(8,128)(2,1)S(1)} %collective-permute-done.16.refs_0_, bf16[128,2048]{1,0:T(8,128)(2,1)S(1)} %collective-permute-done.18.refs_1_, ...), custom_call_target="tpu_custom_call" | custom-call | flops 2147483648 | bytes 10485760 | tf_op jit(solution)/shard_map/project/pallas_call | solution.py:492
  84.9 1.6 %collective-permute-start.33 = (bf16[256,512]{1,0:T(8,128)(2,1)S(1)}, bf16[256,512]{1,0:T(8,128)(2,1)S(1)}, u32[]{:S(2)}, u32[]{:S(2)}) collective-permute-start(bf16[256,512]{1,0:T(8,128)(2,1)S(1)} %get-tuple-element.87), channel_id=1, source_target_pairs={{0,1},{1,2},{2,3},{3,0},{4,5},{5,6},{6,7},{7,4},{8,9},{9,10},{10,1... | collective-permute-start | bytes 786440 | tf_op jit(solution)/shard_map/ppermute | solution.py:692
  86.5 1.3 collective-permute-start.34
  87.8 1.9 %collective-permute-start.35 = (bf16[256,512]{1,0:T(8,128)(2,1)S(1)}, bf16[256,512]{1,0:T(8,128)(2,1)S(1)}, u32[]{:S(2)}, u32[]{:S(2)}) collective-permute-start(bf16[256,512]{1,0:T(8,128)(2,1)S(1)} %get-tuple-element.89), channel_id=1, source_target_pairs={{0,3},{1,0},{2,1},{3,2},{4,7},{5,4},{6,5},{7,6},{8,11},{9,8},{10,9... | collective-permute-start | bytes 786440 | tf_op jit(solution)/shard_map/ppermute | solution.py:692
  89.7 3.0 %project.4 = (bf16[256,512]{1,0:T(8,128)(2,1)S(1)}, bf16[256,512]{1,0:T(8,128)(2,1)S(1)}, bf16[256,512]{1,0:T(8,128)(2,1)S(1)}, bf16[256,512]{1,0:T(8,128)(2,1)S(1)}) custom-call(s32[4]{0:T(128)S(1)} %pad_add_fusion.place, bf16[128,2048]{1,0:T(8,128)(2,1)S(1)} %collective-permute-done.25.refs_0_, bf16[128,2048]{1,0:T(8,128)(2,1)S(1)} %collective-permute-done.19.refs_1_, ...), custom_call_target="tpu_custom_call" | custom-call | flops 2147483648 | bytes 10485760 | tf_op jit(solution)/shard_map/project/pallas_call | solution.py:492
  92.7 2.1 %collective-permute-done.33.refs_1_ = bf16[256,512]{1,0:T(8,128)(2,1)S(1)} collective-permute-done((bf16[256,512]{1,0:T(8,128)(2,1)S(1)}, bf16[256,512]{1,0:T(8,128)(2,1)S(1)}, u32[]{:S(2)}, u32[]{:S(2)}) %collective-permute-start.33) | collective-permute-done | bytes 262176 | tf_op jit(solution)/shard_map/ppermute | solution.py:692
  94.8 3.0 %collective-permute-start.36 = (bf16[256,512]{1,0:T(8,128)(2,1)S(1)}, bf16[256,512]{1,0:T(8,128)(2,1)S(1)}, u32[]{:S(2)}, u32[]{:S(2)}) collective-permute-start(bf16[256,512]{1,0:T(8,128)(2,1)S(1)} %get-tuple-element.90), channel_id=1, source_target_pairs={{0,1},{1,2},{2,3},{3,0},{4,5},{5,6},{6,7},{7,4},{8,9},{9,10},{10,1... | collective-permute-start | bytes 786440 | tf_op jit(solution)/shard_map/ppermute | solution.py:692
  98.5 1.3 collective-permute-start.38
  99.8 3.0 %project.5 = (bf16[256,512]{1,0:T(8,128)(2,1)S(1)}, bf16[256,512]{1,0:T(8,128)(2,1)S(1)}, bf16[256,512]{1,0:T(8,128)(2,1)S(1)}, bf16[256,512]{1,0:T(8,128)(2,1)S(1)}) custom-call(s32[4]{0:T(128)S(1)} %pad_add_fusion.place, bf16[128,2048]{1,0:T(8,128)(2,1)S(1)} %collective-permute-done.17.refs_0_, bf16[128,2048]{1,0:T(8,128)(2,1)S(1)} %collective-permute-done.20.refs_1_, ...), custom_call_target="tpu_custom_call" | custom-call | flops 2147483648 | bytes 10485760 | tf_op jit(solution)/shard_map/project/pallas_call | solution.py:492
  103.6 4.0 %collective-permute-start.30 = (bf16[256,512]{1,0:T(8,128)(2,1)S(1)}, bf16[256,512]{1,0:T(8,128)(2,1)S(1)}, u32[]{:S(2)}, u32[]{:S(2)}) collective-permute-start(bf16[256,512]{1,0:T(8,128)(2,1)S(1)} %get-tuple-element.84), channel_id=1, source_target_pairs={{0,2},{1,3},{2,0},{3,1},{4,6},{5,7},{6,4},{7,5},{8,10},{9,11},{10,... | collective-permute-start | bytes 786440 | tf_op jit(solution)/shard_map/ppermute | solution.py:692
  107.6 1.0 collective-permute-done.36.refs_5_
  108.6 1.4 %collective-permute-start.31 = (bf16[256,512]{1,0:T(8,128)(2,1)S(1)}, bf16[256,512]{1,0:T(8,128)(2,1)S(1)}, u32[]{:S(2)}, u32[]{:S(2)}) collective-permute-start(bf16[256,512]{1,0:T(8,128)(2,1)S(1)} %get-tuple-element.85), channel_id=1, source_target_pairs={{0,3},{1,0},{2,1},{3,2},{4,7},{5,4},{6,5},{7,6},{8,11},{9,8},{10,9... | collective-permute-start | bytes 786440 | tf_op jit(solution)/shard_map/ppermute | solution.py:692
  110.0 3.9 %collective-permute-done.38.refs_7_ = bf16[256,512]{1,0:T(8,128)(2,1)S(1)} collective-permute-done((bf16[256,512]{1,0:T(8,128)(2,1)S(1)}, bf16[256,512]{1,0:T(8,128)(2,1)S(1)}, u32[]{:S(2)}, u32[]{:S(2)}) %collective-permute-start.38) | collective-permute-done | bytes 262176 | tf_op jit(solution)/shard_map/ppermute | solution.py:692
  114.1 1.4 %collective-permute-start.39 = (bf16[256,512]{1,0:T(8,128)(2,1)S(1)}, bf16[256,512]{1,0:T(8,128)(2,1)S(1)}, u32[]{:S(2)}, u32[]{:S(2)}) collective-permute-start(bf16[256,512]{1,0:T(8,128)(2,1)S(1)} %get-tuple-element.93), channel_id=1, source_target_pairs={{0,24},{8,0},{16,8},{24,16},{1,25},{9,1},{17,9},{25,17},{2,26},{10... | collective-permute-start | bytes 786440 | tf_op jit(solution)/shard_map/ppermute | solution.py:692
  116.4 2.9 %collective-permute-done.30.refs_2_ = bf16[256,512]{1,0:T(8,128)(2,1)S(1)} collective-permute-done((bf16[256,512]{1,0:T(8,128)(2,1)S(1)}, bf16[256,512]{1,0:T(8,128)(2,1)S(1)}, u32[]{:S(2)}, u32[]{:S(2)}) %collective-permute-start.30) | collective-permute-done | bytes 262176 | tf_op jit(solution)/shard_map/ppermute | solution.py:692
  119.3 2.6 %collective-permute-done.31.refs_3_ = bf16[256,512]{1,0:T(8,128)(2,1)S(1)} collective-permute-done((bf16[256,512]{1,0:T(8,128)(2,1)S(1)}, bf16[256,512]{1,0:T(8,128)(2,1)S(1)}, u32[]{:S(2)}, u32[]{:S(2)}) %collective-permute-start.31) | collective-permute-done | bytes 262176 | tf_op jit(solution)/shard_map/ppermute | solution.py:692
  122.1 1.2 collective-permute-start.32
  123.3 1.1 collective-permute-done.40.down_ref
  124.4 2.4 %finish.1 = (bf16[256,2048]{1,0:T(8,128)(2,1)}, f32[256,128]{1,0:T(8,128)S(1)}) custom-call(s32[4]{0:T(128)S(1)} %pad_add_fusion.place, bf16[272,512]{1,0:T(8,128)(2,1)S(1)} %get-tuple-element.86.p0, bf16[272,512]{1,0:T(8,128)(2,1)S(1)} %collective-permute-done.26.refs_12_.p1, bf16[272,512]{1,0:T(8,128)(2,1)S(1)} %collective-permute-done.27.refs_13_.p2, ...), custom_call_target="tpu_custom_call" | custom-call | flops 1572864 | bytes 3145728 | tf_op jit(solution)/shard_map/finish/pallas_call | solution.py:654
  126.8 4.9 %collective-permute-done.32.far_ref = bf16[256,512]{1,0:T(8,128)(2,1)S(1)} collective-permute-done((bf16[256,512]{1,0:T(8,128)(2,1)S(1)}, bf16[256,512]{1,0:T(8,128)(2,1)S(1)}, u32[]{:S(2)}, u32[]{:S(2)}) %collective-permute-start.32) | collective-permute-done | bytes 262176 | tf_op jit(solution)/shard_map/ppermute | solution.py:692
  131.6 1.4 %finish_far.1 = bf16[256,2048]{1,0:T(8,128)(2,1)} custom-call(s32[4]{0:T(128)S(1)} %pad_add_fusion.place, bf16[256,512]{1,0:T(8,128)(2,1)S(1)} %collective-permute-done.32.far_ref, f32[256,128]{1,0:T(8,128)S(1)} %get-tuple-element.95.scale_ref, bf16[256,2048]{1,0:T(8,128)(2,1)S(1)} %copy-done.3, ...), custom_call_target="tpu_custom_call", output_to_operand_aliasing={{}: (4, {})} | custom-call | flops 524288 | bytes 1048576 | tf_op jit(solution)/shard_map/finish_far/pallas_call | solution.py:675
  (82 shorter events, 14.4 us)
Async XLA Ops:
  0.0 19.8 %copy-start.10 = (f32[256,16]{0,1:T(8,128)S(1)}, f32[256,16]{0,1:T(8,128)}, u32[]{:S(2)}) copy-start(f32[256,16]{0,1:T(8,128)} %param.15) | copy-start | bytes 49156
  0.0 19.8 %copy-start.13 = (f32[16]{0:T(128)S(1)}, f32[16]{0:T(128)}, u32[]{:S(2)}) copy-start(f32[16]{0:T(128)} %param.17) | copy-start | bytes 196
  0.0 33.3 %collective-permute-start.7 = (bf16[2048,256]{1,0:T(8,128)(2,1)}, bf16[2048,256]{1,0:T(8,128)(2,1)S(1)}, u32[]{:S(2)}, u32[]{:S(2)}) collective-permute-start(bf16[2048,256]{1,0:T(8,128)(2,1)} %refs_2_.7), channel_id=1, source_target_pairs={{0,96},{32,0},{64,32},{96,64},{1,97},{33,1},{65,33},{97,65},{2,98}... | collective-permute-start | bytes 3145736 | tf_op jit(solution)/shard_map/ppermute | solution.py:692
  4.0 29.2 %collective-permute-start.8 = (bf16[2048,256]{1,0:T(8,128)(2,1)}, bf16[2048,256]{1,0:T(8,128)(2,1)S(1)}, u32[]{:S(2)}, u32[]{:S(2)}) collective-permute-start(bf16[2048,256]{1,0:T(8,128)(2,1)} %refs_2_.7), channel_id=1, source_target_pairs={{0,32},{32,64},{64,96},{96,0},{1,33},{33,65},{65,97},{97,1},{2,34}... | collective-permute-start | bytes 3145736 | tf_op jit(solution)/shard_map/ppermute | solution.py:692
  7.6 12.2 %copy-start.5 = (bf16[256,2048]{1,0:T(8,128)(2,1)S(1)}, bf16[256,2048]{1,0:T(8,128)(2,1)}, u32[]{:S(2)}) copy-start(bf16[256,2048]{1,0:T(8,128)(2,1)} %refs_1_.3) | copy-start | bytes 3145732
  7.6 12.2 %copy-start.6 = (bf16[256,128]{1,0:T(8,128)(2,1)S(1)}, bf16[256,128]{1,0:T(8,128)(2,1)}, u32[]{:S(2)}) copy-start(bf16[256,128]{1,0:T(8,128)(2,1)} %read_ref.1) | copy-start | bytes 196612
  7.6 12.2 %copy-start.8 = (bf16[256,128]{1,0:T(8,128)(2,1)S(1)}, bf16[256,128]{1,0:T(8,128)(2,1)}, u32[]{:S(2)}) copy-start(bf16[256,128]{1,0:T(8,128)(2,1)} %refs_2_.4) | copy-start | bytes 196612
  10.2 2.0 %collective-permute-start = (f32[136,1024]{1,0:T(8,128)S(1)}, f32[136,1024]{1,0:T(8,128)S(1)}, u32[]{:S(2)}, u32[]{:S(2)}) collective-permute-start(f32[136,1024]{1,0:T(8,128)S(1)} %get-tuple-element.52), channel_id=1, source_target_pairs={{0,4},{4,0},{1,5},{5,1},{2,6},{6,2},{3,7},{7,3},{8,12},{12,8},{9,1... | collective-permute-start | bytes 1671176 | tf_op jit(solution)/shard_map/ppermute | solution.py:696
  13.1 9.9 %collective-permute-start.1 = (bf16[144,256]{1,0:T(8,128)(2,1)S(1)}, bf16[144,256]{1,0:T(8,128)(2,1)S(1)}, u32[]{:S(2)}, u32[]{:S(2)}) collective-permute-start(bf16[144,256]{1,0:T(8,128)(2,1)S(1)} %get-tuple-element.54), channel_id=1, source_target_pairs={{0,8},{8,16},{16,24},{24,0},{1,9},{9,17},{17,25},{25,1},{2,10},{10... | collective-permute-start | bytes 221192 | tf_op jit(solution)/shard_map/ppermute | solution.py:692
  14.7 8.3 %collective-permute-start.2 = (bf16[144,256]{1,0:T(8,128)(2,1)S(1)}, bf16[144,256]{1,0:T(8,128)(2,1)S(1)}, u32[]{:S(2)}, u32[]{:S(2)}) collective-permute-start(bf16[144,256]{1,0:T(8,128)(2,1)S(1)} %get-tuple-element.55), channel_id=1, source_target_pairs={{0,16},{8,24},{16,0},{24,8},{1,17},{9,25},{17,1},{25,9},{2,18},{10... | collective-permute-start | bytes 221192 | tf_op jit(solution)/shard_map/ppermute | solution.py:692
  17.6 5.4 %collective-permute-start.3 = (bf16[144,256]{1,0:T(8,128)(2,1)S(1)}, bf16[144,256]{1,0:T(8,128)(2,1)S(1)}, u32[]{:S(2)}, u32[]{:S(2)}) collective-permute-start(bf16[144,256]{1,0:T(8,128)(2,1)S(1)} %get-tuple-element.56), channel_id=1, source_target_pairs={{0,24},{8,0},{16,8},{24,16},{1,25},{9,1},{17,9},{25,17},{2,26},{10... | collective-permute-start | bytes 221192 | tf_op jit(solution)/shard_map/ppermute | solution.py:692
  19.8 13.4 %copy-start = (bf16[2048,256]{1,0:T(8,128)(2,1)S(1)}, bf16[2048,256]{1,0:T(8,128)(2,1)}, u32[]{:S(2)}) copy-start(bf16[2048,256]{1,0:T(8,128)(2,1)} %refs_2_.7) | copy-start | bytes 3145732
  23.9 9.4 %collective-permute-start.4 = (bf16[144,256]{1,0:T(8,128)(2,1)S(1)}, bf16[144,256]{1,0:T(8,128)(2,1)S(1)}, u32[]{:S(2)}, u32[]{:S(2)}) collective-permute-start(bf16[144,256]{1,0:T(8,128)(2,1)S(1)} %get-tuple-element.58.p0), channel_id=1, source_target_pairs={{0,32},{32,64},{64,96},{96,0},{1,33},{33,65},{65,97},{97,1},{2,34}... | collective-permute-start | bytes 221192 | tf_op jit(solution)/shard_map/ppermute | solution.py:692
  24.0 9.3 %collective-permute-start.5 = (bf16[144,256]{1,0:T(8,128)(2,1)S(1)}, bf16[144,256]{1,0:T(8,128)(2,1)S(1)}, u32[]{:S(2)}, u32[]{:S(2)}) collective-permute-start(bf16[144,256]{1,0:T(8,128)(2,1)S(1)} %get-tuple-element.58.p0), channel_id=1, source_target_pairs={{0,64},{32,96},{64,0},{96,32},{1,65},{33,97},{65,1},{97,33},{2,66}... | collective-permute-start | bytes 221192 | tf_op jit(solution)/shard_map/ppermute | solution.py:692
  28.6 4.6 %collective-permute-start.6 = (bf16[144,256]{1,0:T(8,128)(2,1)S(1)}, bf16[144,256]{1,0:T(8,128)(2,1)S(1)}, u32[]{:S(2)}, u32[]{:S(2)}) collective-permute-start(bf16[144,256]{1,0:T(8,128)(2,1)S(1)} %get-tuple-element.58.p0), channel_id=1, source_target_pairs={{0,96},{32,0},{64,32},{96,64},{1,97},{33,1},{65,33},{97,65},{2,98}... | collective-permute-start | bytes 221192 | tf_op jit(solution)/shard_map/ppermute | solution.py:692
  33.2 5.7 %collective-permute-start.12 = (bf16[2048,256]{1,0:T(8,128)(2,1)S(1)}, bf16[2048,256]{1,0:T(8,128)(2,1)S(1)}, u32[]{:S(2)}, u32[]{:S(2)}) collective-permute-start(bf16[2048,256]{1,0:T(8,128)(2,1)S(1)} %copy-done), channel_id=1, source_target_pairs={{0,4},{4,0},{1,5},{5,1},{2,6},{6,2},{3,7},{7,3},{8,12},{12,8},{9,1... | collective-permute-start | bytes 3145736 | tf_op jit(solution)/shard_map/ppermute | solution.py:696
  33.3 11.2 %collective-permute-start.13 = (bf16[2048,256]{1,0:T(8,128)(2,1)S(1)}, bf16[2048,256]{1,0:T(8,128)(2,1)S(1)}, u32[]{:S(2)}, u32[]{:S(2)}) collective-permute-start(bf16[2048,256]{1,0:T(8,128)(2,1)S(1)} %collective-permute-done.7.refs_0_.refs_1_.refs_3_), channel_id=1, source_target_pairs={{0,4},{4,0},{1,5},{5,1},{2,6},{6,2},{3,7},{7,3},{8,12},{12,8},{9,1... | collective-permute-start | bytes 3145736 | tf_op jit(solution)/shard_map/ppermute | solution.py:696
  33.9 10.6 %collective-permute-start.14 = (bf16[2048,256]{1,0:T(8,128)(2,1)S(1)}, bf16[2048,256]{1,0:T(8,128)(2,1)S(1)}, u32[]{:S(2)}, u32[]{:S(2)}) collective-permute-start(bf16[2048,256]{1,0:T(8,128)(2,1)S(1)} %collective-permute-done.8.refs_1_.refs_2_.refs_4_), channel_id=1, source_target_pairs={{0,4},{4,0},{1,5},{5,1},{2,6},{6,2},{3,7},{7,3},{8,12},{12,8},{9,1... | collective-permute-start | bytes 3145736 | tf_op jit(solution)/shard_map/ppermute | solution.py:696
  34.6 6.0 %collective-permute-start.10 = (bf16[128,256]{1,0:T(8,128)(2,1)S(1)}, bf16[128,256]{1,0:T(8,128)(2,1)S(1)}, u32[]{:S(2)}, u32[]{:S(2)}) collective-permute-start(bf16[128,256]{1,0:T(8,128)(2,1)S(1)} %get-tuple-element.62), channel_id=1, source_target_pairs={{0,16},{8,24},{16,0},{24,8},{1,17},{9,25},{17,1},{25,9},{2,18},{10... | collective-permute-start | bytes 196616 | tf_op jit(solution)/shard_map/ppermute | solution.py:692
  37.9 4.5 %collective-permute-start.11 = (bf16[128,256]{1,0:T(8,128)(2,1)S(1)}, bf16[128,256]{1,0:T(8,128)(2,1)S(1)}, u32[]{:S(2)}, u32[]{:S(2)}) collective-permute-start(bf16[128,256]{1,0:T(8,128)(2,1)S(1)} %get-tuple-element.63), channel_id=1, source_target_pairs={{0,24},{8,0},{16,8},{24,16},{1,25},{9,1},{17,9},{25,17},{2,26},{10... | collective-permute-start | bytes 196616 | tf_op jit(solution)/shard_map/ppermute | solution.py:692
  39.0 5.5 %collective-permute-start.9 = (bf16[128,256]{1,0:T(8,128)(2,1)S(1)}, bf16[128,256]{1,0:T(8,128)(2,1)S(1)}, u32[]{:S(2)}, u32[]{:S(2)}) collective-permute-start(bf16[128,256]{1,0:T(8,128)(2,1)S(1)} %get-tuple-element.61), channel_id=1, source_target_pairs={{0,8},{8,16},{16,24},{24,0},{1,9},{9,17},{17,25},{25,1},{2,10},{10... | collective-permute-start | bytes 196616 | tf_op jit(solution)/shard_map/ppermute | solution.py:692
  40.7 14.7 %collective-permute-start.21 = (bf16[1024,256]{1,0:T(8,128)(2,1)S(1)}, bf16[1024,256]{1,0:T(8,128)(2,1)S(1)}, u32[]{:S(2)}, u32[]{:S(2)}) collective-permute-start(bf16[1024,256]{1,0:T(8,128)(2,1)S(1)} %slice.8), channel_id=1, source_target_pairs={{0,32},{32,64},{64,96},{96,0},{1,33},{33,65},{65,97},{97,1},{2,34}... | collective-permute-start | bytes 1572872 | tf_op jit(solution)/shard_map/ppermute | solution.py:692
  42.4 13.5 %collective-permute-start.22 = (bf16[1024,256]{1,0:T(8,128)(2,1)S(1)}, bf16[1024,256]{1,0:T(8,128)(2,1)S(1)}, u32[]{:S(2)}, u32[]{:S(2)}) collective-permute-start(bf16[1024,256]{1,0:T(8,128)(2,1)S(1)} %slice.9), channel_id=1, source_target_pairs={{0,96},{32,0},{64,32},{96,64},{1,97},{33,1},{65,33},{97,65},{2,98}... | collective-permute-start | bytes 1572872 | tf_op jit(solution)/shard_map/ppermute | solution.py:692
  45.3 1.6 %collective-permute-start.15 = (bf16[128,1024]{1,0:T(8,128)(2,1)S(1)}, bf16[128,1024]{1,0:T(8,128)(2,1)S(1)}, u32[]{:S(2)}, u32[]{:S(2)}) collective-permute-start(bf16[128,1024]{1,0:T(8,128)(2,1)S(1)} %get-tuple-element.67), channel_id=1, source_target_pairs={{0,4},{4,0},{1,5},{5,1},{2,6},{6,2},{3,7},{7,3},{8,12},{12,8},{9,1... | collective-permute-start | bytes 786440 | tf_op jit(solution)/shard_map/ppermute | solution.py:696
  49.2 15.2 %collective-permute-start.16 = (bf16[128,2048]{1,0:T(8,128)(2,1)S(1)}, bf16[128,2048]{1,0:T(8,128)(2,1)S(1)}, u32[]{:S(2)}, u32[]{:S(2)}) collective-permute-start(bf16[128,2048]{1,0:T(8,128)(2,1)S(1)} %get-tuple-element.69.top_ref), channel_id=1, source_target_pairs={{0,8},{8,16},{16,24},{24,0},{1,9},{9,17},{17,25},{25,1},{2,10},{10... | collective-permute-start | bytes 1572872 | tf_op jit(solution)/shard_map/ppermute | solution.py:692
  50.8 13.7 %collective-permute-start.18 = (bf16[128,2048]{1,0:T(8,128)(2,1)S(1)}, bf16[128,2048]{1,0:T(8,128)(2,1)S(1)}, u32[]{:S(2)}, u32[]{:S(2)}) collective-permute-start(bf16[128,2048]{1,0:T(8,128)(2,1)S(1)} %get-tuple-element.69.top_ref), channel_id=1, source_target_pairs={{0,24},{8,0},{16,8},{24,16},{1,25},{9,1},{17,9},{25,17},{2,26},{10... | collective-permute-start | bytes 1572872 | tf_op jit(solution)/shard_map/ppermute | solution.py:692
  55.9 11.7 %collective-permute-start.23 = (bf16[1024,256]{1,0:T(8,128)(2,1)S(1)}, bf16[1024,256]{1,0:T(8,128)(2,1)S(1)}, u32[]{:S(2)}, u32[]{:S(2)}) collective-permute-start(bf16[1024,256]{1,0:T(8,128)(2,1)S(1)} %collective-permute-done.21.refs_0_.refs_5_), channel_id=1, source_target_pairs={{0,4},{4,0},{1,5},{5,1},{2,6},{6,2},{3,7},{7,3},{8,12},{12,8},{9,1... | collective-permute-start | bytes 1572872 | tf_op jit(solution)/shard_map/ppermute | solution.py:696
  55.9 11.7 %collective-permute-start.24 = (bf16[1024,256]{1,0:T(8,128)(2,1)S(1)}, bf16[1024,256]{1,0:T(8,128)(2,1)S(1)}, u32[]{:S(2)}, u32[]{:S(2)}) collective-permute-start(bf16[1024,256]{1,0:T(8,128)(2,1)S(1)} %collective-permute-done.22.refs_1_.refs_6_), channel_id=1, source_target_pairs={{0,4},{4,0},{1,5},{5,1},{2,6},{6,2},{3,7},{7,3},{8,12},{12,8},{9,1... | collective-permute-start | bytes 1572872 | tf_op jit(solution)/shard_map/ppermute | solution.py:696
  64.5 14.2 %collective-permute-start.19 = (bf16[128,2048]{1,0:T(8,128)(2,1)S(1)}, bf16[128,2048]{1,0:T(8,128)(2,1)S(1)}, u32[]{:S(2)}, u32[]{:S(2)}) collective-permute-start(bf16[128,2048]{1,0:T(8,128)(2,1)S(1)} %get-tuple-element.71.low_ref), channel_id=1, source_target_pairs={{0,24},{8,0},{16,8},{24,16},{1,25},{9,1},{17,9},{25,17},{2,26},{10... | collective-permute-start | bytes 1572872 | tf_op jit(solution)/shard_map/ppermute | solution.py:692
  69.0 9.7 %collective-permute-start.26 = (bf16[272,512]{1,0:T(8,128)(2,1)S(1)}, bf16[272,512]{1,0:T(8,128)(2,1)S(1)}, u32[]{:S(2)}, u32[]{:S(2)}) collective-permute-start(bf16[272,512]{1,0:T(8,128)(2,1)S(1)} %get-tuple-element.77), channel_id=1, source_target_pairs={{0,1},{1,2},{2,3},{3,0},{4,5},{5,6},{6,7},{7,4},{8,9},{9,10},{10,1... | collective-permute-start | bytes 835592 | tf_op jit(solution)/shard_map/ppermute | solution.py:692
  70.6 17.2 %collective-permute-start.25 = (bf16[128,2048]{1,0:T(8,128)(2,1)S(1)}, bf16[128,2048]{1,0:T(8,128)(2,1)S(1)}, u32[]{:S(2)}, u32[]{:S(2)}) collective-permute-start(bf16[128,2048]{1,0:T(8,128)(2,1)S(1)} %get-tuple-element.71.low_ref), channel_id=1, source_target_pairs={{0,8},{8,16},{16,24},{24,0},{1,9},{9,17},{17,25},{25,1},{2,10},{10... | collective-permute-start | bytes 1572872 | tf_op jit(solution)/shard_map/ppermute | solution.py:692
  70.6 14.3 %collective-permute-start.27 = (bf16[272,512]{1,0:T(8,128)(2,1)S(1)}, bf16[272,512]{1,0:T(8,128)(2,1)S(1)}, u32[]{:S(2)}, u32[]{:S(2)}) collective-permute-start(bf16[272,512]{1,0:T(8,128)(2,1)S(1)} %get-tuple-element.78), channel_id=1, source_target_pairs={{0,2},{1,3},{2,0},{3,1},{4,6},{5,7},{6,4},{7,5},{8,10},{9,11},{10,... | collective-permute-start | bytes 835592 | tf_op jit(solution)/shard_map/ppermute | solution.py:692
  71.7 14.8 %collective-permute-start.28 = (bf16[272,512]{1,0:T(8,128)(2,1)S(1)}, bf16[272,512]{1,0:T(8,128)(2,1)S(1)}, u32[]{:S(2)}, u32[]{:S(2)}) collective-permute-start(bf16[272,512]{1,0:T(8,128)(2,1)S(1)} %get-tuple-element.79), channel_id=1, source_target_pairs={{0,3},{1,0},{2,1},{3,2},{4,7},{5,4},{6,5},{7,6},{8,11},{9,8},{10,9... | collective-permute-start | bytes 835592 | tf_op jit(solution)/shard_map/ppermute | solution.py:692
  78.7 19.1 %collective-permute-start.17 = (bf16[128,2048]{1,0:T(8,128)(2,1)S(1)}, bf16[128,2048]{1,0:T(8,128)(2,1)S(1)}, u32[]{:S(2)}, u32[]{:S(2)}) collective-permute-start(bf16[128,2048]{1,0:T(8,128)(2,1)S(1)} %collective-permute-done.16.refs_0_), channel_id=1, source_target_pairs={{0,8},{8,16},{16,24},{24,0},{1,9},{9,17},{17,25},{25,1},{2,10},{10... | collective-permute-start | bytes 1572872 | tf_op jit(solution)/shard_map/ppermute | solution.py:692
  78.7 19.9 %collective-permute-start.20 = (bf16[128,2048]{1,0:T(8,128)(2,1)S(1)}, bf16[128,2048]{1,0:T(8,128)(2,1)S(1)}, u32[]{:S(2)}, u32[]{:S(2)}) collective-permute-start(bf16[128,2048]{1,0:T(8,128)(2,1)S(1)} %collective-permute-done.19.refs_1_), channel_id=1, source_target_pairs={{0,24},{8,0},{16,8},{24,16},{1,25},{9,1},{17,9},{25,17},{2,26},{10... | collective-permute-start | bytes 1572872 | tf_op jit(solution)/shard_map/ppermute | solution.py:692
  84.9 9.9 %collective-permute-start.33 = (bf16[256,512]{1,0:T(8,128)(2,1)S(1)}, bf16[256,512]{1,0:T(8,128)(2,1)S(1)}, u32[]{:S(2)}, u32[]{:S(2)}) collective-permute-start(bf16[256,512]{1,0:T(8,128)(2,1)S(1)} %get-tuple-element.87), channel_id=1, source_target_pairs={{0,1},{1,2},{2,3},{3,0},{4,5},{5,6},{6,7},{7,4},{8,9},{9,10},{10,1... | collective-permute-start | bytes 786440 | tf_op jit(solution)/shard_map/ppermute | solution.py:692
  86.5 16.3 %collective-permute-start.34 = (bf16[256,512]{1,0:T(8,128)(2,1)S(1)}, bf16[256,512]{1,0:T(8,128)(2,1)S(1)}, u32[]{:S(2)}, u32[]{:S(2)}) collective-permute-start(bf16[256,512]{1,0:T(8,128)(2,1)S(1)} %get-tuple-element.88), channel_id=1, source_target_pairs={{0,2},{1,3},{2,0},{3,1},{4,6},{5,7},{6,4},{7,5},{8,10},{9,11},{10,... | collective-permute-start | bytes 786440 | tf_op jit(solution)/shard_map/ppermute | solution.py:692
  87.8 15.8 %collective-permute-start.35 = (bf16[256,512]{1,0:T(8,128)(2,1)S(1)}, bf16[256,512]{1,0:T(8,128)(2,1)S(1)}, u32[]{:S(2)}, u32[]{:S(2)}) collective-permute-start(bf16[256,512]{1,0:T(8,128)(2,1)S(1)} %get-tuple-element.89), channel_id=1, source_target_pairs={{0,3},{1,0},{2,1},{3,2},{4,7},{5,4},{6,5},{7,6},{8,11},{9,8},{10,9... | collective-permute-start | bytes 786440 | tf_op jit(solution)/shard_map/ppermute | solution.py:692
  94.8 13.8 %collective-permute-start.36 = (bf16[256,512]{1,0:T(8,128)(2,1)S(1)}, bf16[256,512]{1,0:T(8,128)(2,1)S(1)}, u32[]{:S(2)}, u32[]{:S(2)}) collective-permute-start(bf16[256,512]{1,0:T(8,128)(2,1)S(1)} %get-tuple-element.90), channel_id=1, source_target_pairs={{0,1},{1,2},{2,3},{3,0},{4,5},{5,6},{6,7},{7,4},{8,9},{9,10},{10,1... | collective-permute-start | bytes 786440 | tf_op jit(solution)/shard_map/ppermute | solution.py:692
  97.8 12.2 %collective-permute-start.37 = (bf16[256,512]{1,0:T(8,128)(2,1)S(1)}, bf16[256,512]{1,0:T(8,128)(2,1)S(1)}, u32[]{:S(2)}, u32[]{:S(2)}) collective-permute-start(bf16[256,512]{1,0:T(8,128)(2,1)S(1)} %get-tuple-element.91), channel_id=1, source_target_pairs={{0,2},{1,3},{2,0},{3,1},{4,6},{5,7},{6,4},{7,5},{8,10},{9,11},{10,... | collective-permute-start | bytes 786440 | tf_op jit(solution)/shard_map/ppermute | solution.py:692
  98.5 15.3 %collective-permute-start.38 = (bf16[256,512]{1,0:T(8,128)(2,1)S(1)}, bf16[256,512]{1,0:T(8,128)(2,1)S(1)}, u32[]{:S(2)}, u32[]{:S(2)}) collective-permute-start(bf16[256,512]{1,0:T(8,128)(2,1)S(1)} %get-tuple-element.92), channel_id=1, source_target_pairs={{0,3},{1,0},{2,1},{3,2},{4,7},{5,4},{6,5},{7,6},{8,11},{9,8},{10,9... | collective-permute-start | bytes 786440 | tf_op jit(solution)/shard_map/ppermute | solution.py:692
  102.8 21.6 %copy-start.3 = (bf16[256,2048]{1,0:T(8,128)(2,1)S(1)}, bf16[256,2048]{1,0:T(8,128)(2,1)}, u32[]{:S(2)}) copy-start(bf16[256,2048]{1,0:T(8,128)(2,1)} %residual_ref.3) | copy-start | bytes 3145732
  102.9 13.5 %collective-permute-start.29 = (bf16[256,512]{1,0:T(8,128)(2,1)S(1)}, bf16[256,512]{1,0:T(8,128)(2,1)S(1)}, u32[]{:S(2)}, u32[]{:S(2)}) collective-permute-start(bf16[256,512]{1,0:T(8,128)(2,1)S(1)} %get-tuple-element.83), channel_id=1, source_target_pairs={{0,1},{1,2},{2,3},{3,0},{4,5},{5,6},{6,7},{7,4},{8,9},{9,10},{10,1... | collective-permute-start | bytes 786440 | tf_op jit(solution)/shard_map/ppermute | solution.py:692
  103.6 15.7 %collective-permute-start.30 = (bf16[256,512]{1,0:T(8,128)(2,1)S(1)}, bf16[256,512]{1,0:T(8,128)(2,1)S(1)}, u32[]{:S(2)}, u32[]{:S(2)}) collective-permute-start(bf16[256,512]{1,0:T(8,128)(2,1)S(1)} %get-tuple-element.84), channel_id=1, source_target_pairs={{0,2},{1,3},{2,0},{3,1},{4,6},{5,7},{6,4},{7,5},{8,10},{9,11},{10,... | collective-permute-start | bytes 786440 | tf_op jit(solution)/shard_map/ppermute | solution.py:692
  108.6 13.3 %collective-permute-start.31 = (bf16[256,512]{1,0:T(8,128)(2,1)S(1)}, bf16[256,512]{1,0:T(8,128)(2,1)S(1)}, u32[]{:S(2)}, u32[]{:S(2)}) collective-permute-start(bf16[256,512]{1,0:T(8,128)(2,1)S(1)} %get-tuple-element.85), channel_id=1, source_target_pairs={{0,3},{1,0},{2,1},{3,2},{4,7},{5,4},{6,5},{7,6},{8,11},{9,8},{10,9... | collective-permute-start | bytes 786440 | tf_op jit(solution)/shard_map/ppermute | solution.py:692
  114.1 9.2 %collective-permute-start.39 = (bf16[256,512]{1,0:T(8,128)(2,1)S(1)}, bf16[256,512]{1,0:T(8,128)(2,1)S(1)}, u32[]{:S(2)}, u32[]{:S(2)}) collective-permute-start(bf16[256,512]{1,0:T(8,128)(2,1)S(1)} %get-tuple-element.93), channel_id=1, source_target_pairs={{0,24},{8,0},{16,8},{24,16},{1,25},{9,1},{17,9},{25,17},{2,26},{10... | collective-permute-start | bytes 786440 | tf_op jit(solution)/shard_map/ppermute | solution.py:692
  115.5 8.9 %collective-permute-start.40 = (bf16[256,512]{1,0:T(8,128)(2,1)S(1)}, bf16[256,512]{1,0:T(8,128)(2,1)S(1)}, u32[]{:S(2)}, u32[]{:S(2)}) collective-permute-start(bf16[256,512]{1,0:T(8,128)(2,1)S(1)} %get-tuple-element.94), channel_id=1, source_target_pairs={{0,8},{8,16},{16,24},{24,0},{1,9},{9,17},{17,25},{25,1},{2,10},{10... | collective-permute-start | bytes 786440 | tf_op jit(solution)/shard_map/ppermute | solution.py:692
  122.1 9.6 %collective-permute-start.32 = (bf16[256,512]{1,0:T(8,128)(2,1)S(1)}, bf16[256,512]{1,0:T(8,128)(2,1)S(1)}, u32[]{:S(2)}, u32[]{:S(2)}) collective-permute-start(bf16[256,512]{1,0:T(8,128)(2,1)S(1)} %far_sums.1._), channel_id=1, source_target_pairs={{0,16},{8,24},{16,0},{24,8},{1,17},{9,25},{17,1},{25,9},{2,18},{10... | collective-permute-start | bytes 786440 | tf_op jit(solution)/shard_map/ppermute | solution.py:692
  (7 other events, 34.0 us)

commit v4 on v3

--- a/solution.py
+++ b/solution.py
@@ -21,7 +21,6 @@
 F32 = jnp.float32
 BF16 = jnp.bfloat16
 HIGHEST = lax.Precision.HIGHEST
-HBM = pl.BlockSpec(memory_space=pltpu.HBM)
 VMEM = pl.BlockSpec(memory_space=pltpu.VMEM)
 SMEM = pl.BlockSpec(memory_space=pltpu.SMEM)
 
@@ -45,16 +44,16 @@
     )
 
 
-def cumulate(step, rate):
+def cumulate(packed):
     ones = jnp.where(lower(ROWS), 1.0, 0.0).astype(F32)
-    column = jnp.broadcast_to(rate, (8, HEADS)).T[:, 0:1]
-    return lax.dot_general(
-        -step * column,
+    cumulative = lax.dot_general(
+        packed[HEADS:],
         ones,
         (((1,), (1,)), ((), ())),
         precision=HIGHEST,
         preferred_element_type=F32,
     )
+    return packed[:HEADS], cumulative
 
 
 def three(row):
@@ -79,29 +78,9 @@
     return block[0:1] + block[1:2] + block[2:3]
 
 
-def fetch(sources, targets, sems):
-    copies = [
-        pltpu.make_async_copy(source, target, sems.at[i])
-        for i, (source, target) in enumerate(zip(sources, targets))
-    ]
-    for copy in copies:
-        copy.start()
-    for copy in copies:
-        copy.wait()
-    return targets
-
-
-def room(sources):
-    targets = [pltpu.VMEM(source.shape, source.dtype) for source in sources]
-    return targets + [pltpu.SemaphoreType.DMA((len(sources),))]
-
-
-def state_kernel(place, *refs):
-    keep_ref, send_ref, state, logs = refs[4:8]
-    value_ref, write_ref, step_ref, rate_ref = fetch(refs[0:4], refs[8:12], refs[12])
+def state_kernel(place, value_ref, write_ref, packed_ref, keep_ref, send_ref, state, logs):
     core = place[0]
-    step = step_ref[...]
-    across = cumulate(step, rate_ref[...])
+    step, across = cumulate(packed_ref[...])
     to_end = (jnp.exp(across[:, ROWS - 1 : ROWS] - across) * step).T
     last = across.T[ROWS - 1 : ROWS]
     write = write_ref[...].T
@@ -122,28 +101,24 @@
     return pl.BlockSpec(shape, lambda i, place: (0,) * len(shape))
 
 
-def local_state(place, values, writes, steps, rate):
+def local_state(place, *sources):
     shape = (WIDTH + 8, SPLIT)
-    sources = (values, writes, steps, rate)
     return pl.pallas_call(
         state_kernel,
         out_shape=[jax.ShapeDtypeStruct(shape, F32)] * 2,
-        in_specs=[SMEM] + [HBM] * 4,
+        in_specs=[SMEM] + [VMEM] * 3,
         out_specs=[VMEM] * 2,
-        scratch_shapes=[pltpu.VMEM((WIDTH, LANES), F32), pltpu.VMEM((8, LANES), F32)]
-        + room(sources),
+        scratch_shapes=[pltpu.VMEM((WIDTH, LANES), F32), pltpu.VMEM((8, LANES), F32)],
         compiler_params=params(),
         cost_estimate=cost(2 * WIDTH * ROWS * LANES, 3 * 2**20),
         name="local_state",
     )(place, *sources)
 
 
-def plain_kernel(*refs):
-    plain_ref, scale_ref = refs[8:10]
-    targets = fetch(refs[0:7], refs[10:17], refs[17])
-    value_ref, gate_ref, write_ref, read_ref, step_ref, rate_ref, skip_ref = targets
-    step = step_ref[...]
-    across = cumulate(step, rate_ref[...])
+def plain_kernel(
+    value_ref, gate_ref, write_ref, read_ref, packed_ref, skip_ref, _, plain_ref, scale_ref
+):
+    step, across = cumulate(packed_ref[...])
     cumulative = across.T
     decay = jnp.exp(cumulative)
     scores = lax.dot_general(
@@ -163,21 +138,19 @@
         scale_ref[:, at] = decay[:, head : head + 1] * gate
 
 
-def plain_part(values, gates, writes, reads, steps, rate, skip, after):
+def plain_part(*sources):
     shape = jax.ShapeDtypeStruct((ROWS, LANES), F32)
-    sources = (values, gates, writes, reads, steps, rate, skip)
     return pl.pallas_call(
         plain_kernel,
         out_shape=(shape, shape),
-        in_specs=[HBM] * 7 + [ANY],
+        in_specs=[VMEM] * 6 + [ANY],
         out_specs=(VMEM, VMEM),
-        scratch_shapes=room(sources),
         compiler_params=params(),
         cost_estimate=cost(
             2 * ROWS * ROWS * LANES, 7 * 2**20, HEADS * ROWS * ROWS + ROWS * LANES
         ),
         name="plain_part",
-    )(*sources, after)
+    )(*sources)
 
 
 def turn_kernel(place, prior_ref, _, out_ref):
@@ -379,63 +352,38 @@
 
 
 def gated_kernel(place, mine_ref, other_ref, read_ref, plain_ref, scale_ref, gain_ref, *refs):
-    top_ref, low_ref, stat_ref, acc = refs[-4:]
-    step = pl.program_id(0)
-    mine = place[0] == step // 2
-    entering = jnp.where(mine, mine_ref[...], other_ref[...])
-    carried = jnp.dot(read_ref[...], entering, preferred_element_type=F32)
-    gated = plain_ref[...] + scale_ref[...] * carried
-    result = (gated * gain_ref[...]).astype(BF16)
-    top_ref[...] = result[:HALF]
-    low_ref[...] = result[HALF:]
-    square = gated * gated
-    part = square[:, 0:128]
-    for at in range(128, square.shape[1], 128):
-        part = part + square[:, at : at + 128]
-
-    @pl.when(step == 0)
-    def _():
-        acc[...] = part
-
-    @pl.when(step > 0)
-    def _():
-        acc[...] += part
-
-    @pl.when(step == pl.num_programs(0) - 1)
-    def _():
-        row = jnp.sum(acc[...].T, axis=0, keepdims=True)
-        stat_ref[...] = jnp.zeros_like(stat_ref)
-        stat_ref[:, 0:ROWS] = stack_rows(three(row), 16).astype(BF16)
+    top_ref, low_ref, stat_ref = refs[-3:]
+    read = read_ref[...]
+    width = 256
+    part = None
+    for start in range(0, LANES, width):
+        at = slice(start, start + width)
+        source = slice(start % SPLIT, start % SPLIT + width)
+        mine = place[0] == start // SPLIT
+        entering = jnp.where(mine, mine_ref[:, source], other_ref[:, source])
+        carried = jnp.dot(read, entering, preferred_element_type=F32)
+        gated = plain_ref[:, at] + scale_ref[:, at] * carried
+        result = (gated * gain_ref[:, at]).astype(BF16)
+        top_ref[:, at] = result[:HALF]
+        low_ref[:, at] = result[HALF:]
+        square = gated * gated
+        square = square[:, :128] + square[:, 128:]
+        part = square if part is None else part + square
+    row = jnp.sum(part.T, axis=0, keepdims=True)
+    stat_ref[...] = jnp.zeros_like(stat_ref)
+    stat_ref[:, 0:ROWS] = stack_rows(three(row), 16).astype(BF16)
 
 
 def gated_part(place, mine, other, reads, plain, scale, gain, after):
-    steps = 4
-    width = LANES // steps
-    half = pl.BlockSpec((HALF, width), lambda i, place: (0, i))
-    wide = pl.BlockSpec((ROWS, width), lambda i, place: (0, i))
-    state = pl.BlockSpec((WIDTH, width), lambda i, place: (0, lax.rem(i, 2)))
     return pl.pallas_call(
         gated_kernel,
-        grid_spec=pltpu.PrefetchScalarGridSpec(
-            num_scalar_prefetch=1,
-            grid=(steps,),
-            in_specs=[
-                state,
-                state,
-                whole((ROWS, WIDTH)),
-                wide,
-                wide,
-                pl.BlockSpec((1, width), lambda i, place: (0, i)),
-            ]
-            + [ANY] * len(after),
-            out_specs=[half, half, whole((16, PIECE))],
-            scratch_shapes=[pltpu.VMEM((ROWS, 128), F32)],
-        ),
         out_shape=(
             jax.ShapeDtypeStruct((HALF, LANES), BF16),
             jax.ShapeDtypeStruct((HALF, LANES), BF16),
             jax.ShapeDtypeStruct((16, PIECE), BF16),
         ),
+        in_specs=[SMEM] + [VMEM] * 6 + [ANY] * len(after),
+        out_specs=[VMEM] * 3,
         compiler_params=params(),
         cost_estimate=cost(2 * ROWS * WIDTH * LANES, 6 * 2**20),
         name="gated_part",
@@ -502,6 +450,24 @@
     return list(pieces)
 
 
+def hold_kernel(value_ref, out_ref):
+    out_ref[...] = value_ref[...]
+
+
+def hold(value, micros):
+    return pl.pallas_call(
+        hold_kernel,
+        out_shape=jax.ShapeDtypeStruct(value.shape, value.dtype),
+        in_specs=[VMEM],
+        out_specs=VMEM,
+        compiler_params=params(),
+        cost_estimate=pl.CostEstimate(
+            flops=micros * 10**9, bytes_accessed=2**20, transcendentals=0
+        ),
+        name="hold",
+    )(value)
+
+
 def near_kernel(top_ref, low_ref, *refs):
     out = refs[-1]
     for side in range(2):
@@ -517,7 +483,7 @@
         out_specs=VMEM,
         out_shape=jax.ShapeDtypeStruct((3, 2, ROWS, 256), BF16),
         compiler_params=params(24),
-        cost_estimate=cost(2 * ROWS * LANES * 3 * PIECE, 8 * 2**20),
+        cost_estimate=cost(2 * ROWS * LANES * 3 * PIECE, 2 * 4 * 2**20),
         name="project_near",
     )(top, low, *weights, *after)
 
@@ -542,7 +508,7 @@
         out_shape=[jax.ShapeDtypeStruct((ROWS + 16, PIECE), BF16)] * 4,
         scratch_shapes=[pltpu.VMEM((4, 2, ROWS, 256), BF16)],
         compiler_params=params(24),
-        cost_estimate=cost(2 * ROWS * LANES * PIECE, 4 * 2**20),
+        cost_estimate=cost(2 * ROWS * LANES * PIECE, 2 * 2 * 2**20),
         name="project_far",
     )(place, top, low, *weights, near, stats)
     return list(pieces)
@@ -722,16 +688,16 @@
     residual,
 ):
     place = jnp.stack([lax.axis_index(name) for name in ("core", "x", "y", "z")]).astype(jnp.int32)
-    rate = decay_rate[None, :]
 
     steps = step_size.T
+    packed = jnp.concatenate([steps, -steps * decay_rate[:, None]], axis=0)
     from_below, from_above = shift(out_weight, "z", 1), shift(out_weight, "z", -1)
-    keep, send = local_state(place, head_values, write_keys, steps, rate)
+    keep, send = local_state(place, head_values, write_keys, packed)
     got = swap(send)
     weight = [out_weight, from_above, from_below]
     swapped = [swap(out_weight)]
     chips = chip_total(place, keep, got, [])
-    sources = (head_values, gate_values, write_keys, read_keys, steps, rate, skip_weight[None, :])
+    sources = (head_values, gate_values, write_keys, read_keys, packed, skip_weight[None, :])
     plain, scale = plain_part(*sources, chips[0])
     prior = turned_prior(place, prior_state, chips[0])
     row, before = row_total(place, scatter(chips, "y"), (prior, plain,))
@@ -747,7 +713,8 @@
     other = swap(other)
     gain = norm_gain[None, :]
     top, low, stats = gated_part(place, mine, other, read_keys, plain, scale, gain, [])
-    top_below, top_above = shift(top, "y", 1), shift(top, "y", -1)
+    top_go = top
+    top_below, top_above = shift(top_go, "y", 1), shift(top_go, "y", -1)
     near = project_near(top, low, weight + swapped, [])
     far_swapped = [swap(part) for part in later(far_weight, [near])]
     weights = weight + far_weight + swapped + far_swapped
@@ -758,6 +725,7 @@
     own = scatter(own)
     first = project(place, [top_below, top_above], weights, None, [], False)
     go = (top_below, low_above)
+    go = later(go, (top_above, low_below, first[0]))
     top_far, low_far = shift(go[0], "y", 1), shift(go[1], "y", -1)
     first = scatter(first)
     second = project(place, [low_below, low_above], weights, None, own[1:] + first[:1], False)

time: 133 us -> 130 us (0.977)
  waiting for transfers between devices: 44 us -> 40.9 us
  Pallas kernels: 28.4 us -> 26.8 us
  other arithmetic: 0.08 us -> 1.6 us
    ppermute x34, waiting for transfers between devices: 40.5 us -> 39 us  [shift(): return lax.ppermute(value, axis, [(i, (i + by) % 4) for i in range(4)])]
    ppermute x7, waiting for transfers between devices: 3.48 us -> 1.96 us  [swap(): return lax.ppermute(value, 'core', [(0, 1), (1, 0)])]
    unnamed x28 -> x20, local copies, waits for them, and re-layouts: 3.48 us -> 3.32 us
  transfers between devices with their start and end apart: 41 -> 41, of which waited for: 18 -> 17; matrix products, arithmetic and copies ran while one was open for 0% -> 1% of each run, Pallas kernels for 20% -> 19%
where the time goes in v4:
time: 130 us
  starting transfers between devices  56.6 us (44%)
  waiting for transfers between devices  40.9 us (31%)
  Pallas kernels  26.8 us (21%)
  local copies, waits for them, and re-layouts  3.39 us (3%)
  other arithmetic  1.6 us (1%)
    ppermute x34, starting transfers between devices, shift(): return lax.ppermute(value, axis, [(i, (i + by) % 4) for i in range(4)])  55.4 us
    ppermute x34, waiting for transfers between devices, shift(): return lax.ppermute(value, axis, [(i, (i + by) % 4) for i in range(4)])  39 us
    pallas_call x3, Pallas kernels, project(): pl.pallas_call(functools.partial(project_kernel, tall, count, count - 3,...  8.94 us
    unnamed x20, local copies, waits for them, and re-layouts  3.32 us
    pallas_call x1, Pallas kernels, plain_part(): pl.pallas_call(plain_kernel, out_shape=(shape, shape), in_specs=[VMEM] *...  2.8 us
  transfers between devices with their start and end apart: 41, of which 17 were waited for; matrix products, arithmetic and copies ran while one was open for 1% of the time, Pallas kernels for 19%

profile of v4, /device:TPU:2, one launch (start us, length us, event | category | flops | bytes accessed | tf_op | source)
XLA Modules:
  0.0 129.6 jit_solution(10710290802320037480)
XLA Ops:
  0.0 1.9 %collective-permute-start.8 = (bf16[2048,256]{1,0:T(8,128)(2,1)}, bf16[2048,256]{1,0:T(8,128)(2,1)S(1)}, u32[]{:S(2)}, u32[]{:S(2)}) collective-permute-start(bf16[2048,256]{1,0:T(8,128)(2,1)} %refs_2_.5), channel_id=1, source_target_pairs={{0,32},{32,64},{64,96},{96,0},{1,33},{33,65},{65,97},{97,1},{2,34}... | collective-permute-start | bytes 3145736 | tf_op jit(solution)/shard_map/ppermute | solution.py:658
  1.9 2.2 %collective-permute-start.7 = (bf16[2048,256]{1,0:T(8,128)(2,1)}, bf16[2048,256]{1,0:T(8,128)(2,1)S(1)}, u32[]{:S(2)}, u32[]{:S(2)}) collective-permute-start(bf16[2048,256]{1,0:T(8,128)(2,1)} %refs_2_.5), channel_id=1, source_target_pairs={{0,96},{32,0},{64,32},{96,64},{1,97},{33,1},{65,33},{97,65},{2,98}... | collective-permute-start | bytes 3145736 | tf_op jit(solution)/shard_map/ppermute | solution.py:658
  7.8 2.3 %local_state.1 = (f32[136,1024]{1,0:T(8,128)S(1)}, f32[136,1024]{1,0:T(8,128)S(1)}) custom-call(s32[4]{0:T(128)S(1)} %pad_add_fusion.place, bf16[256,2048]{1,0:T(8,128)(2,1)S(1)} %copy-done.1, bf16[256,128]{1,0:T(8,128)(2,1)S(1)} %copy-done.7, f32[32,256]{1,0:T(8,128)S(1)} %pad_maximum_fusion.packed_ref), custom_call_target="tpu_custom_call" | custom-call | flops 134217728 | bytes 3145728 | tf_op jit(solution)/shard_map/local_state/pallas_call | solution.py:106
  10.2 1.9 %collective-permute-done.got_ref = f32[136,1024]{1,0:T(8,128)S(1)} collective-permute-done((f32[136,1024]{1,0:T(8,128)S(1)}, f32[136,1024]{1,0:T(8,128)S(1)}, u32[]{:S(2)}, u32[]{:S(2)}) %collective-permute-start) | collective-permute-done | bytes 557088 | tf_op jit(solution)/shard_map/ppermute | solution.py:662
  13.0 1.6 %collective-permute-start.1 = (bf16[144,256]{1,0:T(8,128)(2,1)S(1)}, bf16[144,256]{1,0:T(8,128)(2,1)S(1)}, u32[]{:S(2)}, u32[]{:S(2)}) collective-permute-start(bf16[144,256]{1,0:T(8,128)(2,1)S(1)} %get-tuple-element.56), channel_id=1, source_target_pairs={{0,8},{8,16},{16,24},{24,0},{1,9},{9,17},{17,25},{25,1},{2,10},{10... | collective-permute-start | bytes 221192 | tf_op jit(solution)/shard_map/ppermute | solution.py:658
  14.7 2.9 %collective-permute-start.2 = (bf16[144,256]{1,0:T(8,128)(2,1)S(1)}, bf16[144,256]{1,0:T(8,128)(2,1)S(1)}, u32[]{:S(2)}, u32[]{:S(2)}) collective-permute-start(bf16[144,256]{1,0:T(8,128)(2,1)S(1)} %get-tuple-element.57), channel_id=1, source_target_pairs={{0,16},{8,24},{16,0},{24,8},{1,17},{9,25},{17,1},{25,9},{2,18},{10... | collective-permute-start | bytes 221192 | tf_op jit(solution)/shard_map/ppermute | solution.py:658
  17.6 1.3 %collective-permute-start.3 = (bf16[144,256]{1,0:T(8,128)(2,1)S(1)}, bf16[144,256]{1,0:T(8,128)(2,1)S(1)}, u32[]{:S(2)}, u32[]{:S(2)}) collective-permute-start(bf16[144,256]{1,0:T(8,128)(2,1)S(1)} %get-tuple-element.58), channel_id=1, source_target_pairs={{0,24},{8,0},{16,8},{24,16},{1,25},{9,1},{17,9},{25,17},{2,26},{10... | collective-permute-start | bytes 221192 | tf_op jit(solution)/shard_map/ppermute | solution.py:658
  21.0 2.8 %plain_part.1 = (f32[256,2048]{1,0:T(8,128)S(1)}, f32[256,2048]{1,0:T(8,128)S(1)}) custom-call(bf16[256,2048]{1,0:T(8,128)(2,1)S(1)} %copy-done.2, bf16[256,2048]{1,0:T(8,128)(2,1)S(1)} %copy-done.4, bf16[256,128]{1,0:T(8,128)(2,1)S(1)} %copy-done.7, bf16[256,128]{1,0:T(8,128)(2,1)S(1)} %copy-done.6, f32[32,256]{1,0:T(8,128)S(1)} %pad_maximum_fusion.packed_ref, ...), custom_call_target="tpu_custom_call" | custom-call | flops 268435456 | bytes 7340032 | tf_op jit(solution)/shard_map/plain_part/pallas_call | solution.py:143
  24.7 2.0 %collective-permute-start.6 = (bf16[144,256]{1,0:T(8,128)(2,1)S(1)}, bf16[144,256]{1,0:T(8,128)(2,1)S(1)}, u32[]{:S(2)}, u32[]{:S(2)}) collective-permute-start(bf16[144,256]{1,0:T(8,128)(2,1)S(1)} %get-tuple-element.60.p0), channel_id=1, source_target_pairs={{0,96},{32,0},{64,32},{96,64},{1,97},{33,1},{65,33},{97,65},{2,98}... | collective-permute-start | bytes 221192 | tf_op jit(solution)/shard_map/ppermute | solution.py:658
  28.0 2.0 %collective-permute-done.6.p3 = bf16[144,256]{1,0:T(8,128)(2,1)S(1)} collective-permute-done((bf16[144,256]{1,0:T(8,128)(2,1)S(1)}, bf16[144,256]{1,0:T(8,128)(2,1)S(1)}, u32[]{:S(2)}, u32[]{:S(2)}) %collective-permute-start.6) | collective-permute-done | bytes 73760 | tf_op jit(solution)/shard_map/ppermute | solution.py:658
  29.9 2.7 %collective-permute-done.5.p2 = bf16[144,256]{1,0:T(8,128)(2,1)S(1)} collective-permute-done((bf16[144,256]{1,0:T(8,128)(2,1)S(1)}, bf16[144,256]{1,0:T(8,128)(2,1)S(1)}, u32[]{:S(2)}, u32[]{:S(2)}) %collective-permute-start.5) | collective-permute-done | bytes 73760 | tf_op jit(solution)/shard_map/ppermute | solution.py:658
  35.0 1.8 %collective-permute-start.10 = (bf16[128,256]{1,0:T(8,128)(2,1)S(1)}, bf16[128,256]{1,0:T(8,128)(2,1)S(1)}, u32[]{:S(2)}, u32[]{:S(2)}) collective-permute-start(bf16[128,256]{1,0:T(8,128)(2,1)S(1)} %get-tuple-element.64), channel_id=1, source_target_pairs={{0,16},{8,24},{16,0},{24,8},{1,17},{9,25},{17,1},{25,9},{2,18},{10... | collective-permute-start | bytes 196616 | tf_op jit(solution)/shard_map/ppermute | solution.py:658
  36.8 1.3 %collective-permute-start.11 = (bf16[128,256]{1,0:T(8,128)(2,1)S(1)}, bf16[128,256]{1,0:T(8,128)(2,1)S(1)}, u32[]{:S(2)}, u32[]{:S(2)}) collective-permute-start(bf16[128,256]{1,0:T(8,128)(2,1)S(1)} %get-tuple-element.65), channel_id=1, source_target_pairs={{0,24},{8,0},{16,8},{24,16},{1,25},{9,1},{17,9},{25,17},{2,26},{10... | collective-permute-start | bytes 196616 | tf_op jit(solution)/shard_map/ppermute | solution.py:658
  38.1 3.0 %collective-permute-done.9.p1 = bf16[128,256]{1,0:T(8,128)(2,1)S(1)} collective-permute-done((bf16[128,256]{1,0:T(8,128)(2,1)S(1)}, bf16[128,256]{1,0:T(8,128)(2,1)S(1)}, u32[]{:S(2)}, u32[]{:S(2)}) %collective-permute-start.9) | collective-permute-done | bytes 65568 | tf_op jit(solution)/shard_map/ppermute | solution.py:658
  42.7 1.4 %collective-permute-start.20 = (bf16[1024,256]{1,0:T(8,128)(2,1)S(1)}, bf16[1024,256]{1,0:T(8,128)(2,1)S(1)}, u32[]{:S(2)}, u32[]{:S(2)}) collective-permute-start(bf16[1024,256]{1,0:T(8,128)(2,1)S(1)} %slice.8), channel_id=1, source_target_pairs={{0,32},{32,64},{64,96},{96,0},{1,33},{33,65},{65,97},{97,1},{2,34}... | collective-permute-start | bytes 1572872 | tf_op jit(solution)/shard_map/ppermute | solution.py:658
  44.1 1.9 %collective-permute-start.21 = (bf16[1024,256]{1,0:T(8,128)(2,1)S(1)}, bf16[1024,256]{1,0:T(8,128)(2,1)S(1)}, u32[]{:S(2)}, u32[]{:S(2)}) collective-permute-start(bf16[1024,256]{1,0:T(8,128)(2,1)S(1)} %slice.9), channel_id=1, source_target_pairs={{0,96},{32,0},{64,32},{96,64},{1,97},{33,1},{65,33},{97,65},{2,98}... | collective-permute-start | bytes 1572872 | tf_op jit(solution)/shard_map/ppermute | solution.py:658
  46.0 1.3 gated_part.1
  47.3 2.9 %collective-permute-start.17 = (bf16[128,2048]{1,0:T(8,128)(2,1)S(1)}, bf16[128,2048]{1,0:T(8,128)(2,1)S(1)}, u32[]{:S(2)}, u32[]{:S(2)}) collective-permute-start(bf16[128,2048]{1,0:T(8,128)(2,1)S(1)} %get-tuple-element.71.top_ref), channel_id=1, source_target_pairs={{0,24},{8,0},{16,8},{24,16},{1,25},{9,1},{17,9},{25,17},{2,26},{10... | collective-permute-start | bytes 1572872 | tf_op jit(solution)/shard_map/ppermute | solution.py:658
  50.2 1.8 %project_near.1.refs_4_ = bf16[3,2,256,256]{3,2,1,0:T(8,128)(2,1)S(1)} custom-call(bf16[128,2048]{1,0:T(8,128)(2,1)S(1)} %get-tuple-element.71.top_ref, bf16[128,2048]{1,0:T(8,128)(2,1)S(1)} %get-tuple-element.73.low_ref, bf16[2048,256]{1,0:T(8,128)(2,1)S(1)} %copy-done, bf16[2048,256]{1,0:T(8,128)(2,1)S(1)} %collective-permute-done.7.refs_0_.refs_1_.refs_3_, ...), custom_call_target="tpu_custom_call" | custom-call | flops 1610612736 | bytes 8388608 | tf_op jit(solution)/shard_map/project_near/pallas_call | solution.py:480
  52.1 6.2 %collective-permute-done.20.refs_5_.refs_0_ = bf16[1024,256]{1,0:T(8,128)(2,1)S(1)} collective-permute-done((bf16[1024,256]{1,0:T(8,128)(2,1)S(1)}, bf16[1024,256]{1,0:T(8,128)(2,1)S(1)}, u32[]{:S(2)}, u32[]{:S(2)}) %collective-permute-start.20) | collective-permute-done | bytes 524320 | tf_op jit(solution)/shard_map/ppermute | solution.py:658
  58.8 2.7 %collective-permute-done.17.refs_1_ = bf16[128,2048]{1,0:T(8,128)(2,1)S(1)} collective-permute-done((bf16[128,2048]{1,0:T(8,128)(2,1)S(1)}, bf16[128,2048]{1,0:T(8,128)(2,1)S(1)}, u32[]{:S(2)}, u32[]{:S(2)}) %collective-permute-start.17) | collective-permute-done | bytes 524320 | tf_op jit(solution)/shard_map/ppermute | solution.py:658
  61.5 3.4 %collective-permute-done.16.refs_0_ = bf16[128,2048]{1,0:T(8,128)(2,1)S(1)} collective-permute-done((bf16[128,2048]{1,0:T(8,128)(2,1)S(1)}, bf16[128,2048]{1,0:T(8,128)(2,1)S(1)}, u32[]{:S(2)}, u32[]{:S(2)}) %collective-permute-start.16) | collective-permute-done | bytes 524320 | tf_op jit(solution)/shard_map/ppermute | solution.py:658
  64.9 3.2 %collective-permute-start.18 = (bf16[128,2048]{1,0:T(8,128)(2,1)S(1)}, bf16[128,2048]{1,0:T(8,128)(2,1)S(1)}, u32[]{:S(2)}, u32[]{:S(2)}) collective-permute-start(bf16[128,2048]{1,0:T(8,128)(2,1)S(1)} %get-tuple-element.73.low_ref), channel_id=1, source_target_pairs={{0,24},{8,0},{16,8},{24,16},{1,25},{9,1},{17,9},{25,17},{2,26},{10... | collective-permute-start | bytes 1572872 | tf_op jit(solution)/shard_map/ppermute | solution.py:658
  68.2 1.4 %project_far.1 = (bf16[272,512]{1,0:T(8,128)(2,1)S(1)}, bf16[272,512]{1,0:T(8,128)(2,1)S(1)}, bf16[272,512]{1,0:T(8,128)(2,1)S(1)}, bf16[272,512]{1,0:T(8,128)(2,1)S(1)}) custom-call(s32[4]{0:T(128)S(1)} %pad_add_fusion.place, bf16[128,2048]{1,0:T(8,128)(2,1)S(1)} %get-tuple-element.71.top_ref, bf16[128,2048]{1,0:T(8,128)(2,1)S(1)} %get-tuple-element.73.low_ref, ...), custom_call_target="tpu_custom_call" | custom-call | flops 536870912 | bytes 4194304 | tf_op jit(solution)/shard_map/project_far/pallas_call | solution.py:504
  69.5 1.6 %collective-permute-start.26 = (bf16[272,512]{1,0:T(8,128)(2,1)S(1)}, bf16[272,512]{1,0:T(8,128)(2,1)S(1)}, u32[]{:S(2)}, u32[]{:S(2)}) collective-permute-start(bf16[272,512]{1,0:T(8,128)(2,1)S(1)} %get-tuple-element.82), channel_id=1, source_target_pairs={{0,1},{1,2},{2,3},{3,0},{4,5},{5,6},{6,7},{7,4},{8,9},{9,10},{10,1... | collective-permute-start | bytes 835592 | tf_op jit(solution)/shard_map/ppermute | solution.py:658
  72.2 2.2 %collective-permute-start.28 = (bf16[272,512]{1,0:T(8,128)(2,1)S(1)}, bf16[272,512]{1,0:T(8,128)(2,1)S(1)}, u32[]{:S(2)}, u32[]{:S(2)}) collective-permute-start(bf16[272,512]{1,0:T(8,128)(2,1)S(1)} %get-tuple-element.84), channel_id=1, source_target_pairs={{0,3},{1,0},{2,1},{3,2},{4,7},{5,4},{6,5},{7,6},{8,11},{9,8},{10,9... | collective-permute-start | bytes 835592 | tf_op jit(solution)/shard_map/ppermute | solution.py:658
  74.4 3.0 %project.3 = (bf16[256,512]{1,0:T(8,128)(2,1)S(1)}, bf16[256,512]{1,0:T(8,128)(2,1)S(1)}, bf16[256,512]{1,0:T(8,128)(2,1)S(1)}, bf16[256,512]{1,0:T(8,128)(2,1)S(1)}) custom-call(s32[4]{0:T(128)S(1)} %pad_add_fusion.place, bf16[128,2048]{1,0:T(8,128)(2,1)S(1)} %collective-permute-done.16.refs_0_, bf16[128,2048]{1,0:T(8,128)(2,1)S(1)} %collective-permute-done.17.refs_1_, ...), custom_call_target="tpu_custom_call" | custom-call | flops 2147483648 | bytes 10485760 | tf_op jit(solution)/shard_map/project/pallas_call | solution.py:440
  77.4 1.3 %collective-permute-done.19.refs_0_ = bf16[128,2048]{1,0:T(8,128)(2,1)S(1)} collective-permute-done((bf16[128,2048]{1,0:T(8,128)(2,1)S(1)}, bf16[128,2048]{1,0:T(8,128)(2,1)S(1)}, u32[]{:S(2)}, u32[]{:S(2)}) %collective-permute-start.19) | collective-permute-done | bytes 524320 | tf_op jit(solution)/shard_map/ppermute | solution.py:658
  78.7 3.2 %collective-permute-start.25 = (bf16[128,2048]{1,0:T(8,128)(2,1)S(1)}, bf16[128,2048]{1,0:T(8,128)(2,1)S(1)}, u32[]{:S(2)}, u32[]{:S(2)}) collective-permute-start(bf16[128,2048]{1,0:T(8,128)(2,1)S(1)} %collective-permute-done.18.refs_1_), channel_id=1, source_target_pairs={{0,24},{8,0},{16,8},{24,16},{1,25},{9,1},{17,9},{25,17},{2,26},{10... | collective-permute-start | bytes 1572872 | tf_op jit(solution)/shard_map/ppermute | solution.py:658
  81.9 1.5 %collective-permute-start.33 = (bf16[256,512]{1,0:T(8,128)(2,1)S(1)}, bf16[256,512]{1,0:T(8,128)(2,1)S(1)}, u32[]{:S(2)}, u32[]{:S(2)}) collective-permute-start(bf16[256,512]{1,0:T(8,128)(2,1)S(1)} %get-tuple-element.91), channel_id=1, source_target_pairs={{0,1},{1,2},{2,3},{3,0},{4,5},{5,6},{6,7},{7,4},{8,9},{9,10},{10,1... | collective-permute-start | bytes 786440 | tf_op jit(solution)/shard_map/ppermute | solution.py:658
  84.6 2.2 %collective-permute-start.35 = (bf16[256,512]{1,0:T(8,128)(2,1)S(1)}, bf16[256,512]{1,0:T(8,128)(2,1)S(1)}, u32[]{:S(2)}, u32[]{:S(2)}) collective-permute-start(bf16[256,512]{1,0:T(8,128)(2,1)S(1)} %get-tuple-element.93), channel_id=1, source_target_pairs={{0,3},{1,0},{2,1},{3,2},{4,7},{5,4},{6,5},{7,6},{8,11},{9,8},{10,9... | collective-permute-start | bytes 786440 | tf_op jit(solution)/shard_map/ppermute | solution.py:658
  86.7 3.0 %project.4 = (bf16[256,512]{1,0:T(8,128)(2,1)S(1)}, bf16[256,512]{1,0:T(8,128)(2,1)S(1)}, bf16[256,512]{1,0:T(8,128)(2,1)S(1)}, bf16[256,512]{1,0:T(8,128)(2,1)S(1)}) custom-call(s32[4]{0:T(128)S(1)} %pad_add_fusion.place, bf16[128,2048]{1,0:T(8,128)(2,1)S(1)} %collective-permute-done.19.refs_0_, bf16[128,2048]{1,0:T(8,128)(2,1)S(1)} %collective-permute-done.18.refs_1_, ...), custom_call_target="tpu_custom_call" | custom-call | flops 2147483648 | bytes 10485760 | tf_op jit(solution)/shard_map/project/pallas_call | solution.py:440
  89.7 1.4 %collective-permute-done.33.refs_1_ = bf16[256,512]{1,0:T(8,128)(2,1)S(1)} collective-permute-done((bf16[256,512]{1,0:T(8,128)(2,1)S(1)}, bf16[256,512]{1,0:T(8,128)(2,1)S(1)}, u32[]{:S(2)}, u32[]{:S(2)}) %collective-permute-start.33) | collective-permute-done | bytes 262176 | tf_op jit(solution)/shard_map/ppermute | solution.py:658
  91.1 2.4 %collective-permute-start.36 = (bf16[256,512]{1,0:T(8,128)(2,1)S(1)}, bf16[256,512]{1,0:T(8,128)(2,1)S(1)}, u32[]{:S(2)}, u32[]{:S(2)}) collective-permute-start(bf16[256,512]{1,0:T(8,128)(2,1)S(1)} %get-tuple-element.94), channel_id=1, source_target_pairs={{0,1},{1,2},{2,3},{3,0},{4,5},{5,6},{6,7},{7,4},{8,9},{9,10},{10,1... | collective-permute-start | bytes 786440 | tf_op jit(solution)/shard_map/ppermute | solution.py:658
  93.5 2.2 %collective-permute-start.37 = (bf16[256,512]{1,0:T(8,128)(2,1)S(1)}, bf16[256,512]{1,0:T(8,128)(2,1)S(1)}, u32[]{:S(2)}, u32[]{:S(2)}) collective-permute-start(bf16[256,512]{1,0:T(8,128)(2,1)S(1)} %get-tuple-element.95), channel_id=1, source_target_pairs={{0,2},{1,3},{2,0},{3,1},{4,6},{5,7},{6,4},{7,5},{8,10},{9,11},{10,... | collective-permute-start | bytes 786440 | tf_op jit(solution)/shard_map/ppermute | solution.py:658
  96.0 3.0 %project.5 = (bf16[256,512]{1,0:T(8,128)(2,1)S(1)}, bf16[256,512]{1,0:T(8,128)(2,1)S(1)}, bf16[256,512]{1,0:T(8,128)(2,1)S(1)}, bf16[256,512]{1,0:T(8,128)(2,1)S(1)}) custom-call(s32[4]{0:T(128)S(1)} %pad_add_fusion.place, bf16[128,2048]{1,0:T(8,128)(2,1)S(1)} %collective-permute-done.24.refs_0_, bf16[128,2048]{1,0:T(8,128)(2,1)S(1)} %collective-permute-done.25.refs_1_, ...), custom_call_target="tpu_custom_call" | custom-call | flops 2147483648 | bytes 10485760 | tf_op jit(solution)/shard_map/project/pallas_call | solution.py:440
  99.0 1.8 %collective-permute-start.29 = (bf16[256,512]{1,0:T(8,128)(2,1)S(1)}, bf16[256,512]{1,0:T(8,128)(2,1)S(1)}, u32[]{:S(2)}, u32[]{:S(2)}) collective-permute-start(bf16[256,512]{1,0:T(8,128)(2,1)S(1)} %get-tuple-element.87), channel_id=1, source_target_pairs={{0,1},{1,2},{2,3},{3,0},{4,5},{5,6},{6,7},{7,4},{8,9},{9,10},{10,1... | collective-permute-start | bytes 786440 | tf_op jit(solution)/shard_map/ppermute | solution.py:658
  100.8 2.5 %collective-permute-start.30 = (bf16[256,512]{1,0:T(8,128)(2,1)S(1)}, bf16[256,512]{1,0:T(8,128)(2,1)S(1)}, u32[]{:S(2)}, u32[]{:S(2)}) collective-permute-start(bf16[256,512]{1,0:T(8,128)(2,1)S(1)} %get-tuple-element.88), channel_id=1, source_target_pairs={{0,2},{1,3},{2,0},{3,1},{4,6},{5,7},{6,4},{7,5},{8,10},{9,11},{10,... | collective-permute-start | bytes 786440 | tf_op jit(solution)/shard_map/ppermute | solution.py:658
  103.3 2.1 %collective-permute-done.36.refs_5_ = bf16[256,512]{1,0:T(8,128)(2,1)S(1)} collective-permute-done((bf16[256,512]{1,0:T(8,128)(2,1)S(1)}, bf16[256,512]{1,0:T(8,128)(2,1)S(1)}, u32[]{:S(2)}, u32[]{:S(2)}) %collective-permute-start.36) | collective-permute-done | bytes 262176 | tf_op jit(solution)/shard_map/ppermute | solution.py:658
  105.4 4.3 %collective-permute-start.31 = (bf16[256,512]{1,0:T(8,128)(2,1)S(1)}, bf16[256,512]{1,0:T(8,128)(2,1)S(1)}, u32[]{:S(2)}, u32[]{:S(2)}) collective-permute-start(bf16[256,512]{1,0:T(8,128)(2,1)S(1)} %get-tuple-element.89), channel_id=1, source_target_pairs={{0,3},{1,0},{2,1},{3,2},{4,7},{5,4},{6,5},{7,6},{8,11},{9,8},{10,9... | collective-permute-start | bytes 786440 | tf_op jit(solution)/shard_map/ppermute | solution.py:658
  109.7 1.3 %collective-permute-done.38.refs_7_ = bf16[256,512]{1,0:T(8,128)(2,1)S(1)} collective-permute-done((bf16[256,512]{1,0:T(8,128)(2,1)S(1)}, bf16[256,512]{1,0:T(8,128)(2,1)S(1)}, u32[]{:S(2)}, u32[]{:S(2)}) %collective-permute-start.38) | collective-permute-done | bytes 262176 | tf_op jit(solution)/shard_map/ppermute | solution.py:658
  111.3 1.8 %collective-permute-start.39 = (bf16[256,512]{1,0:T(8,128)(2,1)S(1)}, bf16[256,512]{1,0:T(8,128)(2,1)S(1)}, u32[]{:S(2)}, u32[]{:S(2)}) collective-permute-start(bf16[256,512]{1,0:T(8,128)(2,1)S(1)} %get-tuple-element.97), channel_id=1, source_target_pairs={{0,24},{8,0},{16,8},{24,16},{1,25},{9,1},{17,9},{25,17},{2,26},{10... | collective-permute-start | bytes 786440 | tf_op jit(solution)/shard_map/ppermute | solution.py:658
  113.4 2.8 %collective-permute-done.30.refs_2_ = bf16[256,512]{1,0:T(8,128)(2,1)S(1)} collective-permute-done((bf16[256,512]{1,0:T(8,128)(2,1)S(1)}, bf16[256,512]{1,0:T(8,128)(2,1)S(1)}, u32[]{:S(2)}, u32[]{:S(2)}) %collective-permute-start.30) | collective-permute-done | bytes 262176 | tf_op jit(solution)/shard_map/ppermute | solution.py:658
  116.2 2.6 %collective-permute-done.31.refs_3_ = bf16[256,512]{1,0:T(8,128)(2,1)S(1)} collective-permute-done((bf16[256,512]{1,0:T(8,128)(2,1)S(1)}, bf16[256,512]{1,0:T(8,128)(2,1)S(1)}, u32[]{:S(2)}, u32[]{:S(2)}) %collective-permute-start.31) | collective-permute-done | bytes 262176 | tf_op jit(solution)/shard_map/ppermute | solution.py:658
  119.3 1.4 %collective-permute-done.40.down_ref = bf16[256,512]{1,0:T(8,128)(2,1)S(1)} collective-permute-done((bf16[256,512]{1,0:T(8,128)(2,1)S(1)}, bf16[256,512]{1,0:T(8,128)(2,1)S(1)}, u32[]{:S(2)}, u32[]{:S(2)}) %collective-permute-start.40) | collective-permute-done | bytes 262176 | tf_op jit(solution)/shard_map/ppermute | solution.py:658
  120.7 2.4 %finish.1 = (bf16[256,2048]{1,0:T(8,128)(2,1)}, f32[256,128]{1,0:T(8,128)S(1)}) custom-call(s32[4]{0:T(128)S(1)} %pad_add_fusion.place, bf16[272,512]{1,0:T(8,128)(2,1)S(1)} %get-tuple-element.90.p0, bf16[272,512]{1,0:T(8,128)(2,1)S(1)} %collective-permute-done.26.refs_12_.p1, bf16[272,512]{1,0:T(8,128)(2,1)S(1)} %collective-permute-done.27.refs_13_.p2, ...), custom_call_target="tpu_custom_call" | custom-call | flops 1572864 | bytes 3145728 | tf_op jit(solution)/shard_map/finish/pallas_call | solution.py:620
  123.1 5.1 %collective-permute-done.32.far_ref = bf16[256,512]{1,0:T(8,128)(2,1)S(1)} collective-permute-done((bf16[256,512]{1,0:T(8,128)(2,1)S(1)}, bf16[256,512]{1,0:T(8,128)(2,1)S(1)}, u32[]{:S(2)}, u32[]{:S(2)}) %collective-permute-start.32) | collective-permute-done | bytes 262176 | tf_op jit(solution)/shard_map/ppermute | solution.py:658
  128.2 1.4 %finish_far.1 = bf16[256,2048]{1,0:T(8,128)(2,1)} custom-call(s32[4]{0:T(128)S(1)} %pad_add_fusion.place, bf16[256,512]{1,0:T(8,128)(2,1)S(1)} %collective-permute-done.32.far_ref, f32[256,128]{1,0:T(8,128)S(1)} %get-tuple-element.99.scale_ref, bf16[256,2048]{1,0:T(8,128)(2,1)S(1)} %copy-done.3, ...), custom_call_target="tpu_custom_call", output_to_operand_aliasing={{}: (4, {})} | custom-call | flops 524288 | bytes 1048576 | tf_op jit(solution)/shard_map/finish_far/pallas_call | solution.py:641
  (76 shorter events, 16.8 us)
Async XLA Ops:
  0.0 20.9 %copy-start.6 = (bf16[256,128]{1,0:T(8,128)(2,1)S(1)}, bf16[256,128]{1,0:T(8,128)(2,1)}, u32[]{:S(2)}) copy-start(bf16[256,128]{1,0:T(8,128)(2,1)} %read_ref.3) | copy-start | bytes 196612
  0.0 20.9 %copy-start.9 = (f32[16]{0:T(128)S(1)}, f32[16]{0:T(128)}, u32[]{:S(2)}) copy-start(f32[16]{0:T(128)} %param.17) | copy-start | bytes 196
  0.0 33.1 %collective-permute-start.8 = (bf16[2048,256]{1,0:T(8,128)(2,1)}, bf16[2048,256]{1,0:T(8,128)(2,1)S(1)}, u32[]{:S(2)}, u32[]{:S(2)}) collective-permute-start(bf16[2048,256]{1,0:T(8,128)(2,1)} %refs_2_.5), channel_id=1, source_target_pairs={{0,32},{32,64},{64,96},{96,0},{1,33},{33,65},{65,97},{97,1},{2,34}... | collective-permute-start | bytes 3145736 | tf_op jit(solution)/shard_map/ppermute | solution.py:658
  1.9 31.2 %collective-permute-start.7 = (bf16[2048,256]{1,0:T(8,128)(2,1)}, bf16[2048,256]{1,0:T(8,128)(2,1)S(1)}, u32[]{:S(2)}, u32[]{:S(2)}) collective-permute-start(bf16[2048,256]{1,0:T(8,128)(2,1)} %refs_2_.5), channel_id=1, source_target_pairs={{0,96},{32,0},{64,32},{96,64},{1,97},{33,1},{65,33},{97,65},{2,98}... | collective-permute-start | bytes 3145736 | tf_op jit(solution)/shard_map/ppermute | solution.py:658
  7.8 13.2 %copy-start.2 = (bf16[256,2048]{1,0:T(8,128)(2,1)S(1)}, bf16[256,2048]{1,0:T(8,128)(2,1)}, u32[]{:S(2)}) copy-start(bf16[256,2048]{1,0:T(8,128)(2,1)} %value_ref.3) | copy-start | bytes 3145732
  7.8 13.2 %copy-start.4 = (bf16[256,2048]{1,0:T(8,128)(2,1)S(1)}, bf16[256,2048]{1,0:T(8,128)(2,1)}, u32[]{:S(2)}) copy-start(bf16[256,2048]{1,0:T(8,128)(2,1)} %gate_ref.1) | copy-start | bytes 3145732
  10.1 2.0 %collective-permute-start = (f32[136,1024]{1,0:T(8,128)S(1)}, f32[136,1024]{1,0:T(8,128)S(1)}, u32[]{:S(2)}, u32[]{:S(2)}) collective-permute-start(f32[136,1024]{1,0:T(8,128)S(1)} %get-tuple-element.54), channel_id=1, source_target_pairs={{0,4},{4,0},{1,5},{5,1},{2,6},{6,2},{3,7},{7,3},{8,12},{12,8},{9,1... | collective-permute-start | bytes 1671176 | tf_op jit(solution)/shard_map/ppermute | solution.py:662
  13.0 10.8 %collective-permute-start.1 = (bf16[144,256]{1,0:T(8,128)(2,1)S(1)}, bf16[144,256]{1,0:T(8,128)(2,1)S(1)}, u32[]{:S(2)}, u32[]{:S(2)}) collective-permute-start(bf16[144,256]{1,0:T(8,128)(2,1)S(1)} %get-tuple-element.56), channel_id=1, source_target_pairs={{0,8},{8,16},{16,24},{24,0},{1,9},{9,17},{17,25},{25,1},{2,10},{10... | collective-permute-start | bytes 221192 | tf_op jit(solution)/shard_map/ppermute | solution.py:658
  14.7 9.1 %collective-permute-start.2 = (bf16[144,256]{1,0:T(8,128)(2,1)S(1)}, bf16[144,256]{1,0:T(8,128)(2,1)S(1)}, u32[]{:S(2)}, u32[]{:S(2)}) collective-permute-start(bf16[144,256]{1,0:T(8,128)(2,1)S(1)} %get-tuple-element.57), channel_id=1, source_target_pairs={{0,16},{8,24},{16,0},{24,8},{1,17},{9,25},{17,1},{25,9},{2,18},{10... | collective-permute-start | bytes 221192 | tf_op jit(solution)/shard_map/ppermute | solution.py:658
  17.6 6.3 %collective-permute-start.3 = (bf16[144,256]{1,0:T(8,128)(2,1)S(1)}, bf16[144,256]{1,0:T(8,128)(2,1)S(1)}, u32[]{:S(2)}, u32[]{:S(2)}) collective-permute-start(bf16[144,256]{1,0:T(8,128)(2,1)S(1)} %get-tuple-element.58), channel_id=1, source_target_pairs={{0,24},{8,0},{16,8},{24,16},{1,25},{9,1},{17,9},{25,17},{2,26},{10... | collective-permute-start | bytes 221192 | tf_op jit(solution)/shard_map/ppermute | solution.py:658
  21.0 9.0 %copy-start = (bf16[2048,256]{1,0:T(8,128)(2,1)S(1)}, bf16[2048,256]{1,0:T(8,128)(2,1)}, u32[]{:S(2)}) copy-start(bf16[2048,256]{1,0:T(8,128)(2,1)} %refs_2_.5) | copy-start | bytes 3145732
  24.7 5.2 %collective-permute-start.6 = (bf16[144,256]{1,0:T(8,128)(2,1)S(1)}, bf16[144,256]{1,0:T(8,128)(2,1)S(1)}, u32[]{:S(2)}, u32[]{:S(2)}) collective-permute-start(bf16[144,256]{1,0:T(8,128)(2,1)S(1)} %get-tuple-element.60.p0), channel_id=1, source_target_pairs={{0,96},{32,0},{64,32},{96,64},{1,97},{33,1},{65,33},{97,65},{2,98}... | collective-permute-start | bytes 221192 | tf_op jit(solution)/shard_map/ppermute | solution.py:658
  26.7 6.0 %collective-permute-start.5 = (bf16[144,256]{1,0:T(8,128)(2,1)S(1)}, bf16[144,256]{1,0:T(8,128)(2,1)S(1)}, u32[]{:S(2)}, u32[]{:S(2)}) collective-permute-start(bf16[144,256]{1,0:T(8,128)(2,1)S(1)} %get-tuple-element.60.p0), channel_id=1, source_target_pairs={{0,64},{32,96},{64,0},{96,32},{1,65},{33,97},{65,1},{97,33},{2,66}... | collective-permute-start | bytes 221192 | tf_op jit(solution)/shard_map/ppermute | solution.py:658
  26.7 6.4 %collective-permute-start.4 = (bf16[144,256]{1,0:T(8,128)(2,1)S(1)}, bf16[144,256]{1,0:T(8,128)(2,1)S(1)}, u32[]{:S(2)}, u32[]{:S(2)}) collective-permute-start(bf16[144,256]{1,0:T(8,128)(2,1)S(1)} %get-tuple-element.60.p0), channel_id=1, source_target_pairs={{0,32},{32,64},{64,96},{96,0},{1,33},{33,65},{65,97},{97,1},{2,34}... | collective-permute-start | bytes 221192 | tf_op jit(solution)/shard_map/ppermute | solution.py:658
  29.9 6.9 %collective-permute-start.12 = (bf16[2048,256]{1,0:T(8,128)(2,1)S(1)}, bf16[2048,256]{1,0:T(8,128)(2,1)S(1)}, u32[]{:S(2)}, u32[]{:S(2)}) collective-permute-start(bf16[2048,256]{1,0:T(8,128)(2,1)S(1)} %copy-done), channel_id=1, source_target_pairs={{0,4},{4,0},{1,5},{5,1},{2,6},{6,2},{3,7},{7,3},{8,12},{12,8},{9,1... | collective-permute-start | bytes 3145736 | tf_op jit(solution)/shard_map/ppermute | solution.py:662
  33.1 8.5 %collective-permute-start.13 = (bf16[2048,256]{1,0:T(8,128)(2,1)S(1)}, bf16[2048,256]{1,0:T(8,128)(2,1)S(1)}, u32[]{:S(2)}, u32[]{:S(2)}) collective-permute-start(bf16[2048,256]{1,0:T(8,128)(2,1)S(1)} %collective-permute-done.7.refs_0_.refs_1_.refs_3_), channel_id=1, source_target_pairs={{0,4},{4,0},{1,5},{5,1},{2,6},{6,2},{3,7},{7,3},{8,12},{12,8},{9,1... | collective-permute-start | bytes 3145736 | tf_op jit(solution)/shard_map/ppermute | solution.py:662
  33.1 8.5 %collective-permute-start.14 = (bf16[2048,256]{1,0:T(8,128)(2,1)S(1)}, bf16[2048,256]{1,0:T(8,128)(2,1)S(1)}, u32[]{:S(2)}, u32[]{:S(2)}) collective-permute-start(bf16[2048,256]{1,0:T(8,128)(2,1)S(1)} %collective-permute-done.8.refs_1_.refs_2_.refs_4_), channel_id=1, source_target_pairs={{0,4},{4,0},{1,5},{5,1},{2,6},{6,2},{3,7},{7,3},{8,12},{12,8},{9,1... | collective-permute-start | bytes 3145736 | tf_op jit(solution)/shard_map/ppermute | solution.py:662
  34.3 6.8 %collective-permute-start.9 = (bf16[128,256]{1,0:T(8,128)(2,1)S(1)}, bf16[128,256]{1,0:T(8,128)(2,1)S(1)}, u32[]{:S(2)}, u32[]{:S(2)}) collective-permute-start(bf16[128,256]{1,0:T(8,128)(2,1)S(1)} %get-tuple-element.63), channel_id=1, source_target_pairs={{0,8},{8,16},{16,24},{24,0},{1,9},{9,17},{17,25},{25,1},{2,10},{10... | collective-permute-start | bytes 196616 | tf_op jit(solution)/shard_map/ppermute | solution.py:658
  35.0 6.1 %collective-permute-start.10 = (bf16[128,256]{1,0:T(8,128)(2,1)S(1)}, bf16[128,256]{1,0:T(8,128)(2,1)S(1)}, u32[]{:S(2)}, u32[]{:S(2)}) collective-permute-start(bf16[128,256]{1,0:T(8,128)(2,1)S(1)} %get-tuple-element.64), channel_id=1, source_target_pairs={{0,16},{8,24},{16,0},{24,8},{1,17},{9,25},{17,1},{25,9},{2,18},{10... | collective-permute-start | bytes 196616 | tf_op jit(solution)/shard_map/ppermute | solution.py:658
  36.8 4.8 %collective-permute-start.11 = (bf16[128,256]{1,0:T(8,128)(2,1)S(1)}, bf16[128,256]{1,0:T(8,128)(2,1)S(1)}, u32[]{:S(2)}, u32[]{:S(2)}) collective-permute-start(bf16[128,256]{1,0:T(8,128)(2,1)S(1)} %get-tuple-element.65), channel_id=1, source_target_pairs={{0,24},{8,0},{16,8},{24,16},{1,25},{9,1},{17,9},{25,17},{2,26},{10... | collective-permute-start | bytes 196616 | tf_op jit(solution)/shard_map/ppermute | solution.py:658
  42.5 3.5 %copy-start.8 = (f32[2048]{0:T(1024)S(1)}, f32[2048]{0:T(1024)}, u32[]{:S(2)}) copy-start(f32[2048]{0:T(1024)} %param.19) | copy-start | bytes 24580
  42.5 3.5 %collective-permute-start.15 = (bf16[128,1024]{1,0:T(8,128)(2,1)S(1)}, bf16[128,1024]{1,0:T(8,128)(2,1)S(1)}, u32[]{:S(2)}, u32[]{:S(2)}) collective-permute-start(bf16[128,1024]{1,0:T(8,128)(2,1)S(1)} %get-tuple-element.69), channel_id=1, source_target_pairs={{0,4},{4,0},{1,5},{5,1},{2,6},{6,2},{3,7},{7,3},{8,12},{12,8},{9,1... | collective-permute-start | bytes 786440 | tf_op jit(solution)/shard_map/ppermute | solution.py:662
  42.7 15.6 %collective-permute-start.20 = (bf16[1024,256]{1,0:T(8,128)(2,1)S(1)}, bf16[1024,256]{1,0:T(8,128)(2,1)S(1)}, u32[]{:S(2)}, u32[]{:S(2)}) collective-permute-start(bf16[1024,256]{1,0:T(8,128)(2,1)S(1)} %slice.8), channel_id=1, source_target_pairs={{0,32},{32,64},{64,96},{96,0},{1,33},{33,65},{65,97},{97,1},{2,34}... | collective-permute-start | bytes 1572872 | tf_op jit(solution)/shard_map/ppermute | solution.py:658
  44.1 14.2 %collective-permute-start.21 = (bf16[1024,256]{1,0:T(8,128)(2,1)S(1)}, bf16[1024,256]{1,0:T(8,128)(2,1)S(1)}, u32[]{:S(2)}, u32[]{:S(2)}) collective-permute-start(bf16[1024,256]{1,0:T(8,128)(2,1)S(1)} %slice.9), channel_id=1, source_target_pairs={{0,96},{32,0},{64,32},{96,64},{1,97},{33,1},{65,33},{97,65},{2,98}... | collective-permute-start | bytes 1572872 | tf_op jit(solution)/shard_map/ppermute | solution.py:658
  47.3 14.2 %collective-permute-start.17 = (bf16[128,2048]{1,0:T(8,128)(2,1)S(1)}, bf16[128,2048]{1,0:T(8,128)(2,1)S(1)}, u32[]{:S(2)}, u32[]{:S(2)}) collective-permute-start(bf16[128,2048]{1,0:T(8,128)(2,1)S(1)} %get-tuple-element.71.top_ref), channel_id=1, source_target_pairs={{0,24},{8,0},{16,8},{24,16},{1,25},{9,1},{17,9},{25,17},{2,26},{10... | collective-permute-start | bytes 1572872 | tf_op jit(solution)/shard_map/ppermute | solution.py:658
  50.2 14.7 %collective-permute-start.16 = (bf16[128,2048]{1,0:T(8,128)(2,1)S(1)}, bf16[128,2048]{1,0:T(8,128)(2,1)S(1)}, u32[]{:S(2)}, u32[]{:S(2)}) collective-permute-start(bf16[128,2048]{1,0:T(8,128)(2,1)S(1)} %get-tuple-element.71.top_ref), channel_id=1, source_target_pairs={{0,8},{8,16},{16,24},{24,0},{1,9},{9,17},{17,25},{25,1},{2,10},{10... | collective-permute-start | bytes 1572872 | tf_op jit(solution)/shard_map/ppermute | solution.py:658
  58.3 9.9 %collective-permute-start.22 = (bf16[1024,256]{1,0:T(8,128)(2,1)S(1)}, bf16[1024,256]{1,0:T(8,128)(2,1)S(1)}, u32[]{:S(2)}, u32[]{:S(2)}) collective-permute-start(bf16[1024,256]{1,0:T(8,128)(2,1)S(1)} %collective-permute-done.20.refs_5_.refs_0_), channel_id=1, source_target_pairs={{0,4},{4,0},{1,5},{5,1},{2,6},{6,2},{3,7},{7,3},{8,12},{12,8},{9,1... | collective-permute-start | bytes 1572872 | tf_op jit(solution)/shard_map/ppermute | solution.py:662
  58.3 9.9 %collective-permute-start.23 = (bf16[1024,256]{1,0:T(8,128)(2,1)S(1)}, bf16[1024,256]{1,0:T(8,128)(2,1)S(1)}, u32[]{:S(2)}, u32[]{:S(2)}) collective-permute-start(bf16[1024,256]{1,0:T(8,128)(2,1)S(1)} %collective-permute-done.21.refs_6_.refs_1_), channel_id=1, source_target_pairs={{0,4},{4,0},{1,5},{5,1},{2,6},{6,2},{3,7},{7,3},{8,12},{12,8},{9,1... | collective-permute-start | bytes 1572872 | tf_op jit(solution)/shard_map/ppermute | solution.py:662
  64.9 13.8 %collective-permute-start.19 = (bf16[128,2048]{1,0:T(8,128)(2,1)S(1)}, bf16[128,2048]{1,0:T(8,128)(2,1)S(1)}, u32[]{:S(2)}, u32[]{:S(2)}) collective-permute-start(bf16[128,2048]{1,0:T(8,128)(2,1)S(1)} %get-tuple-element.73.low_ref), channel_id=1, source_target_pairs={{0,8},{8,16},{16,24},{24,0},{1,9},{9,17},{17,25},{25,1},{2,10},{10... | collective-permute-start | bytes 1572872 | tf_op jit(solution)/shard_map/ppermute | solution.py:658
  64.9 13.8 %collective-permute-start.18 = (bf16[128,2048]{1,0:T(8,128)(2,1)S(1)}, bf16[128,2048]{1,0:T(8,128)(2,1)S(1)}, u32[]{:S(2)}, u32[]{:S(2)}) collective-permute-start(bf16[128,2048]{1,0:T(8,128)(2,1)S(1)} %get-tuple-element.73.low_ref), channel_id=1, source_target_pairs={{0,24},{8,0},{16,8},{24,16},{1,25},{9,1},{17,9},{25,17},{2,26},{10... | collective-permute-start | bytes 1572872 | tf_op jit(solution)/shard_map/ppermute | solution.py:658
  69.5 12.4 %collective-permute-start.26 = (bf16[272,512]{1,0:T(8,128)(2,1)S(1)}, bf16[272,512]{1,0:T(8,128)(2,1)S(1)}, u32[]{:S(2)}, u32[]{:S(2)}) collective-permute-start(bf16[272,512]{1,0:T(8,128)(2,1)S(1)} %get-tuple-element.82), channel_id=1, source_target_pairs={{0,1},{1,2},{2,3},{3,0},{4,5},{5,6},{6,7},{7,4},{8,9},{9,10},{10,1... | collective-permute-start | bytes 835592 | tf_op jit(solution)/shard_map/ppermute | solution.py:658
  71.1 12.3 %collective-permute-start.27 = (bf16[272,512]{1,0:T(8,128)(2,1)S(1)}, bf16[272,512]{1,0:T(8,128)(2,1)S(1)}, u32[]{:S(2)}, u32[]{:S(2)}) collective-permute-start(bf16[272,512]{1,0:T(8,128)(2,1)S(1)} %get-tuple-element.83), channel_id=1, source_target_pairs={{0,2},{1,3},{2,0},{3,1},{4,6},{5,7},{6,4},{7,5},{8,10},{9,11},{10,... | collective-permute-start | bytes 835592 | tf_op jit(solution)/shard_map/ppermute | solution.py:658
  72.2 12.3 %collective-permute-start.28 = (bf16[272,512]{1,0:T(8,128)(2,1)S(1)}, bf16[272,512]{1,0:T(8,128)(2,1)S(1)}, u32[]{:S(2)}, u32[]{:S(2)}) collective-permute-start(bf16[272,512]{1,0:T(8,128)(2,1)S(1)} %get-tuple-element.84), channel_id=1, source_target_pairs={{0,3},{1,0},{2,1},{3,2},{4,7},{5,4},{6,5},{7,6},{8,11},{9,8},{10,9... | collective-permute-start | bytes 835592 | tf_op jit(solution)/shard_map/ppermute | solution.py:658
  78.7 14.8 %collective-permute-start.24 = (bf16[128,2048]{1,0:T(8,128)(2,1)S(1)}, bf16[128,2048]{1,0:T(8,128)(2,1)S(1)}, u32[]{:S(2)}, u32[]{:S(2)}) collective-permute-start(bf16[128,2048]{1,0:T(8,128)(2,1)S(1)} %collective-permute-done.16.refs_0_), channel_id=1, source_target_pairs={{0,8},{8,16},{16,24},{24,0},{1,9},{9,17},{17,25},{25,1},{2,10},{10... | collective-permute-start | bytes 1572872 | tf_op jit(solution)/shard_map/ppermute | solution.py:658
  78.7 17.0 %collective-permute-start.25 = (bf16[128,2048]{1,0:T(8,128)(2,1)S(1)}, bf16[128,2048]{1,0:T(8,128)(2,1)S(1)}, u32[]{:S(2)}, u32[]{:S(2)}) collective-permute-start(bf16[128,2048]{1,0:T(8,128)(2,1)S(1)} %collective-permute-done.18.refs_1_), channel_id=1, source_target_pairs={{0,24},{8,0},{16,8},{24,16},{1,25},{9,1},{17,9},{25,17},{2,26},{10... | collective-permute-start | bytes 1572872 | tf_op jit(solution)/shard_map/ppermute | solution.py:658
  81.9 9.1 %collective-permute-start.33 = (bf16[256,512]{1,0:T(8,128)(2,1)S(1)}, bf16[256,512]{1,0:T(8,128)(2,1)S(1)}, u32[]{:S(2)}, u32[]{:S(2)}) collective-permute-start(bf16[256,512]{1,0:T(8,128)(2,1)S(1)} %get-tuple-element.91), channel_id=1, source_target_pairs={{0,1},{1,2},{2,3},{3,0},{4,5},{5,6},{6,7},{7,4},{8,9},{9,10},{10,1... | collective-permute-start | bytes 786440 | tf_op jit(solution)/shard_map/ppermute | solution.py:658
  83.4 15.5 %collective-permute-start.34 = (bf16[256,512]{1,0:T(8,128)(2,1)S(1)}, bf16[256,512]{1,0:T(8,128)(2,1)S(1)}, u32[]{:S(2)}, u32[]{:S(2)}) collective-permute-start(bf16[256,512]{1,0:T(8,128)(2,1)S(1)} %get-tuple-element.92), channel_id=1, source_target_pairs={{0,2},{1,3},{2,0},{3,1},{4,6},{5,7},{6,4},{7,5},{8,10},{9,11},{10,... | collective-permute-start | bytes 786440 | tf_op jit(solution)/shard_map/ppermute | solution.py:658
  84.6 16.2 %collective-permute-start.35 = (bf16[256,512]{1,0:T(8,128)(2,1)S(1)}, bf16[256,512]{1,0:T(8,128)(2,1)S(1)}, u32[]{:S(2)}, u32[]{:S(2)}) collective-permute-start(bf16[256,512]{1,0:T(8,128)(2,1)S(1)} %get-tuple-element.93), channel_id=1, source_target_pairs={{0,3},{1,0},{2,1},{3,2},{4,7},{5,4},{6,5},{7,6},{8,11},{9,8},{10,9... | collective-permute-start | bytes 786440 | tf_op jit(solution)/shard_map/ppermute | solution.py:658
  91.1 14.3 %collective-permute-start.36 = (bf16[256,512]{1,0:T(8,128)(2,1)S(1)}, bf16[256,512]{1,0:T(8,128)(2,1)S(1)}, u32[]{:S(2)}, u32[]{:S(2)}) collective-permute-start(bf16[256,512]{1,0:T(8,128)(2,1)S(1)} %get-tuple-element.94), channel_id=1, source_target_pairs={{0,1},{1,2},{2,3},{3,0},{4,5},{5,6},{6,7},{7,4},{8,9},{9,10},{10,1... | collective-permute-start | bytes 786440 | tf_op jit(solution)/shard_map/ppermute | solution.py:658
  93.5 16.3 %collective-permute-start.37 = (bf16[256,512]{1,0:T(8,128)(2,1)S(1)}, bf16[256,512]{1,0:T(8,128)(2,1)S(1)}, u32[]{:S(2)}, u32[]{:S(2)}) collective-permute-start(bf16[256,512]{1,0:T(8,128)(2,1)S(1)} %get-tuple-element.95), channel_id=1, source_target_pairs={{0,2},{1,3},{2,0},{3,1},{4,6},{5,7},{6,4},{7,5},{8,10},{9,11},{10,... | collective-permute-start | bytes 786440 | tf_op jit(solution)/shard_map/ppermute | solution.py:658
  95.7 15.4 %collective-permute-start.38 = (bf16[256,512]{1,0:T(8,128)(2,1)S(1)}, bf16[256,512]{1,0:T(8,128)(2,1)S(1)}, u32[]{:S(2)}, u32[]{:S(2)}) collective-permute-start(bf16[256,512]{1,0:T(8,128)(2,1)S(1)} %get-tuple-element.96), channel_id=1, source_target_pairs={{0,3},{1,0},{2,1},{3,2},{4,7},{5,4},{6,5},{7,6},{8,11},{9,8},{10,9... | collective-permute-start | bytes 786440 | tf_op jit(solution)/shard_map/ppermute | solution.py:658
  99.0 21.7 %copy-start.3 = (bf16[256,2048]{1,0:T(8,128)(2,1)S(1)}, bf16[256,2048]{1,0:T(8,128)(2,1)}, u32[]{:S(2)}) copy-start(bf16[256,2048]{1,0:T(8,128)(2,1)} %residual_ref.3) | copy-start | bytes 3145732
  99.0 14.5 %collective-permute-start.29 = (bf16[256,512]{1,0:T(8,128)(2,1)S(1)}, bf16[256,512]{1,0:T(8,128)(2,1)S(1)}, u32[]{:S(2)}, u32[]{:S(2)}) collective-permute-start(bf16[256,512]{1,0:T(8,128)(2,1)S(1)} %get-tuple-element.87), channel_id=1, source_target_pairs={{0,1},{1,2},{2,3},{3,0},{4,5},{5,6},{6,7},{7,4},{8,9},{9,10},{10,1... | collective-permute-start | bytes 786440 | tf_op jit(solution)/shard_map/ppermute | solution.py:658
  100.8 15.4 %collective-permute-start.30 = (bf16[256,512]{1,0:T(8,128)(2,1)S(1)}, bf16[256,512]{1,0:T(8,128)(2,1)S(1)}, u32[]{:S(2)}, u32[]{:S(2)}) collective-permute-start(bf16[256,512]{1,0:T(8,128)(2,1)S(1)} %get-tuple-element.88), channel_id=1, source_target_pairs={{0,2},{1,3},{2,0},{3,1},{4,6},{5,7},{6,4},{7,5},{8,10},{9,11},{10,... | collective-permute-start | bytes 786440 | tf_op jit(solution)/shard_map/ppermute | solution.py:658
  105.4 13.4 %collective-permute-start.31 = (bf16[256,512]{1,0:T(8,128)(2,1)S(1)}, bf16[256,512]{1,0:T(8,128)(2,1)S(1)}, u32[]{:S(2)}, u32[]{:S(2)}) collective-permute-start(bf16[256,512]{1,0:T(8,128)(2,1)S(1)} %get-tuple-element.89), channel_id=1, source_target_pairs={{0,3},{1,0},{2,1},{3,2},{4,7},{5,4},{6,5},{7,6},{8,11},{9,8},{10,9... | collective-permute-start | bytes 786440 | tf_op jit(solution)/shard_map/ppermute | solution.py:658
  111.3 8.0 %collective-permute-start.39 = (bf16[256,512]{1,0:T(8,128)(2,1)S(1)}, bf16[256,512]{1,0:T(8,128)(2,1)S(1)}, u32[]{:S(2)}, u32[]{:S(2)}) collective-permute-start(bf16[256,512]{1,0:T(8,128)(2,1)S(1)} %get-tuple-element.97), channel_id=1, source_target_pairs={{0,24},{8,0},{16,8},{24,16},{1,25},{9,1},{17,9},{25,17},{2,26},{10... | collective-permute-start | bytes 786440 | tf_op jit(solution)/shard_map/ppermute | solution.py:658
  113.1 7.6 %collective-permute-start.40 = (bf16[256,512]{1,0:T(8,128)(2,1)S(1)}, bf16[256,512]{1,0:T(8,128)(2,1)S(1)}, u32[]{:S(2)}, u32[]{:S(2)}) collective-permute-start(bf16[256,512]{1,0:T(8,128)(2,1)S(1)} %get-tuple-element.98), channel_id=1, source_target_pairs={{0,8},{8,16},{16,24},{24,0},{1,9},{9,17},{17,25},{25,1},{2,10},{10... | collective-permute-start | bytes 786440 | tf_op jit(solution)/shard_map/ppermute | solution.py:658
  118.9 9.2 %collective-permute-start.32 = (bf16[256,512]{1,0:T(8,128)(2,1)S(1)}, bf16[256,512]{1,0:T(8,128)(2,1)S(1)}, u32[]{:S(2)}, u32[]{:S(2)}) collective-permute-start(bf16[256,512]{1,0:T(8,128)(2,1)S(1)} %far_sums.1._), channel_id=1, source_target_pairs={{0,16},{8,24},{16,0},{24,8},{1,17},{9,25},{17,1},{25,9},{2,18},{10... | collective-permute-start | bytes 786440 | tf_op jit(solution)/shard_map/ppermute | solution.py:658
  (3 other events, 3.3 us)

commit v5 on v4

--- a/solution.py
+++ b/solution.py
@@ -78,23 +78,25 @@
     return block[0:1] + block[1:2] + block[2:3]
 
 
-def state_kernel(place, value_ref, write_ref, packed_ref, keep_ref, send_ref, state, logs):
+def state_kernel(place, value_ref, write_ref, packed_ref, keep_ref, send_ref):
     core = place[0]
     step, across = cumulate(packed_ref[...])
-    to_end = (jnp.exp(across[:, ROWS - 1 : ROWS] - across) * step).T
-    last = across.T[ROWS - 1 : ROWS]
+    to_end = jnp.exp(across[:, ROWS - 1 : ROWS] - across) * step
+    half = HEADS // 2
+    turned = lambda rows: jnp.where(
+        core == 0, rows, jnp.concatenate([rows[half:], rows[:half]], axis=0)
+    )
+    to_end = turned(to_end).T
+    last = turned(across).T[ROWS - 1 : ROWS]
     write = write_ref[...].T
     for head in range(HEADS):
-        at = slice(head * WIDTH, (head + 1) * WIDTH)
-        weighted = (value_ref[:, at].astype(F32) * to_end[:, head : head + 1]).astype(BF16)
-        state[:, at] = jnp.dot(write, weighted, preferred_element_type=F32)
-        logs[:, at] = jnp.broadcast_to(last[:, head : head + 1], (8, WIDTH))
-    mine = pl.ds(pl.multiple_of(core * SPLIT, SPLIT), SPLIT)
-    other = pl.ds(pl.multiple_of((1 - core) * SPLIT, SPLIT), SPLIT)
-    keep_ref[0:WIDTH, :] = state[:, mine]
-    keep_ref[WIDTH:, :] = logs[:, mine]
-    send_ref[0:WIDTH, :] = state[:, other]
-    send_ref[WIDTH:, :] = logs[:, other]
+        from_head = lax.rem(core * half + head, HEADS)
+        source = pl.ds(pl.multiple_of(from_head * WIDTH, WIDTH), WIDTH)
+        weighted = (value_ref[:, source].astype(F32) * to_end[:, head : head + 1]).astype(BF16)
+        out_ref = keep_ref if head < half else send_ref
+        at = slice(head % half * WIDTH, (head % half + 1) * WIDTH)
+        out_ref[0:WIDTH, at] = jnp.dot(write, weighted, preferred_element_type=F32)
+        out_ref[WIDTH:, at] = jnp.broadcast_to(last[:, head : head + 1], (8, WIDTH))
 
 
 def whole(shape):
@@ -108,7 +110,6 @@
         out_shape=[jax.ShapeDtypeStruct(shape, F32)] * 2,
         in_specs=[SMEM] + [VMEM] * 3,
         out_specs=[VMEM] * 2,
-        scratch_shapes=[pltpu.VMEM((WIDTH, LANES), F32), pltpu.VMEM((8, LANES), F32)],
         compiler_params=params(),
         cost_estimate=cost(2 * WIDTH * ROWS * LANES, 3 * 2**20),
         name="local_state",

time: 130 us -> 130 us (level)
  no operation moved by 1% of the time
where the time goes in v5:
time: 130 us; the launch traced here: 129 us
  starting transfers between devices  56.5 us (43%)
  waiting for transfers between devices  40.9 us (31%)
  Pallas kernels  26.7 us (21%)
  local copies, waits for them, and re-layouts  3.39 us (3%)
  other arithmetic  1.6 us (1%)
    ppermute x34, starting transfers between devices, shift(): return lax.ppermute(value, axis, [(i, (i + by) % 4) for i in range(4)])  55.3 us
    ppermute x34, waiting for transfers between devices, shift(): return lax.ppermute(value, axis, [(i, (i + by) % 4) for i in range(4)])  38.9 us
    pallas_call x3, Pallas kernels, project(): pl.pallas_call(functools.partial(project_kernel, tall, count, count - 3,...  8.94 us
    unnamed x20, local copies, waits for them, and re-layouts  3.32 us
    pallas_call x1, Pallas kernels, plain_part(): pl.pallas_call(plain_kernel, out_shape=(shape, shape), in_specs=[VMEM] *...  2.8 us
  transfers between devices with their start and end apart: 41, of which 17 were waited for; matrix products, arithmetic and copies ran while one was open for 1% of the time, Pallas kernels for 19%

profile of v5, /device:TPU:2, one launch (start us, length us, event | category | flops | bytes accessed | tf_op | source)
XLA Modules:
  0.0 129.3 jit_solution(16481709088503781466)
XLA Ops:
  0.0 1.9 %collective-permute-start.8 = (bf16[2048,256]{1,0:T(8,128)(2,1)}, bf16[2048,256]{1,0:T(8,128)(2,1)S(1)}, u32[]{:S(2)}, u32[]{:S(2)}) collective-permute-start(bf16[2048,256]{1,0:T(8,128)(2,1)} %refs_2_.5), channel_id=1, source_target_pairs={{0,32},{32,64},{64,96},{96,0},{1,33},{33,65},{65,97},{97,1},{2,34}... | collective-permute-start | bytes 3145736 | tf_op jit(solution)/shard_map/ppermute | solution.py:659
  1.9 2.2 %collective-permute-start.7 = (bf16[2048,256]{1,0:T(8,128)(2,1)}, bf16[2048,256]{1,0:T(8,128)(2,1)S(1)}, u32[]{:S(2)}, u32[]{:S(2)}) collective-permute-start(bf16[2048,256]{1,0:T(8,128)(2,1)} %refs_2_.5), channel_id=1, source_target_pairs={{0,96},{32,0},{64,32},{96,64},{1,97},{33,1},{65,33},{97,65},{2,98}... | collective-permute-start | bytes 3145736 | tf_op jit(solution)/shard_map/ppermute | solution.py:659
  7.8 2.3 %local_state.1 = (f32[136,1024]{1,0:T(8,128)S(1)}, f32[136,1024]{1,0:T(8,128)S(1)}) custom-call(s32[4]{0:T(128)S(1)} %pad_add_fusion.place, bf16[256,2048]{1,0:T(8,128)(2,1)S(1)} %copy-done.1, bf16[256,128]{1,0:T(8,128)(2,1)S(1)} %copy-done.7, f32[32,256]{1,0:T(8,128)S(1)} %pad_maximum_fusion.packed_ref), custom_call_target="tpu_custom_call" | custom-call | flops 134217728 | bytes 3145728 | tf_op jit(solution)/shard_map/local_state/pallas_call | solution.py:108
  10.2 1.9 %collective-permute-done.got_ref = f32[136,1024]{1,0:T(8,128)S(1)} collective-permute-done((f32[136,1024]{1,0:T(8,128)S(1)}, f32[136,1024]{1,0:T(8,128)S(1)}, u32[]{:S(2)}, u32[]{:S(2)}) %collective-permute-start) | collective-permute-done | bytes 557088 | tf_op jit(solution)/shard_map/ppermute | solution.py:663
  12.9 1.6 %collective-permute-start.1 = (bf16[144,256]{1,0:T(8,128)(2,1)S(1)}, bf16[144,256]{1,0:T(8,128)(2,1)S(1)}, u32[]{:S(2)}, u32[]{:S(2)}) collective-permute-start(bf16[144,256]{1,0:T(8,128)(2,1)S(1)} %get-tuple-element.56), channel_id=1, source_target_pairs={{0,8},{8,16},{16,24},{24,0},{1,9},{9,17},{17,25},{25,1},{2,10},{10... | collective-permute-start | bytes 221192 | tf_op jit(solution)/shard_map/ppermute | solution.py:659
  14.6 2.9 %collective-permute-start.2 = (bf16[144,256]{1,0:T(8,128)(2,1)S(1)}, bf16[144,256]{1,0:T(8,128)(2,1)S(1)}, u32[]{:S(2)}, u32[]{:S(2)}) collective-permute-start(bf16[144,256]{1,0:T(8,128)(2,1)S(1)} %get-tuple-element.57), channel_id=1, source_target_pairs={{0,16},{8,24},{16,0},{24,8},{1,17},{9,25},{17,1},{25,9},{2,18},{10... | collective-permute-start | bytes 221192 | tf_op jit(solution)/shard_map/ppermute | solution.py:659
  17.5 1.3 %collective-permute-start.3 = (bf16[144,256]{1,0:T(8,128)(2,1)S(1)}, bf16[144,256]{1,0:T(8,128)(2,1)S(1)}, u32[]{:S(2)}, u32[]{:S(2)}) collective-permute-start(bf16[144,256]{1,0:T(8,128)(2,1)S(1)} %get-tuple-element.58), channel_id=1, source_target_pairs={{0,24},{8,0},{16,8},{24,16},{1,25},{9,1},{17,9},{25,17},{2,26},{10... | collective-permute-start | bytes 221192 | tf_op jit(solution)/shard_map/ppermute | solution.py:659
  20.9 2.8 %plain_part.1 = (f32[256,2048]{1,0:T(8,128)S(1)}, f32[256,2048]{1,0:T(8,128)S(1)}) custom-call(bf16[256,2048]{1,0:T(8,128)(2,1)S(1)} %copy-done.2, bf16[256,2048]{1,0:T(8,128)(2,1)S(1)} %copy-done.4, bf16[256,128]{1,0:T(8,128)(2,1)S(1)} %copy-done.7, bf16[256,128]{1,0:T(8,128)(2,1)S(1)} %copy-done.6, f32[32,256]{1,0:T(8,128)S(1)} %pad_maximum_fusion.packed_ref, ...), custom_call_target="tpu_custom_call" | custom-call | flops 268435456 | bytes 7340032 | tf_op jit(solution)/shard_map/plain_part/pallas_call | solution.py:144
  24.6 2.0 %collective-permute-start.6 = (bf16[144,256]{1,0:T(8,128)(2,1)S(1)}, bf16[144,256]{1,0:T(8,128)(2,1)S(1)}, u32[]{:S(2)}, u32[]{:S(2)}) collective-permute-start(bf16[144,256]{1,0:T(8,128)(2,1)S(1)} %get-tuple-element.60.p0), channel_id=1, source_target_pairs={{0,96},{32,0},{64,32},{96,64},{1,97},{33,1},{65,33},{97,65},{2,98}... | collective-permute-start | bytes 221192 | tf_op jit(solution)/shard_map/ppermute | solution.py:659
  27.9 2.0 %collective-permute-done.6.p3 = bf16[144,256]{1,0:T(8,128)(2,1)S(1)} collective-permute-done((bf16[144,256]{1,0:T(8,128)(2,1)S(1)}, bf16[144,256]{1,0:T(8,128)(2,1)S(1)}, u32[]{:S(2)}, u32[]{:S(2)}) %collective-permute-start.6) | collective-permute-done | bytes 73760 | tf_op jit(solution)/shard_map/ppermute | solution.py:659
  29.9 2.7 %collective-permute-done.5.p2 = bf16[144,256]{1,0:T(8,128)(2,1)S(1)} collective-permute-done((bf16[144,256]{1,0:T(8,128)(2,1)S(1)}, bf16[144,256]{1,0:T(8,128)(2,1)S(1)}, u32[]{:S(2)}, u32[]{:S(2)}) %collective-permute-start.5) | collective-permute-done | bytes 73760 | tf_op jit(solution)/shard_map/ppermute | solution.py:659
  35.0 1.8 %collective-permute-start.10 = (bf16[128,256]{1,0:T(8,128)(2,1)S(1)}, bf16[128,256]{1,0:T(8,128)(2,1)S(1)}, u32[]{:S(2)}, u32[]{:S(2)}) collective-permute-start(bf16[128,256]{1,0:T(8,128)(2,1)S(1)} %get-tuple-element.64), channel_id=1, source_target_pairs={{0,16},{8,24},{16,0},{24,8},{1,17},{9,25},{17,1},{25,9},{2,18},{10... | collective-permute-start | bytes 196616 | tf_op jit(solution)/shard_map/ppermute | solution.py:659
  36.8 1.3 %collective-permute-start.11 = (bf16[128,256]{1,0:T(8,128)(2,1)S(1)}, bf16[128,256]{1,0:T(8,128)(2,1)S(1)}, u32[]{:S(2)}, u32[]{:S(2)}) collective-permute-start(bf16[128,256]{1,0:T(8,128)(2,1)S(1)} %get-tuple-element.65), channel_id=1, source_target_pairs={{0,24},{8,0},{16,8},{24,16},{1,25},{9,1},{17,9},{25,17},{2,26},{10... | collective-permute-start | bytes 196616 | tf_op jit(solution)/shard_map/ppermute | solution.py:659
  38.1 2.9 %collective-permute-done.9.p1 = bf16[128,256]{1,0:T(8,128)(2,1)S(1)} collective-permute-done((bf16[128,256]{1,0:T(8,128)(2,1)S(1)}, bf16[128,256]{1,0:T(8,128)(2,1)S(1)}, u32[]{:S(2)}, u32[]{:S(2)}) %collective-permute-start.9) | collective-permute-done | bytes 65568 | tf_op jit(solution)/shard_map/ppermute | solution.py:659
  42.6 1.5 %collective-permute-start.20 = (bf16[1024,256]{1,0:T(8,128)(2,1)S(1)}, bf16[1024,256]{1,0:T(8,128)(2,1)S(1)}, u32[]{:S(2)}, u32[]{:S(2)}) collective-permute-start(bf16[1024,256]{1,0:T(8,128)(2,1)S(1)} %slice.8), channel_id=1, source_target_pairs={{0,32},{32,64},{64,96},{96,0},{1,33},{33,65},{65,97},{97,1},{2,34}... | collective-permute-start | bytes 1572872 | tf_op jit(solution)/shard_map/ppermute | solution.py:659
  44.1 1.8 %collective-permute-start.21 = (bf16[1024,256]{1,0:T(8,128)(2,1)S(1)}, bf16[1024,256]{1,0:T(8,128)(2,1)S(1)}, u32[]{:S(2)}, u32[]{:S(2)}) collective-permute-start(bf16[1024,256]{1,0:T(8,128)(2,1)S(1)} %slice.9), channel_id=1, source_target_pairs={{0,96},{32,0},{64,32},{96,64},{1,97},{33,1},{65,33},{97,65},{2,98}... | collective-permute-start | bytes 1572872 | tf_op jit(solution)/shard_map/ppermute | solution.py:659
  46.0 1.3 gated_part.1
  47.2 2.7 %collective-permute-start.17 = (bf16[128,2048]{1,0:T(8,128)(2,1)S(1)}, bf16[128,2048]{1,0:T(8,128)(2,1)S(1)}, u32[]{:S(2)}, u32[]{:S(2)}) collective-permute-start(bf16[128,2048]{1,0:T(8,128)(2,1)S(1)} %get-tuple-element.71.top_ref), channel_id=1, source_target_pairs={{0,24},{8,0},{16,8},{24,16},{1,25},{9,1},{17,9},{25,17},{2,26},{10... | collective-permute-start | bytes 1572872 | tf_op jit(solution)/shard_map/ppermute | solution.py:659
  50.0 1.8 %project_near.1.refs_4_ = bf16[3,2,256,256]{3,2,1,0:T(8,128)(2,1)S(1)} custom-call(bf16[128,2048]{1,0:T(8,128)(2,1)S(1)} %get-tuple-element.71.top_ref, bf16[128,2048]{1,0:T(8,128)(2,1)S(1)} %get-tuple-element.73.low_ref, bf16[2048,256]{1,0:T(8,128)(2,1)S(1)} %copy-done, bf16[2048,256]{1,0:T(8,128)(2,1)S(1)} %collective-permute-done.7.refs_0_.refs_1_.refs_3_, ...), custom_call_target="tpu_custom_call" | custom-call | flops 1610612736 | bytes 8388608 | tf_op jit(solution)/shard_map/project_near/pallas_call | solution.py:481
  51.8 6.4 %collective-permute-done.20.refs_5_.refs_0_ = bf16[1024,256]{1,0:T(8,128)(2,1)S(1)} collective-permute-done((bf16[1024,256]{1,0:T(8,128)(2,1)S(1)}, bf16[1024,256]{1,0:T(8,128)(2,1)S(1)}, u32[]{:S(2)}, u32[]{:S(2)}) %collective-permute-start.20) | collective-permute-done | bytes 524320 | tf_op jit(solution)/shard_map/ppermute | solution.py:659
  58.8 2.5 %collective-permute-done.17.refs_1_ = bf16[128,2048]{1,0:T(8,128)(2,1)S(1)} collective-permute-done((bf16[128,2048]{1,0:T(8,128)(2,1)S(1)}, bf16[128,2048]{1,0:T(8,128)(2,1)S(1)}, u32[]{:S(2)}, u32[]{:S(2)}) %collective-permute-start.17) | collective-permute-done | bytes 524320 | tf_op jit(solution)/shard_map/ppermute | solution.py:659
  61.3 3.4 %collective-permute-done.16.refs_0_ = bf16[128,2048]{1,0:T(8,128)(2,1)S(1)} collective-permute-done((bf16[128,2048]{1,0:T(8,128)(2,1)S(1)}, bf16[128,2048]{1,0:T(8,128)(2,1)S(1)}, u32[]{:S(2)}, u32[]{:S(2)}) %collective-permute-start.16) | collective-permute-done | bytes 524320 | tf_op jit(solution)/shard_map/ppermute | solution.py:659
  64.7 3.2 %collective-permute-start.18 = (bf16[128,2048]{1,0:T(8,128)(2,1)S(1)}, bf16[128,2048]{1,0:T(8,128)(2,1)S(1)}, u32[]{:S(2)}, u32[]{:S(2)}) collective-permute-start(bf16[128,2048]{1,0:T(8,128)(2,1)S(1)} %get-tuple-element.73.low_ref), channel_id=1, source_target_pairs={{0,24},{8,0},{16,8},{24,16},{1,25},{9,1},{17,9},{25,17},{2,26},{10... | collective-permute-start | bytes 1572872 | tf_op jit(solution)/shard_map/ppermute | solution.py:659
  67.9 1.4 %project_far.1 = (bf16[272,512]{1,0:T(8,128)(2,1)S(1)}, bf16[272,512]{1,0:T(8,128)(2,1)S(1)}, bf16[272,512]{1,0:T(8,128)(2,1)S(1)}, bf16[272,512]{1,0:T(8,128)(2,1)S(1)}) custom-call(s32[4]{0:T(128)S(1)} %pad_add_fusion.place, bf16[128,2048]{1,0:T(8,128)(2,1)S(1)} %get-tuple-element.71.top_ref, bf16[128,2048]{1,0:T(8,128)(2,1)S(1)} %get-tuple-element.73.low_ref, ...), custom_call_target="tpu_custom_call" | custom-call | flops 536870912 | bytes 4194304 | tf_op jit(solution)/shard_map/project_far/pallas_call | solution.py:505
  69.3 1.6 %collective-permute-start.26 = (bf16[272,512]{1,0:T(8,128)(2,1)S(1)}, bf16[272,512]{1,0:T(8,128)(2,1)S(1)}, u32[]{:S(2)}, u32[]{:S(2)}) collective-permute-start(bf16[272,512]{1,0:T(8,128)(2,1)S(1)} %get-tuple-element.82), channel_id=1, source_target_pairs={{0,1},{1,2},{2,3},{3,0},{4,5},{5,6},{6,7},{7,4},{8,9},{9,10},{10,1... | collective-permute-start | bytes 835592 | tf_op jit(solution)/shard_map/ppermute | solution.py:659
  72.0 2.2 %collective-permute-start.28 = (bf16[272,512]{1,0:T(8,128)(2,1)S(1)}, bf16[272,512]{1,0:T(8,128)(2,1)S(1)}, u32[]{:S(2)}, u32[]{:S(2)}) collective-permute-start(bf16[272,512]{1,0:T(8,128)(2,1)S(1)} %get-tuple-element.84), channel_id=1, source_target_pairs={{0,3},{1,0},{2,1},{3,2},{4,7},{5,4},{6,5},{7,6},{8,11},{9,8},{10,9... | collective-permute-start | bytes 835592 | tf_op jit(solution)/shard_map/ppermute | solution.py:659
  74.1 3.0 %project.3 = (bf16[256,512]{1,0:T(8,128)(2,1)S(1)}, bf16[256,512]{1,0:T(8,128)(2,1)S(1)}, bf16[256,512]{1,0:T(8,128)(2,1)S(1)}, bf16[256,512]{1,0:T(8,128)(2,1)S(1)}) custom-call(s32[4]{0:T(128)S(1)} %pad_add_fusion.place, bf16[128,2048]{1,0:T(8,128)(2,1)S(1)} %collective-permute-done.16.refs_0_, bf16[128,2048]{1,0:T(8,128)(2,1)S(1)} %collective-permute-done.17.refs_1_, ...), custom_call_target="tpu_custom_call" | custom-call | flops 2147483648 | bytes 10485760 | tf_op jit(solution)/shard_map/project/pallas_call | solution.py:441
  77.1 1.3 %collective-permute-done.19.refs_0_ = bf16[128,2048]{1,0:T(8,128)(2,1)S(1)} collective-permute-done((bf16[128,2048]{1,0:T(8,128)(2,1)S(1)}, bf16[128,2048]{1,0:T(8,128)(2,1)S(1)}, u32[]{:S(2)}, u32[]{:S(2)}) %collective-permute-start.19) | collective-permute-done | bytes 524320 | tf_op jit(solution)/shard_map/ppermute | solution.py:659
  78.5 3.2 %collective-permute-start.25 = (bf16[128,2048]{1,0:T(8,128)(2,1)S(1)}, bf16[128,2048]{1,0:T(8,128)(2,1)S(1)}, u32[]{:S(2)}, u32[]{:S(2)}) collective-permute-start(bf16[128,2048]{1,0:T(8,128)(2,1)S(1)} %collective-permute-done.18.refs_1_), channel_id=1, source_target_pairs={{0,24},{8,0},{16,8},{24,16},{1,25},{9,1},{17,9},{25,17},{2,26},{10... | collective-permute-start | bytes 1572872 | tf_op jit(solution)/shard_map/ppermute | solution.py:659
  81.7 1.5 %collective-permute-start.33 = (bf16[256,512]{1,0:T(8,128)(2,1)S(1)}, bf16[256,512]{1,0:T(8,128)(2,1)S(1)}, u32[]{:S(2)}, u32[]{:S(2)}) collective-permute-start(bf16[256,512]{1,0:T(8,128)(2,1)S(1)} %get-tuple-element.91), channel_id=1, source_target_pairs={{0,1},{1,2},{2,3},{3,0},{4,5},{5,6},{6,7},{7,4},{8,9},{9,10},{10,1... | collective-permute-start | bytes 786440 | tf_op jit(solution)/shard_map/ppermute | solution.py:659
  84.3 2.2 %collective-permute-start.35 = (bf16[256,512]{1,0:T(8,128)(2,1)S(1)}, bf16[256,512]{1,0:T(8,128)(2,1)S(1)}, u32[]{:S(2)}, u32[]{:S(2)}) collective-permute-start(bf16[256,512]{1,0:T(8,128)(2,1)S(1)} %get-tuple-element.93), channel_id=1, source_target_pairs={{0,3},{1,0},{2,1},{3,2},{4,7},{5,4},{6,5},{7,6},{8,11},{9,8},{10,9... | collective-permute-start | bytes 786440 | tf_op jit(solution)/shard_map/ppermute | solution.py:659
  86.5 3.0 %project.4 = (bf16[256,512]{1,0:T(8,128)(2,1)S(1)}, bf16[256,512]{1,0:T(8,128)(2,1)S(1)}, bf16[256,512]{1,0:T(8,128)(2,1)S(1)}, bf16[256,512]{1,0:T(8,128)(2,1)S(1)}) custom-call(s32[4]{0:T(128)S(1)} %pad_add_fusion.place, bf16[128,2048]{1,0:T(8,128)(2,1)S(1)} %collective-permute-done.19.refs_0_, bf16[128,2048]{1,0:T(8,128)(2,1)S(1)} %collective-permute-done.18.refs_1_, ...), custom_call_target="tpu_custom_call" | custom-call | flops 2147483648 | bytes 10485760 | tf_op jit(solution)/shard_map/project/pallas_call | solution.py:441
  89.5 1.4 %collective-permute-done.33.refs_1_ = bf16[256,512]{1,0:T(8,128)(2,1)S(1)} collective-permute-done((bf16[256,512]{1,0:T(8,128)(2,1)S(1)}, bf16[256,512]{1,0:T(8,128)(2,1)S(1)}, u32[]{:S(2)}, u32[]{:S(2)}) %collective-permute-start.33) | collective-permute-done | bytes 262176 | tf_op jit(solution)/shard_map/ppermute | solution.py:659
  90.8 2.4 %collective-permute-start.36 = (bf16[256,512]{1,0:T(8,128)(2,1)S(1)}, bf16[256,512]{1,0:T(8,128)(2,1)S(1)}, u32[]{:S(2)}, u32[]{:S(2)}) collective-permute-start(bf16[256,512]{1,0:T(8,128)(2,1)S(1)} %get-tuple-element.94), channel_id=1, source_target_pairs={{0,1},{1,2},{2,3},{3,0},{4,5},{5,6},{6,7},{7,4},{8,9},{9,10},{10,1... | collective-permute-start | bytes 786440 | tf_op jit(solution)/shard_map/ppermute | solution.py:659
  93.3 2.2 %collective-permute-start.37 = (bf16[256,512]{1,0:T(8,128)(2,1)S(1)}, bf16[256,512]{1,0:T(8,128)(2,1)S(1)}, u32[]{:S(2)}, u32[]{:S(2)}) collective-permute-start(bf16[256,512]{1,0:T(8,128)(2,1)S(1)} %get-tuple-element.95), channel_id=1, source_target_pairs={{0,2},{1,3},{2,0},{3,1},{4,6},{5,7},{6,4},{7,5},{8,10},{9,11},{10,... | collective-permute-start | bytes 786440 | tf_op jit(solution)/shard_map/ppermute | solution.py:659
  95.7 3.0 %project.5 = (bf16[256,512]{1,0:T(8,128)(2,1)S(1)}, bf16[256,512]{1,0:T(8,128)(2,1)S(1)}, bf16[256,512]{1,0:T(8,128)(2,1)S(1)}, bf16[256,512]{1,0:T(8,128)(2,1)S(1)}) custom-call(s32[4]{0:T(128)S(1)} %pad_add_fusion.place, bf16[128,2048]{1,0:T(8,128)(2,1)S(1)} %collective-permute-done.24.refs_0_, bf16[128,2048]{1,0:T(8,128)(2,1)S(1)} %collective-permute-done.25.refs_1_, ...), custom_call_target="tpu_custom_call" | custom-call | flops 2147483648 | bytes 10485760 | tf_op jit(solution)/shard_map/project/pallas_call | solution.py:441
  98.7 1.8 %collective-permute-start.29 = (bf16[256,512]{1,0:T(8,128)(2,1)S(1)}, bf16[256,512]{1,0:T(8,128)(2,1)S(1)}, u32[]{:S(2)}, u32[]{:S(2)}) collective-permute-start(bf16[256,512]{1,0:T(8,128)(2,1)S(1)} %get-tuple-element.87), channel_id=1, source_target_pairs={{0,1},{1,2},{2,3},{3,0},{4,5},{5,6},{6,7},{7,4},{8,9},{9,10},{10,1... | collective-permute-start | bytes 786440 | tf_op jit(solution)/shard_map/ppermute | solution.py:659
  100.5 2.6 %collective-permute-start.30 = (bf16[256,512]{1,0:T(8,128)(2,1)S(1)}, bf16[256,512]{1,0:T(8,128)(2,1)S(1)}, u32[]{:S(2)}, u32[]{:S(2)}) collective-permute-start(bf16[256,512]{1,0:T(8,128)(2,1)S(1)} %get-tuple-element.88), channel_id=1, source_target_pairs={{0,2},{1,3},{2,0},{3,1},{4,6},{5,7},{6,4},{7,5},{8,10},{9,11},{10,... | collective-permute-start | bytes 786440 | tf_op jit(solution)/shard_map/ppermute | solution.py:659
  103.1 2.1 %collective-permute-done.36.refs_5_ = bf16[256,512]{1,0:T(8,128)(2,1)S(1)} collective-permute-done((bf16[256,512]{1,0:T(8,128)(2,1)S(1)}, bf16[256,512]{1,0:T(8,128)(2,1)S(1)}, u32[]{:S(2)}, u32[]{:S(2)}) %collective-permute-start.36) | collective-permute-done | bytes 262176 | tf_op jit(solution)/shard_map/ppermute | solution.py:659
  105.2 4.3 %collective-permute-start.31 = (bf16[256,512]{1,0:T(8,128)(2,1)S(1)}, bf16[256,512]{1,0:T(8,128)(2,1)S(1)}, u32[]{:S(2)}, u32[]{:S(2)}) collective-permute-start(bf16[256,512]{1,0:T(8,128)(2,1)S(1)} %get-tuple-element.89), channel_id=1, source_target_pairs={{0,3},{1,0},{2,1},{3,2},{4,7},{5,4},{6,5},{7,6},{8,11},{9,8},{10,9... | collective-permute-start | bytes 786440 | tf_op jit(solution)/shard_map/ppermute | solution.py:659
  109.5 1.3 %collective-permute-done.38.refs_7_ = bf16[256,512]{1,0:T(8,128)(2,1)S(1)} collective-permute-done((bf16[256,512]{1,0:T(8,128)(2,1)S(1)}, bf16[256,512]{1,0:T(8,128)(2,1)S(1)}, u32[]{:S(2)}, u32[]{:S(2)}) %collective-permute-start.38) | collective-permute-done | bytes 262176 | tf_op jit(solution)/shard_map/ppermute | solution.py:659
  111.1 1.7 %collective-permute-start.39 = (bf16[256,512]{1,0:T(8,128)(2,1)S(1)}, bf16[256,512]{1,0:T(8,128)(2,1)S(1)}, u32[]{:S(2)}, u32[]{:S(2)}) collective-permute-start(bf16[256,512]{1,0:T(8,128)(2,1)S(1)} %get-tuple-element.97), channel_id=1, source_target_pairs={{0,24},{8,0},{16,8},{24,16},{1,25},{9,1},{17,9},{25,17},{2,26},{10... | collective-permute-start | bytes 786440 | tf_op jit(solution)/shard_map/ppermute | solution.py:659
  113.2 2.8 %collective-permute-done.30.refs_2_ = bf16[256,512]{1,0:T(8,128)(2,1)S(1)} collective-permute-done((bf16[256,512]{1,0:T(8,128)(2,1)S(1)}, bf16[256,512]{1,0:T(8,128)(2,1)S(1)}, u32[]{:S(2)}, u32[]{:S(2)}) %collective-permute-start.30) | collective-permute-done | bytes 262176 | tf_op jit(solution)/shard_map/ppermute | solution.py:659
  116.0 2.6 %collective-permute-done.31.refs_3_ = bf16[256,512]{1,0:T(8,128)(2,1)S(1)} collective-permute-done((bf16[256,512]{1,0:T(8,128)(2,1)S(1)}, bf16[256,512]{1,0:T(8,128)(2,1)S(1)}, u32[]{:S(2)}, u32[]{:S(2)}) %collective-permute-start.31) | collective-permute-done | bytes 262176 | tf_op jit(solution)/shard_map/ppermute | solution.py:659
  119.0 1.4 %collective-permute-done.40.down_ref = bf16[256,512]{1,0:T(8,128)(2,1)S(1)} collective-permute-done((bf16[256,512]{1,0:T(8,128)(2,1)S(1)}, bf16[256,512]{1,0:T(8,128)(2,1)S(1)}, u32[]{:S(2)}, u32[]{:S(2)}) %collective-permute-start.40) | collective-permute-done | bytes 262176 | tf_op jit(solution)/shard_map/ppermute | solution.py:659
  120.4 2.4 %finish.1 = (bf16[256,2048]{1,0:T(8,128)(2,1)}, f32[256,128]{1,0:T(8,128)S(1)}) custom-call(s32[4]{0:T(128)S(1)} %pad_add_fusion.place, bf16[272,512]{1,0:T(8,128)(2,1)S(1)} %get-tuple-element.90.p0, bf16[272,512]{1,0:T(8,128)(2,1)S(1)} %collective-permute-done.26.refs_12_.p1, bf16[272,512]{1,0:T(8,128)(2,1)S(1)} %collective-permute-done.27.refs_13_.p2, ...), custom_call_target="tpu_custom_call" | custom-call | flops 1572864 | bytes 3145728 | tf_op jit(solution)/shard_map/finish/pallas_call | solution.py:621
  122.8 5.1 %collective-permute-done.32.far_ref = bf16[256,512]{1,0:T(8,128)(2,1)S(1)} collective-permute-done((bf16[256,512]{1,0:T(8,128)(2,1)S(1)}, bf16[256,512]{1,0:T(8,128)(2,1)S(1)}, u32[]{:S(2)}, u32[]{:S(2)}) %collective-permute-start.32) | collective-permute-done | bytes 262176 | tf_op jit(solution)/shard_map/ppermute | solution.py:659
  127.9 1.4 %finish_far.1 = bf16[256,2048]{1,0:T(8,128)(2,1)} custom-call(s32[4]{0:T(128)S(1)} %pad_add_fusion.place, bf16[256,512]{1,0:T(8,128)(2,1)S(1)} %collective-permute-done.32.far_ref, f32[256,128]{1,0:T(8,128)S(1)} %get-tuple-element.99.scale_ref, bf16[256,2048]{1,0:T(8,128)(2,1)S(1)} %copy-done.3, ...), custom_call_target="tpu_custom_call", output_to_operand_aliasing={{}: (4, {})} | custom-call | flops 524288 | bytes 1048576 | tf_op jit(solution)/shard_map/finish_far/pallas_call | solution.py:642
  (76 shorter events, 16.8 us)
Async XLA Ops:
  0.0 20.9 %copy-start.6 = (bf16[256,128]{1,0:T(8,128)(2,1)S(1)}, bf16[256,128]{1,0:T(8,128)(2,1)}, u32[]{:S(2)}) copy-start(bf16[256,128]{1,0:T(8,128)(2,1)} %read_ref.3) | copy-start | bytes 196612
  0.0 20.9 %copy-start.9 = (f32[16]{0:T(128)S(1)}, f32[16]{0:T(128)}, u32[]{:S(2)}) copy-start(f32[16]{0:T(128)} %param.17) | copy-start | bytes 196
  0.0 33.0 %collective-permute-start.8 = (bf16[2048,256]{1,0:T(8,128)(2,1)}, bf16[2048,256]{1,0:T(8,128)(2,1)S(1)}, u32[]{:S(2)}, u32[]{:S(2)}) collective-permute-start(bf16[2048,256]{1,0:T(8,128)(2,1)} %refs_2_.5), channel_id=1, source_target_pairs={{0,32},{32,64},{64,96},{96,0},{1,33},{33,65},{65,97},{97,1},{2,34}... | collective-permute-start | bytes 3145736 | tf_op jit(solution)/shard_map/ppermute | solution.py:659
  1.9 31.1 %collective-permute-start.7 = (bf16[2048,256]{1,0:T(8,128)(2,1)}, bf16[2048,256]{1,0:T(8,128)(2,1)S(1)}, u32[]{:S(2)}, u32[]{:S(2)}) collective-permute-start(bf16[2048,256]{1,0:T(8,128)(2,1)} %refs_2_.5), channel_id=1, source_target_pairs={{0,96},{32,0},{64,32},{96,64},{1,97},{33,1},{65,33},{97,65},{2,98}... | collective-permute-start | bytes 3145736 | tf_op jit(solution)/shard_map/ppermute | solution.py:659
  7.8 13.1 %copy-start.2 = (bf16[256,2048]{1,0:T(8,128)(2,1)S(1)}, bf16[256,2048]{1,0:T(8,128)(2,1)}, u32[]{:S(2)}) copy-start(bf16[256,2048]{1,0:T(8,128)(2,1)} %value_ref.3) | copy-start | bytes 3145732
  7.8 13.1 %copy-start.4 = (bf16[256,2048]{1,0:T(8,128)(2,1)S(1)}, bf16[256,2048]{1,0:T(8,128)(2,1)}, u32[]{:S(2)}) copy-start(bf16[256,2048]{1,0:T(8,128)(2,1)} %gate_ref.1) | copy-start | bytes 3145732
  10.1 2.0 %collective-permute-start = (f32[136,1024]{1,0:T(8,128)S(1)}, f32[136,1024]{1,0:T(8,128)S(1)}, u32[]{:S(2)}, u32[]{:S(2)}) collective-permute-start(f32[136,1024]{1,0:T(8,128)S(1)} %get-tuple-element.54), channel_id=1, source_target_pairs={{0,4},{4,0},{1,5},{5,1},{2,6},{6,2},{3,7},{7,3},{8,12},{12,8},{9,1... | collective-permute-start | bytes 1671176 | tf_op jit(solution)/shard_map/ppermute | solution.py:663
  12.9 10.8 %collective-permute-start.1 = (bf16[144,256]{1,0:T(8,128)(2,1)S(1)}, bf16[144,256]{1,0:T(8,128)(2,1)S(1)}, u32[]{:S(2)}, u32[]{:S(2)}) collective-permute-start(bf16[144,256]{1,0:T(8,128)(2,1)S(1)} %get-tuple-element.56), channel_id=1, source_target_pairs={{0,8},{8,16},{16,24},{24,0},{1,9},{9,17},{17,25},{25,1},{2,10},{10... | collective-permute-start | bytes 221192 | tf_op jit(solution)/shard_map/ppermute | solution.py:659
  14.6 9.2 %collective-permute-start.2 = (bf16[144,256]{1,0:T(8,128)(2,1)S(1)}, bf16[144,256]{1,0:T(8,128)(2,1)S(1)}, u32[]{:S(2)}, u32[]{:S(2)}) collective-permute-start(bf16[144,256]{1,0:T(8,128)(2,1)S(1)} %get-tuple-element.57), channel_id=1, source_target_pairs={{0,16},{8,24},{16,0},{24,8},{1,17},{9,25},{17,1},{25,9},{2,18},{10... | collective-permute-start | bytes 221192 | tf_op jit(solution)/shard_map/ppermute | solution.py:659
  17.5 6.3 %collective-permute-start.3 = (bf16[144,256]{1,0:T(8,128)(2,1)S(1)}, bf16[144,256]{1,0:T(8,128)(2,1)S(1)}, u32[]{:S(2)}, u32[]{:S(2)}) collective-permute-start(bf16[144,256]{1,0:T(8,128)(2,1)S(1)} %get-tuple-element.58), channel_id=1, source_target_pairs={{0,24},{8,0},{16,8},{24,16},{1,25},{9,1},{17,9},{25,17},{2,26},{10... | collective-permute-start | bytes 221192 | tf_op jit(solution)/shard_map/ppermute | solution.py:659
  20.9 9.0 %copy-start = (bf16[2048,256]{1,0:T(8,128)(2,1)S(1)}, bf16[2048,256]{1,0:T(8,128)(2,1)}, u32[]{:S(2)}) copy-start(bf16[2048,256]{1,0:T(8,128)(2,1)} %refs_2_.5) | copy-start | bytes 3145732
  24.6 5.3 %collective-permute-start.6 = (bf16[144,256]{1,0:T(8,128)(2,1)S(1)}, bf16[144,256]{1,0:T(8,128)(2,1)S(1)}, u32[]{:S(2)}, u32[]{:S(2)}) collective-permute-start(bf16[144,256]{1,0:T(8,128)(2,1)S(1)} %get-tuple-element.60.p0), channel_id=1, source_target_pairs={{0,96},{32,0},{64,32},{96,64},{1,97},{33,1},{65,33},{97,65},{2,98}... | collective-permute-start | bytes 221192 | tf_op jit(solution)/shard_map/ppermute | solution.py:659
  26.7 6.0 %collective-permute-start.5 = (bf16[144,256]{1,0:T(8,128)(2,1)S(1)}, bf16[144,256]{1,0:T(8,128)(2,1)S(1)}, u32[]{:S(2)}, u32[]{:S(2)}) collective-permute-start(bf16[144,256]{1,0:T(8,128)(2,1)S(1)} %get-tuple-element.60.p0), channel_id=1, source_target_pairs={{0,64},{32,96},{64,0},{96,32},{1,65},{33,97},{65,1},{97,33},{2,66}... | collective-permute-start | bytes 221192 | tf_op jit(solution)/shard_map/ppermute | solution.py:659
  26.7 6.4 %collective-permute-start.4 = (bf16[144,256]{1,0:T(8,128)(2,1)S(1)}, bf16[144,256]{1,0:T(8,128)(2,1)S(1)}, u32[]{:S(2)}, u32[]{:S(2)}) collective-permute-start(bf16[144,256]{1,0:T(8,128)(2,1)S(1)} %get-tuple-element.60.p0), channel_id=1, source_target_pairs={{0,32},{32,64},{64,96},{96,0},{1,33},{33,65},{65,97},{97,1},{2,34}... | collective-permute-start | bytes 221192 | tf_op jit(solution)/shard_map/ppermute | solution.py:659
  29.9 6.9 %collective-permute-start.12 = (bf16[2048,256]{1,0:T(8,128)(2,1)S(1)}, bf16[2048,256]{1,0:T(8,128)(2,1)S(1)}, u32[]{:S(2)}, u32[]{:S(2)}) collective-permute-start(bf16[2048,256]{1,0:T(8,128)(2,1)S(1)} %copy-done), channel_id=1, source_target_pairs={{0,4},{4,0},{1,5},{5,1},{2,6},{6,2},{3,7},{7,3},{8,12},{12,8},{9,1... | collective-permute-start | bytes 3145736 | tf_op jit(solution)/shard_map/ppermute | solution.py:663
  33.0 8.5 %collective-permute-start.13 = (bf16[2048,256]{1,0:T(8,128)(2,1)S(1)}, bf16[2048,256]{1,0:T(8,128)(2,1)S(1)}, u32[]{:S(2)}, u32[]{:S(2)}) collective-permute-start(bf16[2048,256]{1,0:T(8,128)(2,1)S(1)} %collective-permute-done.7.refs_0_.refs_1_.refs_3_), channel_id=1, source_target_pairs={{0,4},{4,0},{1,5},{5,1},{2,6},{6,2},{3,7},{7,3},{8,12},{12,8},{9,1... | collective-permute-start | bytes 3145736 | tf_op jit(solution)/shard_map/ppermute | solution.py:663
  33.0 8.5 %collective-permute-start.14 = (bf16[2048,256]{1,0:T(8,128)(2,1)S(1)}, bf16[2048,256]{1,0:T(8,128)(2,1)S(1)}, u32[]{:S(2)}, u32[]{:S(2)}) collective-permute-start(bf16[2048,256]{1,0:T(8,128)(2,1)S(1)} %collective-permute-done.8.refs_1_.refs_2_.refs_4_), channel_id=1, source_target_pairs={{0,4},{4,0},{1,5},{5,1},{2,6},{6,2},{3,7},{7,3},{8,12},{12,8},{9,1... | collective-permute-start | bytes 3145736 | tf_op jit(solution)/shard_map/ppermute | solution.py:663
  34.2 6.8 %collective-permute-start.9 = (bf16[128,256]{1,0:T(8,128)(2,1)S(1)}, bf16[128,256]{1,0:T(8,128)(2,1)S(1)}, u32[]{:S(2)}, u32[]{:S(2)}) collective-permute-start(bf16[128,256]{1,0:T(8,128)(2,1)S(1)} %get-tuple-element.63), channel_id=1, source_target_pairs={{0,8},{8,16},{16,24},{24,0},{1,9},{9,17},{17,25},{25,1},{2,10},{10... | collective-permute-start | bytes 196616 | tf_op jit(solution)/shard_map/ppermute | solution.py:659
  35.0 6.1 %collective-permute-start.10 = (bf16[128,256]{1,0:T(8,128)(2,1)S(1)}, bf16[128,256]{1,0:T(8,128)(2,1)S(1)}, u32[]{:S(2)}, u32[]{:S(2)}) collective-permute-start(bf16[128,256]{1,0:T(8,128)(2,1)S(1)} %get-tuple-element.64), channel_id=1, source_target_pairs={{0,16},{8,24},{16,0},{24,8},{1,17},{9,25},{17,1},{25,9},{2,18},{10... | collective-permute-start | bytes 196616 | tf_op jit(solution)/shard_map/ppermute | solution.py:659
  36.8 4.8 %collective-permute-start.11 = (bf16[128,256]{1,0:T(8,128)(2,1)S(1)}, bf16[128,256]{1,0:T(8,128)(2,1)S(1)}, u32[]{:S(2)}, u32[]{:S(2)}) collective-permute-start(bf16[128,256]{1,0:T(8,128)(2,1)S(1)} %get-tuple-element.65), channel_id=1, source_target_pairs={{0,24},{8,0},{16,8},{24,16},{1,25},{9,1},{17,9},{25,17},{2,26},{10... | collective-permute-start | bytes 196616 | tf_op jit(solution)/shard_map/ppermute | solution.py:659
  42.4 3.5 %copy-start.8 = (f32[2048]{0:T(1024)S(1)}, f32[2048]{0:T(1024)}, u32[]{:S(2)}) copy-start(f32[2048]{0:T(1024)} %param.19) | copy-start | bytes 24580
  42.5 3.5 %collective-permute-start.15 = (bf16[128,1024]{1,0:T(8,128)(2,1)S(1)}, bf16[128,1024]{1,0:T(8,128)(2,1)S(1)}, u32[]{:S(2)}, u32[]{:S(2)}) collective-permute-start(bf16[128,1024]{1,0:T(8,128)(2,1)S(1)} %get-tuple-element.69), channel_id=1, source_target_pairs={{0,4},{4,0},{1,5},{5,1},{2,6},{6,2},{3,7},{7,3},{8,12},{12,8},{9,1... | collective-permute-start | bytes 786440 | tf_op jit(solution)/shard_map/ppermute | solution.py:663
  42.6 15.6 %collective-permute-start.20 = (bf16[1024,256]{1,0:T(8,128)(2,1)S(1)}, bf16[1024,256]{1,0:T(8,128)(2,1)S(1)}, u32[]{:S(2)}, u32[]{:S(2)}) collective-permute-start(bf16[1024,256]{1,0:T(8,128)(2,1)S(1)} %slice.8), channel_id=1, source_target_pairs={{0,32},{32,64},{64,96},{96,0},{1,33},{33,65},{65,97},{97,1},{2,34}... | collective-permute-start | bytes 1572872 | tf_op jit(solution)/shard_map/ppermute | solution.py:659
  44.1 14.1 %collective-permute-start.21 = (bf16[1024,256]{1,0:T(8,128)(2,1)S(1)}, bf16[1024,256]{1,0:T(8,128)(2,1)S(1)}, u32[]{:S(2)}, u32[]{:S(2)}) collective-permute-start(bf16[1024,256]{1,0:T(8,128)(2,1)S(1)} %slice.9), channel_id=1, source_target_pairs={{0,96},{32,0},{64,32},{96,64},{1,97},{33,1},{65,33},{97,65},{2,98}... | collective-permute-start | bytes 1572872 | tf_op jit(solution)/shard_map/ppermute | solution.py:659
  47.2 14.0 %collective-permute-start.17 = (bf16[128,2048]{1,0:T(8,128)(2,1)S(1)}, bf16[128,2048]{1,0:T(8,128)(2,1)S(1)}, u32[]{:S(2)}, u32[]{:S(2)}) collective-permute-start(bf16[128,2048]{1,0:T(8,128)(2,1)S(1)} %get-tuple-element.71.top_ref), channel_id=1, source_target_pairs={{0,24},{8,0},{16,8},{24,16},{1,25},{9,1},{17,9},{25,17},{2,26},{10... | collective-permute-start | bytes 1572872 | tf_op jit(solution)/shard_map/ppermute | solution.py:659
  50.0 14.7 %collective-permute-start.16 = (bf16[128,2048]{1,0:T(8,128)(2,1)S(1)}, bf16[128,2048]{1,0:T(8,128)(2,1)S(1)}, u32[]{:S(2)}, u32[]{:S(2)}) collective-permute-start(bf16[128,2048]{1,0:T(8,128)(2,1)S(1)} %get-tuple-element.71.top_ref), channel_id=1, source_target_pairs={{0,8},{8,16},{16,24},{24,0},{1,9},{9,17},{17,25},{25,1},{2,10},{10... | collective-permute-start | bytes 1572872 | tf_op jit(solution)/shard_map/ppermute | solution.py:659
  58.2 9.7 %collective-permute-start.22 = (bf16[1024,256]{1,0:T(8,128)(2,1)S(1)}, bf16[1024,256]{1,0:T(8,128)(2,1)S(1)}, u32[]{:S(2)}, u32[]{:S(2)}) collective-permute-start(bf16[1024,256]{1,0:T(8,128)(2,1)S(1)} %collective-permute-done.20.refs_5_.refs_0_), channel_id=1, source_target_pairs={{0,4},{4,0},{1,5},{5,1},{2,6},{6,2},{3,7},{7,3},{8,12},{12,8},{9,1... | collective-permute-start | bytes 1572872 | tf_op jit(solution)/shard_map/ppermute | solution.py:663
  58.2 9.7 %collective-permute-start.23 = (bf16[1024,256]{1,0:T(8,128)(2,1)S(1)}, bf16[1024,256]{1,0:T(8,128)(2,1)S(1)}, u32[]{:S(2)}, u32[]{:S(2)}) collective-permute-start(bf16[1024,256]{1,0:T(8,128)(2,1)S(1)} %collective-permute-done.21.refs_6_.refs_1_), channel_id=1, source_target_pairs={{0,4},{4,0},{1,5},{5,1},{2,6},{6,2},{3,7},{7,3},{8,12},{12,8},{9,1... | collective-permute-start | bytes 1572872 | tf_op jit(solution)/shard_map/ppermute | solution.py:663
  64.7 13.8 %collective-permute-start.19 = (bf16[128,2048]{1,0:T(8,128)(2,1)S(1)}, bf16[128,2048]{1,0:T(8,128)(2,1)S(1)}, u32[]{:S(2)}, u32[]{:S(2)}) collective-permute-start(bf16[128,2048]{1,0:T(8,128)(2,1)S(1)} %get-tuple-element.73.low_ref), channel_id=1, source_target_pairs={{0,8},{8,16},{16,24},{24,0},{1,9},{9,17},{17,25},{25,1},{2,10},{10... | collective-permute-start | bytes 1572872 | tf_op jit(solution)/shard_map/ppermute | solution.py:659
  64.7 13.8 %collective-permute-start.18 = (bf16[128,2048]{1,0:T(8,128)(2,1)S(1)}, bf16[128,2048]{1,0:T(8,128)(2,1)S(1)}, u32[]{:S(2)}, u32[]{:S(2)}) collective-permute-start(bf16[128,2048]{1,0:T(8,128)(2,1)S(1)} %get-tuple-element.73.low_ref), channel_id=1, source_target_pairs={{0,24},{8,0},{16,8},{24,16},{1,25},{9,1},{17,9},{25,17},{2,26},{10... | collective-permute-start | bytes 1572872 | tf_op jit(solution)/shard_map/ppermute | solution.py:659
  69.3 12.4 %collective-permute-start.26 = (bf16[272,512]{1,0:T(8,128)(2,1)S(1)}, bf16[272,512]{1,0:T(8,128)(2,1)S(1)}, u32[]{:S(2)}, u32[]{:S(2)}) collective-permute-start(bf16[272,512]{1,0:T(8,128)(2,1)S(1)} %get-tuple-element.82), channel_id=1, source_target_pairs={{0,1},{1,2},{2,3},{3,0},{4,5},{5,6},{6,7},{7,4},{8,9},{9,10},{10,1... | collective-permute-start | bytes 835592 | tf_op jit(solution)/shard_map/ppermute | solution.py:659
  70.9 12.3 %collective-permute-start.27 = (bf16[272,512]{1,0:T(8,128)(2,1)S(1)}, bf16[272,512]{1,0:T(8,128)(2,1)S(1)}, u32[]{:S(2)}, u32[]{:S(2)}) collective-permute-start(bf16[272,512]{1,0:T(8,128)(2,1)S(1)} %get-tuple-element.83), channel_id=1, source_target_pairs={{0,2},{1,3},{2,0},{3,1},{4,6},{5,7},{6,4},{7,5},{8,10},{9,11},{10,... | collective-permute-start | bytes 835592 | tf_op jit(solution)/shard_map/ppermute | solution.py:659
  72.0 12.3 %collective-permute-start.28 = (bf16[272,512]{1,0:T(8,128)(2,1)S(1)}, bf16[272,512]{1,0:T(8,128)(2,1)S(1)}, u32[]{:S(2)}, u32[]{:S(2)}) collective-permute-start(bf16[272,512]{1,0:T(8,128)(2,1)S(1)} %get-tuple-element.84), channel_id=1, source_target_pairs={{0,3},{1,0},{2,1},{3,2},{4,7},{5,4},{6,5},{7,6},{8,11},{9,8},{10,9... | collective-permute-start | bytes 835592 | tf_op jit(solution)/shard_map/ppermute | solution.py:659
  78.5 14.8 %collective-permute-start.24 = (bf16[128,2048]{1,0:T(8,128)(2,1)S(1)}, bf16[128,2048]{1,0:T(8,128)(2,1)S(1)}, u32[]{:S(2)}, u32[]{:S(2)}) collective-permute-start(bf16[128,2048]{1,0:T(8,128)(2,1)S(1)} %collective-permute-done.16.refs_0_), channel_id=1, source_target_pairs={{0,8},{8,16},{16,24},{24,0},{1,9},{9,17},{17,25},{25,1},{2,10},{10... | collective-permute-start | bytes 1572872 | tf_op jit(solution)/shard_map/ppermute | solution.py:659
  78.5 17.0 %collective-permute-start.25 = (bf16[128,2048]{1,0:T(8,128)(2,1)S(1)}, bf16[128,2048]{1,0:T(8,128)(2,1)S(1)}, u32[]{:S(2)}, u32[]{:S(2)}) collective-permute-start(bf16[128,2048]{1,0:T(8,128)(2,1)S(1)} %collective-permute-done.18.refs_1_), channel_id=1, source_target_pairs={{0,24},{8,0},{16,8},{24,16},{1,25},{9,1},{17,9},{25,17},{2,26},{10... | collective-permute-start | bytes 1572872 | tf_op jit(solution)/shard_map/ppermute | solution.py:659
  81.7 9.1 %collective-permute-start.33 = (bf16[256,512]{1,0:T(8,128)(2,1)S(1)}, bf16[256,512]{1,0:T(8,128)(2,1)S(1)}, u32[]{:S(2)}, u32[]{:S(2)}) collective-permute-start(bf16[256,512]{1,0:T(8,128)(2,1)S(1)} %get-tuple-element.91), channel_id=1, source_target_pairs={{0,1},{1,2},{2,3},{3,0},{4,5},{5,6},{6,7},{7,4},{8,9},{9,10},{10,1... | collective-permute-start | bytes 786440 | tf_op jit(solution)/shard_map/ppermute | solution.py:659
  83.2 15.5 %collective-permute-start.34 = (bf16[256,512]{1,0:T(8,128)(2,1)S(1)}, bf16[256,512]{1,0:T(8,128)(2,1)S(1)}, u32[]{:S(2)}, u32[]{:S(2)}) collective-permute-start(bf16[256,512]{1,0:T(8,128)(2,1)S(1)} %get-tuple-element.92), channel_id=1, source_target_pairs={{0,2},{1,3},{2,0},{3,1},{4,6},{5,7},{6,4},{7,5},{8,10},{9,11},{10,... | collective-permute-start | bytes 786440 | tf_op jit(solution)/shard_map/ppermute | solution.py:659
  84.3 16.2 %collective-permute-start.35 = (bf16[256,512]{1,0:T(8,128)(2,1)S(1)}, bf16[256,512]{1,0:T(8,128)(2,1)S(1)}, u32[]{:S(2)}, u32[]{:S(2)}) collective-permute-start(bf16[256,512]{1,0:T(8,128)(2,1)S(1)} %get-tuple-element.93), channel_id=1, source_target_pairs={{0,3},{1,0},{2,1},{3,2},{4,7},{5,4},{6,5},{7,6},{8,11},{9,8},{10,9... | collective-permute-start | bytes 786440 | tf_op jit(solution)/shard_map/ppermute | solution.py:659
  90.8 14.4 %collective-permute-start.36 = (bf16[256,512]{1,0:T(8,128)(2,1)S(1)}, bf16[256,512]{1,0:T(8,128)(2,1)S(1)}, u32[]{:S(2)}, u32[]{:S(2)}) collective-permute-start(bf16[256,512]{1,0:T(8,128)(2,1)S(1)} %get-tuple-element.94), channel_id=1, source_target_pairs={{0,1},{1,2},{2,3},{3,0},{4,5},{5,6},{6,7},{7,4},{8,9},{9,10},{10,1... | collective-permute-start | bytes 786440 | tf_op jit(solution)/shard_map/ppermute | solution.py:659
  93.3 16.2 %collective-permute-start.37 = (bf16[256,512]{1,0:T(8,128)(2,1)S(1)}, bf16[256,512]{1,0:T(8,128)(2,1)S(1)}, u32[]{:S(2)}, u32[]{:S(2)}) collective-permute-start(bf16[256,512]{1,0:T(8,128)(2,1)S(1)} %get-tuple-element.95), channel_id=1, source_target_pairs={{0,2},{1,3},{2,0},{3,1},{4,6},{5,7},{6,4},{7,5},{8,10},{9,11},{10,... | collective-permute-start | bytes 786440 | tf_op jit(solution)/shard_map/ppermute | solution.py:659
  95.4 15.4 %collective-permute-start.38 = (bf16[256,512]{1,0:T(8,128)(2,1)S(1)}, bf16[256,512]{1,0:T(8,128)(2,1)S(1)}, u32[]{:S(2)}, u32[]{:S(2)}) collective-permute-start(bf16[256,512]{1,0:T(8,128)(2,1)S(1)} %get-tuple-element.96), channel_id=1, source_target_pairs={{0,3},{1,0},{2,1},{3,2},{4,7},{5,4},{6,5},{7,6},{8,11},{9,8},{10,9... | collective-permute-start | bytes 786440 | tf_op jit(solution)/shard_map/ppermute | solution.py:659
  98.7 21.7 %copy-start.3 = (bf16[256,2048]{1,0:T(8,128)(2,1)S(1)}, bf16[256,2048]{1,0:T(8,128)(2,1)}, u32[]{:S(2)}) copy-start(bf16[256,2048]{1,0:T(8,128)(2,1)} %residual_ref.3) | copy-start | bytes 3145732
  98.7 14.5 %collective-permute-start.29 = (bf16[256,512]{1,0:T(8,128)(2,1)S(1)}, bf16[256,512]{1,0:T(8,128)(2,1)S(1)}, u32[]{:S(2)}, u32[]{:S(2)}) collective-permute-start(bf16[256,512]{1,0:T(8,128)(2,1)S(1)} %get-tuple-element.87), channel_id=1, source_target_pairs={{0,1},{1,2},{2,3},{3,0},{4,5},{5,6},{6,7},{7,4},{8,9},{9,10},{10,1... | collective-permute-start | bytes 786440 | tf_op jit(solution)/shard_map/ppermute | solution.py:659
  100.5 15.4 %collective-permute-start.30 = (bf16[256,512]{1,0:T(8,128)(2,1)S(1)}, bf16[256,512]{1,0:T(8,128)(2,1)S(1)}, u32[]{:S(2)}, u32[]{:S(2)}) collective-permute-start(bf16[256,512]{1,0:T(8,128)(2,1)S(1)} %get-tuple-element.88), channel_id=1, source_target_pairs={{0,2},{1,3},{2,0},{3,1},{4,6},{5,7},{6,4},{7,5},{8,10},{9,11},{10,... | collective-permute-start | bytes 786440 | tf_op jit(solution)/shard_map/ppermute | solution.py:659
  105.2 13.4 %collective-permute-start.31 = (bf16[256,512]{1,0:T(8,128)(2,1)S(1)}, bf16[256,512]{1,0:T(8,128)(2,1)S(1)}, u32[]{:S(2)}, u32[]{:S(2)}) collective-permute-start(bf16[256,512]{1,0:T(8,128)(2,1)S(1)} %get-tuple-element.89), channel_id=1, source_target_pairs={{0,3},{1,0},{2,1},{3,2},{4,7},{5,4},{6,5},{7,6},{8,11},{9,8},{10,9... | collective-permute-start | bytes 786440 | tf_op jit(solution)/shard_map/ppermute | solution.py:659
  111.1 8.0 %collective-permute-start.39 = (bf16[256,512]{1,0:T(8,128)(2,1)S(1)}, bf16[256,512]{1,0:T(8,128)(2,1)S(1)}, u32[]{:S(2)}, u32[]{:S(2)}) collective-permute-start(bf16[256,512]{1,0:T(8,128)(2,1)S(1)} %get-tuple-element.97), channel_id=1, source_target_pairs={{0,24},{8,0},{16,8},{24,16},{1,25},{9,1},{17,9},{25,17},{2,26},{10... | collective-permute-start | bytes 786440 | tf_op jit(solution)/shard_map/ppermute | solution.py:659
  112.8 7.6 %collective-permute-start.40 = (bf16[256,512]{1,0:T(8,128)(2,1)S(1)}, bf16[256,512]{1,0:T(8,128)(2,1)S(1)}, u32[]{:S(2)}, u32[]{:S(2)}) collective-permute-start(bf16[256,512]{1,0:T(8,128)(2,1)S(1)} %get-tuple-element.98), channel_id=1, source_target_pairs={{0,8},{8,16},{16,24},{24,0},{1,9},{9,17},{17,25},{25,1},{2,10},{10... | collective-permute-start | bytes 786440 | tf_op jit(solution)/shard_map/ppermute | solution.py:659
  118.7 9.2 %collective-permute-start.32 = (bf16[256,512]{1,0:T(8,128)(2,1)S(1)}, bf16[256,512]{1,0:T(8,128)(2,1)S(1)}, u32[]{:S(2)}, u32[]{:S(2)}) collective-permute-start(bf16[256,512]{1,0:T(8,128)(2,1)S(1)} %far_sums.1._), channel_id=1, source_target_pairs={{0,16},{8,24},{16,0},{24,8},{1,17},{9,25},{17,1},{25,9},{2,18},{10... | collective-permute-start | bytes 786440 | tf_op jit(solution)/shard_map/ppermute | solution.py:659
  (3 other events, 3.3 us)
